TPU v7x, 32 devices: a whole 2x2x4 slice. The times are simulated.
32 devices in a mesh: groups: 2 (over x), row: 8 (over z, y), col: 2 (over core).
Axes of the slice: x: 2, y: 2, z: 4, core: 2. Of those that a mesh axis runs over, the one named last changes fastest.
Arguments:
- features: bfloat16 [8192, 128], P(('groups', 'row', 'col')), parts along dimension 0, may hold values from -6 to 6
- node_order: int32 [32, 256], P(('groups', 'row', 'col')), parts along dimension 0, may hold values from 0 to 255, each once within a row
- weight_first: bfloat16 [128, 256], replicated, may hold values from -0.5 to 0.5
- weight_second: bfloat16 [256, 128], replicated, may hold values from -0.375 to 0.375
- adjacency_tiles: bfloat16 [16, 2, 32, 128, 128], P(('groups', 'row'), 'col'), parts along dimension 0, as said below
- tile_rows: int32 [16, 2, 32], P(('groups', 'row'), 'col'), parts along dimension 0, may hold values from 0 to 3, as said below
- tile_cols: int32 [16, 2, 32], P(('groups', 'row'), 'col'), parts along dimension 0, may hold values from 0 to 15, as said below
- tile_counts: int32 [16, 2], P(('groups', 'row'), 'col'), parts along dimension 0, may hold values from 1 to 32, as said below
- logit_grads: bfloat16 [8192, 128], P(('groups', 'row', 'col')), parts along dimension 0, may hold values from -6 to 6
Outputs:
- logits: bfloat16 [8192, 128], P(('groups', 'row', 'col')), parts along dimension 0
- grad_first: float32 [256, 256], P('groups'), parts along dimension 0
- grad_second: float32 [512, 128], P('groups'), parts along dimension 0
There are 2 independent parts, one for each index of `groups`. A program takes and returns all parts, laid end to end along the dimension named above; an argument that names none is the same for every part. Nothing has to cross between parts.
Inputs may be any that keep to these rules, and one draw needn't show every extreme that they name: `adjacency_tiles`: the live slots of a device name distinct block positions. The adjacency is symmetric: block (j, i) is present exactly when block (i, j) is, and holds its transpose. `tile_rows`: row block of a slot inside its device's row slab. `tile_cols`: column block of a slot inside its device's column set. `tile_counts`: every diagonal block is present. Some device holds exactly 32 live slots in every draw.
All inputs are finite; a program needn't handle non-finite values.
Results may differ from a plain program's by a relative error of at most 0.0055.
Values may be sent and summed in bfloat16 or wider, within the bound.
No kernel may reach another device: no remote copies, remote signals or barrier semaphores. Data moves between devices by JAX's collectives and lax.ppermute only.
A program may use at most 128 MiB of HBM per device.

v0:
```python
import math

import jax
import jax.numpy as jnp
from jax import lax
from jax.sharding import PartitionSpec as P


def slot_products(tile_set, row_ids, col_ids, live_count, source, blocks):
    slot_total = tile_set.shape[0]
    live_mask = jnp.arange(slot_total, dtype=jnp.int32) < live_count
    picked = source[col_ids]
    product = jnp.einsum("tmk,tkf->tmf", tile_set, picked, preferred_element_type=jnp.float32)
    onehot = (
        (row_ids[None, :] == jnp.arange(blocks, dtype=jnp.int32)[:, None]) & live_mask[None, :]
    ).astype(jnp.float32)
    return jnp.einsum("st,tmf->smf", onehot, product, precision=lax.Precision.HIGHEST)


def shards(
    features,
    node_order,
    weight_first,
    weight_second,
    adjacency_tiles,
    tile_rows,
    tile_cols,
    tile_counts,
    logit_grads,
):
    tile_set = adjacency_tiles[0, 0]
    row_ids = tile_rows[0, 0]
    col_ids = tile_cols[0, 0]
    live_count = tile_counts[0, 0]
    block_size = tile_set.shape[-1]
    node_rows = features.shape[0]
    feat_width = features.shape[1]
    class_width = logit_grads.shape[1]
    slab_blocks = lax.axis_size("col") * node_rows // block_size
    nodes_total = node_rows * lax.axis_size("row") * lax.axis_size("col")
    ordered = jnp.take(features, node_order[0], axis=0)
    feature_set = lax.all_gather(ordered, "row", axis=0, tiled=True).reshape(
        -1, block_size, feat_width
    )
    first_terms = slot_products(tile_set, row_ids, col_ids, live_count, feature_set, slab_blocks)
    aggregated = lax.psum_scatter(
        first_terms.reshape(-1, feat_width), "col", scatter_dimension=0, tiled=True
    ).astype(jnp.bfloat16)
    pre_act = jnp.dot(aggregated, weight_first, preferred_element_type=jnp.float32)
    hidden = jax.nn.silu(pre_act).astype(jnp.bfloat16)
    projected = jnp.dot(hidden, weight_second, preferred_element_type=jnp.float32).astype(
        jnp.bfloat16
    )
    projected_set = lax.all_gather(projected, "row", axis=0, tiled=True).reshape(
        -1, block_size, class_width
    )
    second_terms = slot_products(tile_set, row_ids, col_ids, live_count, projected_set, slab_blocks)
    logits = lax.psum_scatter(
        second_terms.reshape(-1, class_width), "col", scatter_dimension=0, tiled=True
    ).astype(jnp.bfloat16)
    grad_set = lax.all_gather(logit_grads, "row", axis=0, tiled=True).reshape(
        -1, block_size, class_width
    )
    back_terms = slot_products(tile_set, row_ids, col_ids, live_count, grad_set, slab_blocks)
    back_grads = lax.psum_scatter(
        back_terms.reshape(-1, class_width), "col", scatter_dimension=0, tiled=True
    ).astype(jnp.bfloat16)
    second_local = jnp.einsum("nh,nc->hc", hidden, back_grads, preferred_element_type=jnp.float32)
    hidden_grads = jnp.einsum(
        "nc,hc->nh", back_grads, weight_second, preferred_element_type=jnp.float32
    )
    sigmoid_pre = jax.nn.sigmoid(pre_act)
    pre_grads = (hidden_grads * sigmoid_pre * (1.0 + pre_act * (1.0 - sigmoid_pre))).astype(
        jnp.bfloat16
    )
    first_local = jnp.einsum("nf,nh->fh", aggregated, pre_grads, preferred_element_type=jnp.float32)
    grad_first, grad_second = lax.psum((first_local, second_local), ("row", "col"))
    grad_scale = 1.0 / math.sqrt(nodes_total)
    return (logits, grad_first * grad_scale, grad_second * grad_scale)


def solution(mesh):
    return jax.shard_map(
        shards,
        mesh=mesh,
        in_specs=(
            P(("groups", "row", "col"), None),
            P(("groups", "row", "col"), None),
            P(),
            P(),
            P(("groups", "row"), "col", None, None, None),
            P(("groups", "row"), "col", None),
            P(("groups", "row"), "col", None),
            P(("groups", "row"), "col"),
            P(("groups", "row", "col"), None),
        ),
        out_specs=(P(("groups", "row", "col"), None), P("groups", None), P("groups", None)),
        check_vma=False,
    )
```

profile of v0, /device:TPU:0, one launch (start us, length us, event | category | flops | bytes accessed | tf_op | source)
XLA Modules:
  0.0 243.3 jit_solution(9943022263113845781)
XLA Ops:
  7.2 0.0 copy-start
  7.2 0.0 reduce-scatter.4.cloned.1.call-start
  7.2 0.7 fusion.28
  8.0 0.7 compare_select_fusion
  8.7 0.7 compare_and_fusion
  9.3 1.6 gather_fusion
  10.9 0.1 broadcast_select_fusion
  11.0 33.0 %all_gather.9 = bf16[2048,128]{1,0:T(8,128)(2,1)S(1)} all-gather(bf16[256,128]{1,0:T(8,128)(2,1)S(1)} %broadcast_select_fusion), channel_id=1, replica_groups=mesh['groups'=2,'row'=8,'col'=2] {'row'}, dimensions={0}, use_global_device_ids=true | all-gather | bytes 589824 | tf_op jit(solution)/shard_map/all_gather | solution.py:42
  44.0 0.7 gather_fusion.1
  44.8 0.0 copy-done
  44.8 2.2 fusion.13
  47.0 0.0 copy-start.3
  47.0 2.4 copy.15
  49.4 0.0 copy-start.1
  50.1 0.0 copy-done.3
  50.1 0.8 fusion.4
  51.0 0.7 copy.12
  51.7 0.0 reduce-scatter.4.cloned.1.call-update
  51.7 0.0 reduce-scatter.8.cloned.1.call-start
  51.8 0.0 copy-done.1
  51.8 31.3 %all_gather.11 = bf16[2048,128]{1,0:T(8,128)(2,1)S(1)} all-gather(bf16[256,128]{1,0:T(8,128)(2,1)S(1)} %copy-done.1), channel_id=1, replica_groups=mesh['groups'=2,'row'=8,'col'=2] {'row'}, dimensions={0}, use_global_device_ids=true | all-gather | bytes 589824 | tf_op jit(solution)/shard_map/all_gather | solution.py:61
  83.1 1.6 gather_fusion.3
  84.7 2.1 fusion.9
  86.8 2.1 copy.17
  88.9 0.0 copy-start.5
  88.9 0.0 copy-start.2
  88.9 2.4 fusion
  91.3 0.7 copy.14
  92.0 0.0 reduce-scatter.8.cloned.1.call-update
  92.0 0.0 all-reduce.3.cloned.1.call-start
  92.1 0.0 reduce-scatter.4.cloned.1.call-done
  92.1 0.0 copy-done.5
  92.1 1.8 multiply_convert_fusion
  93.9 0.0 copy-done.2
  93.9 0.2 convolution_convert_fusion
  94.1 31.4 %all_gather.10 = bf16[2048,128]{1,0:T(8,128)(2,1)S(1)} all-gather(bf16[256,128]{1,0:T(8,128)(2,1)S(1)} %convolution_convert_fusion), channel_id=1, replica_groups=mesh['groups'=2,'row'=8,'col'=2] {'row'}, dimensions={0}, use_global_device_ids=true | all-gather | bytes 589824 | tf_op jit(solution)/shard_map/all_gather | solution.py:54
  125.5 0.7 gather_fusion.2
  126.2 2.2 fusion.11
  128.5 0.0 copy-start.4
  128.5 2.4 copy.16
  130.9 0.0 reduce-scatter.8.cloned.1.call-done
  130.9 1.8 fusion.19
  132.7 0.0 copy-done.4
  132.7 2.0 fusion.8
  134.8 0.0 all-reduce.3.cloned.1.call-update
  134.8 0.0 reduce-scatter.6.cloned.1.call-start
  134.8 0.8 fusion.2
  135.7 0.7 copy.13
  136.4 0.0 reduce-scatter.6.cloned.1.call-update
  136.4 88.5 %all-reduce.3.cloned.1.call-done = (f32[128,256]{1,0:T(8,128)}, f32[256,128]{1,0:T(8,128)}) async-done(((f32[128,256]{1,0:T(8,128)}, f32[256,128]{1,0:T(8,128)}), (f32[128,256]{1,0:T(8,128)}, f32[256,128]{1,0:T(8,128)})) %all-reduce.3.cloned.1.call-update) | async-done | bytes 262160 | tf_op jit(solution)/shard_map/psum | solution.py:77
  224.9 1.6 broadcast_multiply_fusion
  226.5 1.6 broadcast_multiply_fusion.1
  228.1 7.2 %reduce-scatter.6.cloned.1.call-done = f32[256,128]{1,0:T(8,128)} async-done(((f32[512,128]{1,0:T(8,128)}), f32[256,128]{1,0:T(8,128)}) %reduce-scatter.6.cloned.1.call-update) | async-done | bytes 131088 | tf_op jit(solution)/shard_map/reduce_scatter | solution.py:58
  235.2 1.5 convert_element_type.24
  (3 shorter events, 0.0 us)
Async XLA Ops:
  7.2 37.6 %copy-start = (bf16[1,1,32,128,128]{4,3,2,1,0:T(8,128)(2,1)S(1)}, bf16[1,1,32,128,128]{4,3,2,1,0:T(8,128)(2,1)}, u32[]{:S(2)}) copy-start(bf16[1,1,32,128,128]{4,3,2,1,0:T(8,128)(2,1)} %param.13) | copy-start | bytes 3145732
  7.2 84.9 %reduce-scatter.4.cloned.1.call-start = ((), (), s32[]{:S(2)}) async-start(), calls=%async_computation.3 | async-start | bytes 393216 | tf_op jit(solution)/shard_map/reduce_scatter | solution.py:46
  47.0 3.1 %copy-start.3 = (s32[1,1,32]{2,1,0:T(1,128)S(1)}, s32[1,1,32]{2,1,0:T(1,128)}, u32[]{:S(2)}) copy-start(s32[1,1,32]{2,1,0:T(1,128)} %param.14) | copy-start | bytes 388
  49.4 2.3 copy-start.1
  51.7 79.2 %reduce-scatter.8.cloned.1.call-start = ((), (), s32[]{:S(2)}) async-start(), calls=%async_computation.5 | async-start | bytes 393216 | tf_op jit(solution)/shard_map/reduce_scatter | solution.py:65
  88.9 3.2 %copy-start.5 = (bf16[128,256]{1,0:T(8,128)(2,1)S(1)}, bf16[128,256]{1,0:T(8,128)(2,1)}, u32[]{:S(2)}) copy-start(bf16[128,256]{1,0:T(8,128)(2,1)} %param.11) | copy-start | bytes 196612
  88.9 5.0 %copy-start.2 = (bf16[256,128]{1,0:T(8,128)(2,1)S(1)}, bf16[256,128]{1,0:T(8,128)(2,1)}, u32[]{:S(2)}) copy-start(bf16[256,128]{1,0:T(8,128)(2,1)} %param.12) | copy-start | bytes 196612
  92.0 132.9 %all-reduce.3.cloned.1.call-start = ((), (), s32[]{:S(2)}) async-start(), calls=%async_computation.6 | async-start | bytes 524288 | tf_op jit(solution)/shard_map/psum | solution.py:77
  128.5 4.2 %copy-start.4 = (f32[256,128]{1,0:T(8,128)S(1)}, f32[256,128]{1,0:T(8,128)}, u32[]{:S(2)}) copy-start(f32[256,128]{1,0:T(8,128)} %reduce-scatter.4.cloned.1.call-done) | copy-start | bytes 393220
  134.8 100.5 %reduce-scatter.6.cloned.1.call-start = ((), (), s32[]{:S(2)}) async-start(), calls=%async_computation.4 | async-start | bytes 393216 | tf_op jit(solution)/shard_map/reduce_scatter | solution.py:58
Sparse Core Ops, SparseCore 0:
  51.8 8.7 reduce-scatter.3
  92.1 8.8 reduce-scatter.7
  134.9 89.9 all-reduce.2
  227.0 8.1 reduce-scatter.5
where the time goes:
time: 244 us; the launch traced here: 243 us
  waiting for transfers between devices  95.8 us (39%)
  blocking collectives  95.7 us (39%)
  matrix products  16.4 us (7%)
  between operations  14.6 us (6%)
  local copies, waits for them, and re-layouts  13.7 us (6%)
  other arithmetic  6.9 us (3%)
    psum x1, waiting for transfers between devices, shards(): lax.psum((first_local, second_local), ('row', 'col'))  88.5 us
    all_gather x1, blocking collectives, shards(): lax.all_gather(ordered, 'row', axis=0, tiled=True)  33 us
    all_gather x1, blocking collectives, shards(): lax.all_gather(projected, 'row', axis=0, tiled=True)  31.4 us
    all_gather x1, blocking collectives, shards(): lax.all_gather(logit_grads, 'row', axis=0, tiled=True)  31.3 us
    reduce_scatter x1, waiting for transfers between devices, shards(): lax.psum_scatter(second_terms.reshape(-1, class_width), 'col', scatter_di...  7.16 us
    dot_general x3, local copies, waits for them, and re-layouts, slot_products(): jnp.einsum('tmk,tkf->tmf', tile_set, picked, preferred_element_type=jnp.f...  6.86 us
    dot_general x3, matrix products, slot_products(): jnp.einsum('tmk,tkf->tmf', tile_set, picked, preferred_element_type=jnp.f...  6.55 us
  transfers between devices with their start and end apart: 4, of which 2 were waited for; matrix products, arithmetic and copies ran while one was open for 9% of the time, Pallas kernels for 0%

commit v1 on v0

v1 whole, which is shorter than its diff:
```python
import functools
import math

import jax
import jax.numpy as jnp
from jax import lax
from jax.experimental import pallas as pl
from jax.experimental.pallas import tpu as pltpu
from jax.sharding import PartitionSpec as P

VMEM = pl.BlockSpec(memory_space=pltpu.VMEM)
SMEM = pl.BlockSpec(memory_space=pltpu.SMEM)


def dot(a, b, contract=((1,), (0,))):
    return lax.dot_general(a, b, (contract, ((), ())), preferred_element_type=jnp.float32)


def call(kernel, out_shape, in_specs, flops, name, *args):
    total = sum(a.size * a.dtype.itemsize for a in args)
    outs = out_shape if isinstance(out_shape, (tuple, list)) else (out_shape,)
    total += sum(math.prod(o.shape) * jnp.dtype(o.dtype).itemsize for o in outs)
    return pl.pallas_call(
        kernel,
        out_shape=out_shape,
        in_specs=in_specs,
        out_specs=jax.tree.map(lambda _: VMEM, out_shape),
        name=name,
        cost_estimate=pl.CostEstimate(flops=flops, bytes_accessed=total, transcendentals=0),
        compiler_params=pltpu.CompilerParams(vmem_limit_bytes=2 * total + (12 << 20)),
    )(*args)


def order_kernel(order_ref, features_ref, grads_ref, out_ref):
    nodes, feat = features_ref.shape
    source = lax.broadcasted_iota(jnp.int32, (nodes, nodes), 0)
    picks = (source == order_ref[...]).astype(jnp.float32).astype(jnp.bfloat16)
    ordered = dot(picks, features_ref[...], ((0,), (0,)))
    out_ref[:, :feat] = ordered.astype(jnp.bfloat16)
    out_ref[:, feat:] = grads_ref[...]


def dense_kernel(blocks, count_ref, rows_ref, cols_ref, tiles_ref, out_ref):
    size = tiles_ref.shape[-1]
    own = lax.axis_index("row")
    out_ref[...] = jnp.zeros_like(out_ref)

    def place(slot, carry):
        column = cols_ref[0, slot]
        piece = lax.bitwise_xor(column // blocks, own)
        row_at = pl.multiple_of(rows_ref[0, slot] * size, size)
        col_at = pl.multiple_of((piece * blocks + column % blocks) * size, size)
        out_ref[pl.ds(row_at, size), pl.ds(col_at, size)] = tiles_ref[slot]
        return carry

    lax.fori_loop(0, count_ref[0, 0], place, 0)


def products(dense_ref, pieces, chunk):
    depth = pieces[0].shape[0]
    for start in range(0, dense_ref.shape[0], chunk):
        total = None
        for k, piece in enumerate(pieces):
            term = dot(dense_ref[start : start + chunk, k * depth : (k + 1) * depth], piece[...])
            total = term if total is None else total + term
        yield start, total


def first_kernel(dense_ref, *refs):
    *pieces, out_ref = refs
    for start, total in products(dense_ref, pieces, 128):
        out_ref[start : start + 128, :] = total


def middle_kernel(mine_ref, theirs_ref, first_ref, second_ref, out_ref):
    feat = first_ref.shape[0]
    half = first_ref.shape[1] // 2
    nodes = out_ref.shape[0] // 2
    col = lax.axis_index("col")
    hid_at = pl.ds(pl.multiple_of(col * half, half), half)
    summed = mine_ref[...] + theirs_ref[...]
    aggregated = summed[:, :feat].astype(jnp.bfloat16)
    back = summed[:, feat:].astype(jnp.bfloat16)
    first_half = first_ref[:, hid_at]
    second_half = second_ref[hid_at, :]

    at = pl.ds(pl.multiple_of(col * nodes, nodes), nodes)
    own = (mine_ref[at, :feat] + theirs_ref[at, :feat]).astype(jnp.bfloat16)
    own_pre = dot(own, first_ref[...])
    own_hidden = (own_pre * jax.nn.sigmoid(own_pre)).astype(jnp.bfloat16)
    out_ref[:nodes, :] = dot(own_hidden, second_ref[...]).astype(jnp.bfloat16)

    pre = dot(aggregated, first_half)
    gate = jax.nn.sigmoid(pre)
    hidden = (pre * gate).astype(jnp.bfloat16)
    hidden_grads = dot(back, second_half, ((1,), (1,)))
    pre_grads = (hidden_grads * gate * (1.0 + pre * (1.0 - gate))).astype(jnp.bfloat16)
    out_ref[nodes : nodes + half, :] = dot(hidden, back, ((0,), (0,))).astype(jnp.bfloat16)
    out_ref[nodes + half :, :] = dot(aggregated, pre_grads, ((0,), (0,))).astype(jnp.bfloat16)


def second_kernel(dense_ref, *refs):
    *pieces, keep_ref, send_ref = refs
    nodes = keep_ref.shape[0]
    col = lax.axis_index("col")
    tops = [piece.at[:nodes, :] for piece in pieces]
    for where, ref in ((col, keep_ref), (1 - col, send_ref)):
        slab = dense_ref.at[pl.ds(pl.multiple_of(where * nodes, nodes), nodes), :]
        for start, total in products(slab, tops, 128):
            ref[start : start + 128, :] = total
    grads = pieces[0][nodes:, :].astype(jnp.float32)
    for piece in pieces[1:]:
        grads = grads + piece[nodes:, :].astype(jnp.float32)
    send_ref[nodes:, :] = grads


def last_kernel(scale, keep_ref, sent_ref, theirs_ref, logits_ref, first_ref, second_ref):
    nodes = keep_ref.shape[0]
    half = second_ref.shape[0] // 2
    col = lax.axis_index("col")
    logits_ref[...] = (keep_ref[...] + theirs_ref[:nodes, :]).astype(jnp.bfloat16)
    for where, ref in ((col, sent_ref), (1 - col, theirs_ref)):
        at = pl.ds(pl.multiple_of(where * half, half), half)
        second_ref[at, :] = ref[nodes : nodes + half, :] * scale
        first_ref[:, at] = ref[nodes + half :, :] * scale


def exchange(x, axis, mask):
    size = lax.axis_size(axis)
    return lax.ppermute(x, axis, [(i, i ^ mask) for i in range(size)])


def gather_rows(x):
    size = lax.axis_size("row")
    inner = 1 << ((size.bit_length() - 1) // 2)
    found = {0: x}
    for mask in range(inner, size, inner):
        found[mask] = exchange(x, "row", mask)
    for low in range(1, inner):
        for mask in range(0, size, inner):
            found[mask + low] = exchange(found[mask], "row", low)
    return [found[k] for k in range(size)]


def shards(
    features,
    node_order,
    weight_first,
    weight_second,
    adjacency_tiles,
    tile_rows,
    tile_cols,
    tile_counts,
    logit_grads,
):
    tiles = adjacency_tiles[0, 0]
    size = tiles.shape[-1]
    nodes, feat = features.shape
    hid, classes = weight_second.shape
    rows, cols = lax.axis_size("row"), lax.axis_size("col")
    slab = cols * nodes
    set_nodes = rows * nodes
    shape = jax.ShapeDtypeStruct
    bf16, f32 = jnp.bfloat16, jnp.float32

    source = call(
        order_kernel, shape((nodes, feat + classes), bf16), [VMEM] * 3,
        2 * nodes * nodes * feat, "order", node_order, features, logit_grads,
    )
    dense = call(
        functools.partial(dense_kernel, nodes // size), shape((slab, set_nodes), bf16),
        [SMEM] * 3 + [VMEM], 0, "dense", tile_counts, tile_rows[0], tile_cols[0], tiles,
    )
    pieces = gather_rows(source)
    partial = call(
        first_kernel, shape((slab, feat + classes), f32), [VMEM] * (1 + rows),
        2 * slab * set_nodes * (feat + classes), "first", dense, *pieces,
    )
    theirs = exchange(partial, "col", 1)
    middle = call(
        middle_kernel, shape((nodes + hid, classes), bf16), [VMEM] * 4,
        10 * slab * feat * hid, "middle", partial, theirs, weight_first, weight_second,
    )
    pieces = gather_rows(middle)
    keep, send = call(
        second_kernel, (shape((nodes, classes), f32), shape((nodes + hid, classes), f32)),
        [VMEM] * (1 + rows), 2 * slab * set_nodes * classes, "second", dense, *pieces,
    )
    theirs = exchange(send, "col", 1)
    return call(
        functools.partial(last_kernel, 1.0 / math.sqrt(set_nodes * cols)),
        (shape((nodes, classes), bf16), shape((feat, hid), f32), shape((hid, classes), f32)),
        [VMEM] * 3, 0, "last", keep, send, theirs,
    )


def solution(mesh):
    return jax.shard_map(
        shards,
        mesh=mesh,
        in_specs=(
            P(("groups", "row", "col"), None),
            P(("groups", "row", "col"), None),
            P(),
            P(),
            P(("groups", "row"), "col", None, None, None),
            P(("groups", "row"), "col", None),
            P(("groups", "row"), "col", None),
            P(("groups", "row"), "col"),
            P(("groups", "row", "col"), None),
        ),
        out_specs=(P(("groups", "row", "col"), None), P("groups", None), P("groups", None)),
        check_vma=False,
    )
```

time: 244 us -> 55.3 us (0.23)
  blocking collectives: 95.7 us -> 0 us
  waiting for transfers between devices: 95.8 us -> 24 us
  starting transfers between devices: 0.16 us -> 20.8 us
  matrix products: 16.4 us -> 0 us
  between operations: 14.6 us -> 1.41 us
  local copies, waits for them, and re-layouts: 13.7 us -> 4.89 us
  other arithmetic: 6.9 us -> 0 us
  Pallas kernels: 0 us -> 3.81 us
    all_gather x3 -> x0, blocking collectives: 95.7 us -> none  [the longest x1 33 us: shards(): lax.all_gather(ordered, 'row', axis=0, tiled=True)]
    psum x1 -> x0, waiting for transfers between devices: 88.5 us -> none  [shards(): lax.psum((first_local, second_local), ('row', 'col'))]
    ppermute x0 -> x16, waiting for transfers between devices: none -> 24 us  [exchange(): return lax.ppermute(x, axis, [(i, i ^ mask) for i in range(size)])]
    ppermute x0 -> x16, starting transfers between devices: none -> 20.8 us  [exchange(): return lax.ppermute(x, axis, [(i, i ^ mask) for i in range(size)])]
    dot_general x10 -> x0, matrix products: 16.4 us -> none  [the longest x3 6.55 us: slot_products(): jnp.einsum('tmk,tkf->tmf', tile_set, picked, preferred_element_type=jnp.f...]
    dot_general x6 -> x0, local copies, waits for them, and re-layouts: 9 us -> none  [the longest x3 6.86 us: slot_products(): jnp.einsum('tmk,tkf->tmf', tile_set, picked, preferred_element_type=jnp.f...]
    reduce_scatter x3 -> x0, waiting for transfers between devices: 7.2 us -> none  [the longest x1 7.16 us: shards(): lax.psum_scatter(second_terms.reshape(-1, class_width), 'col', scatter_di...]
    unnamed x12 -> x16, local copies, waits for them, and re-layouts: 0.03 us -> 4.89 us
  transfers between devices with their start and end apart: 4 -> 16, of which waited for: 2 -> 9; matrix products, arithmetic and copies ran while one was open for 9% -> 0% of each run, Pallas kernels for 0% -> 2%
where the time goes in v1:
time: 55.3 us; the launch traced here: 55 us
  waiting for transfers between devices  24 us (43%)
  starting transfers between devices  20.8 us (38%)
  local copies, waits for them, and re-layouts  4.89 us (9%)
  Pallas kernels  3.81 us (7%)
  between operations  1.41 us (3%)
    ppermute x16, waiting for transfers between devices, exchange(): return lax.ppermute(x, axis, [(i, i ^ mask) for i in range(size)])  24 us
    ppermute x16, starting transfers between devices, exchange(): return lax.ppermute(x, axis, [(i, i ^ mask) for i in range(size)])  20.8 us
    unnamed x16, local copies, waits for them, and re-layouts  4.89 us
    pallas_call x6, Pallas kernels, call(): pl.pallas_call(kernel, out_shape=out_shape, in_specs=in_specs, out_specs=...  3.81 us
  transfers between devices with their start and end apart: 16, of which 9 were waited for; matrix products, arithmetic and copies ran while one was open for 0% of the time, Pallas kernels for 2%

profile of v1, /device:TPU:0, one launch (start us, length us, event | category | flops | bytes accessed | tf_op | source)
XLA Modules:
  0.0 55.0 jit_solution(1679168716726818437)
XLA Ops:
  0.6 0.0 copy-start.3
  0.6 0.8 %copy-done.3 = bf16[256,128]{1,0:T(8,128)(2,1)S(1)} copy-done((bf16[256,128]{1,0:T(8,128)(2,1)S(1)}, bf16[256,128]{1,0:T(8,128)(2,1)}, u32[]{:S(2)}) %copy-start.3) | copy-done | bytes 65560
  1.5 0.0 copy-start.4
  1.5 0.8 %copy-done.4 = bf16[256,128]{1,0:T(8,128)(2,1)S(1)} copy-done((bf16[256,128]{1,0:T(8,128)(2,1)S(1)}, bf16[256,128]{1,0:T(8,128)(2,1)}, u32[]{:S(2)}) %copy-start.4) | copy-done | bytes 65560
  2.3 0.0 copy-start.5
  2.3 0.7 %copy-done.5 = s32[1,256]{1,0:T(1,128)S(1)} copy-done((s32[1,256]{1,0:T(1,128)S(1)}, s32[1,256]{1,0:T(1,128)}, u32[]{:S(2)}) %copy-start.5) | copy-done | bytes 1048
  3.0 0.2 order.1.refs_0_
  3.2 5.1 %collective-permute-start.5 = (bf16[256,256]{1,0:T(8,128)(2,1)S(1)}, bf16[256,256]{1,0:T(8,128)(2,1)S(1)}, u32[]{:S(2)}, u32[]{:S(2)}) collective-permute-start(bf16[256,256]{1,0:T(8,128)(2,1)S(1)} %order.1.refs_0_), channel_id=1, source_target_pairs={{0,12},{2,14},{4,8},{6,10},{8,4},{10,6},{12,0},{14,2},{1,13},{3,15... | collective-permute-start | bytes 393224 | tf_op jit(solution)/shard_map/ppermute | solution.py:130
  8.3 0.0 collective-permute-start.3
  8.3 0.6 %collective-permute-start.1 = (bf16[256,256]{1,0:T(8,128)(2,1)S(1)}, bf16[256,256]{1,0:T(8,128)(2,1)S(1)}, u32[]{:S(2)}, u32[]{:S(2)}) collective-permute-start(bf16[256,256]{1,0:T(8,128)(2,1)S(1)} %order.1.refs_0_), channel_id=1, source_target_pairs={{0,4},{2,6},{4,0},{6,2},{8,12},{10,14},{12,8},{14,10},{1,5},{3,7},... | collective-permute-start | bytes 393224 | tf_op jit(solution)/shard_map/ppermute | solution.py:130
  9.0 1.7 %collective-permute-start = (bf16[256,256]{1,0:T(8,128)(2,1)S(1)}, bf16[256,256]{1,0:T(8,128)(2,1)S(1)}, u32[]{:S(2)}, u32[]{:S(2)}) collective-permute-start(bf16[256,256]{1,0:T(8,128)(2,1)S(1)} %order.1.refs_0_), channel_id=1, source_target_pairs={{0,2},{2,0},{4,6},{6,4},{8,10},{10,8},{12,14},{14,12},{1,3},{3,1},... | collective-permute-start | bytes 393224 | tf_op jit(solution)/shard_map/ppermute | solution.py:130
  10.6 2.1 %collective-permute-done.5.refs_6_ = bf16[256,256]{1,0:T(8,128)(2,1)S(1)} collective-permute-done((bf16[256,256]{1,0:T(8,128)(2,1)S(1)}, bf16[256,256]{1,0:T(8,128)(2,1)S(1)}, u32[]{:S(2)}, u32[]{:S(2)}) %collective-permute-start.5) | collective-permute-done | bytes 131104 | tf_op jit(solution)/shard_map/ppermute | solution.py:130
  12.8 1.7 %collective-permute-start.6 = (bf16[256,256]{1,0:T(8,128)(2,1)S(1)}, bf16[256,256]{1,0:T(8,128)(2,1)S(1)}, u32[]{:S(2)}, u32[]{:S(2)}) collective-permute-start(bf16[256,256]{1,0:T(8,128)(2,1)S(1)} %collective-permute-done.5.refs_6_), channel_id=1, source_target_pairs={{0,2},{2,0},{4,6},{6,4},{8,10},{10,8},{12,14},{14,12},{1,3},{3,1},... | collective-permute-start | bytes 393224 | tf_op jit(solution)/shard_map/ppermute | solution.py:130
  14.5 4.9 %collective-permute-done.3.refs_4_ = bf16[256,256]{1,0:T(8,128)(2,1)S(1)} collective-permute-done((bf16[256,256]{1,0:T(8,128)(2,1)S(1)}, bf16[256,256]{1,0:T(8,128)(2,1)S(1)}, u32[]{:S(2)}, u32[]{:S(2)}) %collective-permute-start.3) | collective-permute-done | bytes 131104 | tf_op jit(solution)/shard_map/ppermute | solution.py:130
  19.4 1.5 %collective-permute-start.4 = (bf16[256,256]{1,0:T(8,128)(2,1)S(1)}, bf16[256,256]{1,0:T(8,128)(2,1)S(1)}, u32[]{:S(2)}, u32[]{:S(2)}) collective-permute-start(bf16[256,256]{1,0:T(8,128)(2,1)S(1)} %collective-permute-done.3.refs_4_), channel_id=1, source_target_pairs={{0,2},{2,0},{4,6},{6,4},{8,10},{10,8},{12,14},{14,12},{1,3},{3,1},... | collective-permute-start | bytes 393224 | tf_op jit(solution)/shard_map/ppermute | solution.py:130
  20.9 0.0 collective-permute-done.1.refs_2_
  20.9 0.5 collective-permute-start.2
  22.1 0.0 copy-start
  22.1 1.2 %copy-done = bf16[1,1,32,128,128]{4,3,2,1,0:T(8,128)(2,1)S(1)} copy-done((bf16[1,1,32,128,128]{4,3,2,1,0:T(8,128)(2,1)S(1)}, bf16[1,1,32,128,128]{4,3,2,1,0:T(8,128)(2,1)}, u32[]{:S(2)}) %copy-start) | copy-done | bytes 1048600
  23.3 0.0 copy-start.6
  23.3 0.7 %copy-done.6 = s32[1,1,32]{2,1,0:T(1,128)S(1)} copy-done((s32[1,1,32]{2,1,0:T(1,128)S(1)}, s32[1,1,32]{2,1,0:T(1,128)}, u32[]{:S(2)}) %copy-start.6) | copy-done | bytes 152
  24.0 0.0 copy-start.7
  24.0 0.7 %copy-done.7 = s32[1,1,32]{2,1,0:T(1,128)S(1)} copy-done((s32[1,1,32]{2,1,0:T(1,128)S(1)}, s32[1,1,32]{2,1,0:T(1,128)}, u32[]{:S(2)}) %copy-start.7) | copy-done | bytes 152
  24.7 0.9 %dense.1.dense_ref = bf16[512,2048]{1,0:T(8,128)(2,1)S(1)} custom-call(s32[1,1]{1,0:T(1,128)S(6)} %copy.12.count_ref, s32[1,32]{1,0:T(1,128)S(1)} %bitcast.4, s32[1,32]{1,0:T(1,128)S(1)} %bitcast.5, bf16[32,128,128]{2,1,0:T(8,128)(2,1)S(1)} %bitcast.3), custom_call_target="tpu_custom_call" | custom-call | bytes 3145988 | tf_op jit(solution)/shard_map/dense/pallas_call | solution.py:23
  25.5 0.0 copy-start.1
  25.5 0.0 copy-start.2
  25.5 0.0 collective-permute-done.refs_1_
  25.6 0.0 collective-permute-done.6.refs_7_
  25.6 0.0 collective-permute-done.4.refs_5_
  25.6 1.2 %collective-permute-done.2.refs_3_ = bf16[256,256]{1,0:T(8,128)(2,1)S(1)} collective-permute-done((bf16[256,256]{1,0:T(8,128)(2,1)S(1)}, bf16[256,256]{1,0:T(8,128)(2,1)S(1)}, u32[]{:S(2)}, u32[]{:S(2)}) %collective-permute-start.2) | collective-permute-done | bytes 131104 | tf_op jit(solution)/shard_map/ppermute | solution.py:130
  26.8 0.7 %first.1.mine_ref = f32[512,256]{1,0:T(8,128)S(1)} custom-call(bf16[512,2048]{1,0:T(8,128)(2,1)S(1)} %dense.1.dense_ref, bf16[256,256]{1,0:T(8,128)(2,1)S(1)} %order.1.refs_0_, bf16[256,256]{1,0:T(8,128)(2,1)S(1)} %collective-permute-done.refs_1_, bf16[256,256]{1,0:T(8,128)(2,1)S(1)} %collective-permute-done.1.refs_2_, ...), custom_call_target="tpu_custom_call" | custom-call | flops 536870912 | bytes 3670016 | tf_op jit(solution)/shard_map/first/pallas_call | solution.py:23
  27.5 0.1 collective-permute-start.7
  27.6 1.9 %collective-permute-done.7.theirs_ref = f32[512,256]{1,0:T(8,128)S(1)} collective-permute-done((f32[512,256]{1,0:T(8,128)S(1)}, f32[512,256]{1,0:T(8,128)S(1)}, u32[]{:S(2)}, u32[]{:S(2)}) %collective-permute-start.7) | collective-permute-done | bytes 524320 | tf_op jit(solution)/shard_map/ppermute | solution.py:130
  29.5 0.0 copy-done.1
  29.5 0.0 copy-done.2
  29.5 0.5 middle.1.refs_0_
  30.0 2.4 %collective-permute-start.13 = (bf16[512,128]{1,0:T(8,128)(2,1)S(1)}, bf16[512,128]{1,0:T(8,128)(2,1)S(1)}, u32[]{:S(2)}, u32[]{:S(2)}) collective-permute-start(bf16[512,128]{1,0:T(8,128)(2,1)S(1)} %middle.1.refs_0_), channel_id=1, source_target_pairs={{0,12},{2,14},{4,8},{6,10},{8,4},{10,6},{12,0},{14,2},{1,13},{3,15... | collective-permute-start | bytes 393224 | tf_op jit(solution)/shard_map/ppermute | solution.py:130
  32.4 0.1 collective-permute-start.11
  32.5 2.0 %collective-permute-start.9 = (bf16[512,128]{1,0:T(8,128)(2,1)S(1)}, bf16[512,128]{1,0:T(8,128)(2,1)S(1)}, u32[]{:S(2)}, u32[]{:S(2)}) collective-permute-start(bf16[512,128]{1,0:T(8,128)(2,1)S(1)} %middle.1.refs_0_), channel_id=1, source_target_pairs={{0,4},{2,6},{4,0},{6,2},{8,12},{10,14},{12,8},{14,10},{1,5},{3,7},... | collective-permute-start | bytes 393224 | tf_op jit(solution)/shard_map/ppermute | solution.py:130
  34.5 1.5 %collective-permute-start.8 = (bf16[512,128]{1,0:T(8,128)(2,1)S(1)}, bf16[512,128]{1,0:T(8,128)(2,1)S(1)}, u32[]{:S(2)}, u32[]{:S(2)}) collective-permute-start(bf16[512,128]{1,0:T(8,128)(2,1)S(1)} %middle.1.refs_0_), channel_id=1, source_target_pairs={{0,2},{2,0},{4,6},{6,4},{8,10},{10,8},{12,14},{14,12},{1,3},{3,1},... | collective-permute-start | bytes 393224 | tf_op jit(solution)/shard_map/ppermute | solution.py:130
  36.0 2.4 %collective-permute-done.13.refs_6_ = bf16[512,128]{1,0:T(8,128)(2,1)S(1)} collective-permute-done((bf16[512,128]{1,0:T(8,128)(2,1)S(1)}, bf16[512,128]{1,0:T(8,128)(2,1)S(1)}, u32[]{:S(2)}, u32[]{:S(2)}) %collective-permute-start.13) | collective-permute-done | bytes 131104 | tf_op jit(solution)/shard_map/ppermute | solution.py:130
  38.4 1.5 %collective-permute-start.14 = (bf16[512,128]{1,0:T(8,128)(2,1)S(1)}, bf16[512,128]{1,0:T(8,128)(2,1)S(1)}, u32[]{:S(2)}, u32[]{:S(2)}) collective-permute-start(bf16[512,128]{1,0:T(8,128)(2,1)S(1)} %collective-permute-done.13.refs_6_), channel_id=1, source_target_pairs={{0,2},{2,0},{4,6},{6,4},{8,10},{10,8},{12,14},{14,12},{1,3},{3,1},... | collective-permute-start | bytes 393224 | tf_op jit(solution)/shard_map/ppermute | solution.py:130
  39.9 4.5 %collective-permute-done.11.refs_4_ = bf16[512,128]{1,0:T(8,128)(2,1)S(1)} collective-permute-done((bf16[512,128]{1,0:T(8,128)(2,1)S(1)}, bf16[512,128]{1,0:T(8,128)(2,1)S(1)}, u32[]{:S(2)}, u32[]{:S(2)}) %collective-permute-start.11) | collective-permute-done | bytes 131104 | tf_op jit(solution)/shard_map/ppermute | solution.py:130
  44.4 1.5 %collective-permute-start.12 = (bf16[512,128]{1,0:T(8,128)(2,1)S(1)}, bf16[512,128]{1,0:T(8,128)(2,1)S(1)}, u32[]{:S(2)}, u32[]{:S(2)}) collective-permute-start(bf16[512,128]{1,0:T(8,128)(2,1)S(1)} %collective-permute-done.11.refs_4_), channel_id=1, source_target_pairs={{0,2},{2,0},{4,6},{6,4},{8,10},{10,8},{12,14},{14,12},{1,3},{3,1},... | collective-permute-start | bytes 393224 | tf_op jit(solution)/shard_map/ppermute | solution.py:130
  45.9 0.0 collective-permute-done.9.refs_2_
  45.9 0.5 collective-permute-start.10
  46.4 0.0 collective-permute-done.8.refs_1_
  46.4 0.0 collective-permute-done.14.refs_7_
  46.4 4.1 %collective-permute-done.12.refs_5_ = bf16[512,128]{1,0:T(8,128)(2,1)S(1)} collective-permute-done((bf16[512,128]{1,0:T(8,128)(2,1)S(1)}, bf16[512,128]{1,0:T(8,128)(2,1)S(1)}, u32[]{:S(2)}, u32[]{:S(2)}) %collective-permute-start.12) | collective-permute-done | bytes 131104 | tf_op jit(solution)/shard_map/ppermute | solution.py:130
  50.5 1.4 %collective-permute-done.10.refs_3_ = bf16[512,128]{1,0:T(8,128)(2,1)S(1)} collective-permute-done((bf16[512,128]{1,0:T(8,128)(2,1)S(1)}, bf16[512,128]{1,0:T(8,128)(2,1)S(1)}, u32[]{:S(2)}, u32[]{:S(2)}) %collective-permute-start.10) | collective-permute-done | bytes 131104 | tf_op jit(solution)/shard_map/ppermute | solution.py:130
  51.9 0.7 %second.1 = (f32[256,128]{1,0:T(8,128)S(1)}, f32[512,128]{1,0:T(8,128)S(1)}) custom-call(bf16[512,2048]{1,0:T(8,128)(2,1)S(1)} %dense.1.dense_ref, bf16[512,128]{1,0:T(8,128)(2,1)S(1)} %middle.1.refs_0_, bf16[512,128]{1,0:T(8,128)(2,1)S(1)} %collective-permute-done.8.refs_1_, bf16[512,128]{1,0:T(8,128)(2,1)S(1)} %collective-permute-done.9.refs_2_, ...), custom_call_target="tpu_custom_call" | custom-call | flops 268435456 | bytes 3538944 | tf_op jit(solution)/shard_map/second/pallas_call | solution.py:23
  52.6 0.1 collective-permute-start.15
  52.7 1.5 %collective-permute-done.15.theirs_ref = f32[512,128]{1,0:T(8,128)S(1)} collective-permute-done((f32[512,128]{1,0:T(8,128)S(1)}, f32[512,128]{1,0:T(8,128)S(1)}, u32[]{:S(2)}, u32[]{:S(2)}) %collective-permute-start.15) | collective-permute-done | bytes 262176 | tf_op jit(solution)/shard_map/ppermute | solution.py:130
  54.2 0.8 %last.1 = (bf16[256,128]{1,0:T(8,128)(2,1)}, f32[128,256]{1,0:T(8,128)}, f32[256,128]{1,0:T(8,128)}) custom-call(f32[256,128]{1,0:T(8,128)S(1)} %get-tuple-element.5.keep_ref, f32[512,128]{1,0:T(8,128)S(1)} %get-tuple-element.6.sent_ref, f32[512,128]{1,0:T(8,128)S(1)} %collective-permute-done.15.theirs_ref), custom_call_target="tpu_custom_call" | custom-call | bytes 983040 | tf_op jit(solution)/shard_map/last/pallas_call | solution.py:23
Async XLA Ops:
  0.6 0.8 %copy-start.3 = (bf16[256,128]{1,0:T(8,128)(2,1)S(1)}, bf16[256,128]{1,0:T(8,128)(2,1)}, u32[]{:S(2)}) copy-start(bf16[256,128]{1,0:T(8,128)(2,1)} %features_ref.1) | copy-start | bytes 196612
  1.5 0.8 %copy-start.4 = (bf16[256,128]{1,0:T(8,128)(2,1)S(1)}, bf16[256,128]{1,0:T(8,128)(2,1)}, u32[]{:S(2)}) copy-start(bf16[256,128]{1,0:T(8,128)(2,1)} %grads_ref.1) | copy-start | bytes 196612
  2.3 0.7 %copy-start.5 = (s32[1,256]{1,0:T(1,128)S(1)}, s32[1,256]{1,0:T(1,128)}, u32[]{:S(2)}) copy-start(s32[1,256]{1,0:T(1,128)} %order_ref.1) | copy-start | bytes 3076
  3.2 9.5 %collective-permute-start.5 = (bf16[256,256]{1,0:T(8,128)(2,1)S(1)}, bf16[256,256]{1,0:T(8,128)(2,1)S(1)}, u32[]{:S(2)}, u32[]{:S(2)}) collective-permute-start(bf16[256,256]{1,0:T(8,128)(2,1)S(1)} %order.1.refs_0_), channel_id=1, source_target_pairs={{0,12},{2,14},{4,8},{6,10},{8,4},{10,6},{12,0},{14,2},{1,13},{3,15... | collective-permute-start | bytes 393224 | tf_op jit(solution)/shard_map/ppermute | solution.py:130
  8.3 11.1 %collective-permute-start.3 = (bf16[256,256]{1,0:T(8,128)(2,1)S(1)}, bf16[256,256]{1,0:T(8,128)(2,1)S(1)}, u32[]{:S(2)}, u32[]{:S(2)}) collective-permute-start(bf16[256,256]{1,0:T(8,128)(2,1)S(1)} %order.1.refs_0_), channel_id=1, source_target_pairs={{0,8},{2,10},{4,12},{6,14},{8,0},{10,2},{12,4},{14,6},{1,9},{3,11}... | collective-permute-start | bytes 393224 | tf_op jit(solution)/shard_map/ppermute | solution.py:130
  8.3 12.6 %collective-permute-start.1 = (bf16[256,256]{1,0:T(8,128)(2,1)S(1)}, bf16[256,256]{1,0:T(8,128)(2,1)S(1)}, u32[]{:S(2)}, u32[]{:S(2)}) collective-permute-start(bf16[256,256]{1,0:T(8,128)(2,1)S(1)} %order.1.refs_0_), channel_id=1, source_target_pairs={{0,4},{2,6},{4,0},{6,2},{8,12},{10,14},{12,8},{14,10},{1,5},{3,7},... | collective-permute-start | bytes 393224 | tf_op jit(solution)/shard_map/ppermute | solution.py:130
  9.0 16.6 %collective-permute-start = (bf16[256,256]{1,0:T(8,128)(2,1)S(1)}, bf16[256,256]{1,0:T(8,128)(2,1)S(1)}, u32[]{:S(2)}, u32[]{:S(2)}) collective-permute-start(bf16[256,256]{1,0:T(8,128)(2,1)S(1)} %order.1.refs_0_), channel_id=1, source_target_pairs={{0,2},{2,0},{4,6},{6,4},{8,10},{10,8},{12,14},{14,12},{1,3},{3,1},... | collective-permute-start | bytes 393224 | tf_op jit(solution)/shard_map/ppermute | solution.py:130
  12.8 12.8 %collective-permute-start.6 = (bf16[256,256]{1,0:T(8,128)(2,1)S(1)}, bf16[256,256]{1,0:T(8,128)(2,1)S(1)}, u32[]{:S(2)}, u32[]{:S(2)}) collective-permute-start(bf16[256,256]{1,0:T(8,128)(2,1)S(1)} %collective-permute-done.5.refs_6_), channel_id=1, source_target_pairs={{0,2},{2,0},{4,6},{6,4},{8,10},{10,8},{12,14},{14,12},{1,3},{3,1},... | collective-permute-start | bytes 393224 | tf_op jit(solution)/shard_map/ppermute | solution.py:130
  19.4 6.2 %collective-permute-start.4 = (bf16[256,256]{1,0:T(8,128)(2,1)S(1)}, bf16[256,256]{1,0:T(8,128)(2,1)S(1)}, u32[]{:S(2)}, u32[]{:S(2)}) collective-permute-start(bf16[256,256]{1,0:T(8,128)(2,1)S(1)} %collective-permute-done.3.refs_4_), channel_id=1, source_target_pairs={{0,2},{2,0},{4,6},{6,4},{8,10},{10,8},{12,14},{14,12},{1,3},{3,1},... | collective-permute-start | bytes 393224 | tf_op jit(solution)/shard_map/ppermute | solution.py:130
  20.9 5.8 %collective-permute-start.2 = (bf16[256,256]{1,0:T(8,128)(2,1)S(1)}, bf16[256,256]{1,0:T(8,128)(2,1)S(1)}, u32[]{:S(2)}, u32[]{:S(2)}) collective-permute-start(bf16[256,256]{1,0:T(8,128)(2,1)S(1)} %collective-permute-done.1.refs_2_), channel_id=1, source_target_pairs={{0,2},{2,0},{4,6},{6,4},{8,10},{10,8},{12,14},{14,12},{1,3},{3,1},... | collective-permute-start | bytes 393224 | tf_op jit(solution)/shard_map/ppermute | solution.py:130
  22.1 1.2 %copy-start = (bf16[1,1,32,128,128]{4,3,2,1,0:T(8,128)(2,1)S(1)}, bf16[1,1,32,128,128]{4,3,2,1,0:T(8,128)(2,1)}, u32[]{:S(2)}) copy-start(bf16[1,1,32,128,128]{4,3,2,1,0:T(8,128)(2,1)} %param.13) | copy-start | bytes 3145732
  23.3 0.7 %copy-start.6 = (s32[1,1,32]{2,1,0:T(1,128)S(1)}, s32[1,1,32]{2,1,0:T(1,128)}, u32[]{:S(2)}) copy-start(s32[1,1,32]{2,1,0:T(1,128)} %param.14) | copy-start | bytes 388
  24.0 0.7 %copy-start.7 = (s32[1,1,32]{2,1,0:T(1,128)S(1)}, s32[1,1,32]{2,1,0:T(1,128)}, u32[]{:S(2)}) copy-start(s32[1,1,32]{2,1,0:T(1,128)} %param.15) | copy-start | bytes 388
  25.5 4.0 %copy-start.1 = (bf16[128,256]{1,0:T(8,128)(2,1)S(1)}, bf16[128,256]{1,0:T(8,128)(2,1)}, u32[]{:S(2)}) copy-start(bf16[128,256]{1,0:T(8,128)(2,1)} %first_ref.1) | copy-start | bytes 196612
  25.5 3.9 %copy-start.2 = (bf16[256,128]{1,0:T(8,128)(2,1)S(1)}, bf16[256,128]{1,0:T(8,128)(2,1)}, u32[]{:S(2)}) copy-start(bf16[256,128]{1,0:T(8,128)(2,1)} %second_ref.1) | copy-start | bytes 196612
  27.5 2.0 %collective-permute-start.7 = (f32[512,256]{1,0:T(8,128)S(1)}, f32[512,256]{1,0:T(8,128)S(1)}, u32[]{:S(2)}, u32[]{:S(2)}) collective-permute-start(f32[512,256]{1,0:T(8,128)S(1)} %first.1.mine_ref), channel_id=1, source_target_pairs={{0,1},{1,0},{2,3},{3,2},{4,5},{5,4},{6,7},{7,6},{8,9},{9,8},{10,11... | collective-permute-start | bytes 1572872 | tf_op jit(solution)/shard_map/ppermute | solution.py:130
  30.0 8.3 %collective-permute-start.13 = (bf16[512,128]{1,0:T(8,128)(2,1)S(1)}, bf16[512,128]{1,0:T(8,128)(2,1)S(1)}, u32[]{:S(2)}, u32[]{:S(2)}) collective-permute-start(bf16[512,128]{1,0:T(8,128)(2,1)S(1)} %middle.1.refs_0_), channel_id=1, source_target_pairs={{0,12},{2,14},{4,8},{6,10},{8,4},{10,6},{12,0},{14,2},{1,13},{3,15... | collective-permute-start | bytes 393224 | tf_op jit(solution)/shard_map/ppermute | solution.py:130
  32.4 12.0 %collective-permute-start.11 = (bf16[512,128]{1,0:T(8,128)(2,1)S(1)}, bf16[512,128]{1,0:T(8,128)(2,1)S(1)}, u32[]{:S(2)}, u32[]{:S(2)}) collective-permute-start(bf16[512,128]{1,0:T(8,128)(2,1)S(1)} %middle.1.refs_0_), channel_id=1, source_target_pairs={{0,8},{2,10},{4,12},{6,14},{8,0},{10,2},{12,4},{14,6},{1,9},{3,11}... | collective-permute-start | bytes 393224 | tf_op jit(solution)/shard_map/ppermute | solution.py:130
  32.5 13.4 %collective-permute-start.9 = (bf16[512,128]{1,0:T(8,128)(2,1)S(1)}, bf16[512,128]{1,0:T(8,128)(2,1)S(1)}, u32[]{:S(2)}, u32[]{:S(2)}) collective-permute-start(bf16[512,128]{1,0:T(8,128)(2,1)S(1)} %middle.1.refs_0_), channel_id=1, source_target_pairs={{0,4},{2,6},{4,0},{6,2},{8,12},{10,14},{12,8},{14,10},{1,5},{3,7},... | collective-permute-start | bytes 393224 | tf_op jit(solution)/shard_map/ppermute | solution.py:130
  34.5 11.9 %collective-permute-start.8 = (bf16[512,128]{1,0:T(8,128)(2,1)S(1)}, bf16[512,128]{1,0:T(8,128)(2,1)S(1)}, u32[]{:S(2)}, u32[]{:S(2)}) collective-permute-start(bf16[512,128]{1,0:T(8,128)(2,1)S(1)} %middle.1.refs_0_), channel_id=1, source_target_pairs={{0,2},{2,0},{4,6},{6,4},{8,10},{10,8},{12,14},{14,12},{1,3},{3,1},... | collective-permute-start | bytes 393224 | tf_op jit(solution)/shard_map/ppermute | solution.py:130
  38.4 8.0 %collective-permute-start.14 = (bf16[512,128]{1,0:T(8,128)(2,1)S(1)}, bf16[512,128]{1,0:T(8,128)(2,1)S(1)}, u32[]{:S(2)}, u32[]{:S(2)}) collective-permute-start(bf16[512,128]{1,0:T(8,128)(2,1)S(1)} %collective-permute-done.13.refs_6_), channel_id=1, source_target_pairs={{0,2},{2,0},{4,6},{6,4},{8,10},{10,8},{12,14},{14,12},{1,3},{3,1},... | collective-permute-start | bytes 393224 | tf_op jit(solution)/shard_map/ppermute | solution.py:130
  44.4 6.1 %collective-permute-start.12 = (bf16[512,128]{1,0:T(8,128)(2,1)S(1)}, bf16[512,128]{1,0:T(8,128)(2,1)S(1)}, u32[]{:S(2)}, u32[]{:S(2)}) collective-permute-start(bf16[512,128]{1,0:T(8,128)(2,1)S(1)} %collective-permute-done.11.refs_4_), channel_id=1, source_target_pairs={{0,2},{2,0},{4,6},{6,4},{8,10},{10,8},{12,14},{14,12},{1,3},{3,1},... | collective-permute-start | bytes 393224 | tf_op jit(solution)/shard_map/ppermute | solution.py:130
  45.9 6.0 %collective-permute-start.10 = (bf16[512,128]{1,0:T(8,128)(2,1)S(1)}, bf16[512,128]{1,0:T(8,128)(2,1)S(1)}, u32[]{:S(2)}, u32[]{:S(2)}) collective-permute-start(bf16[512,128]{1,0:T(8,128)(2,1)S(1)} %collective-permute-done.9.refs_2_), channel_id=1, source_target_pairs={{0,2},{2,0},{4,6},{6,4},{8,10},{10,8},{12,14},{14,12},{1,3},{3,1},... | collective-permute-start | bytes 393224 | tf_op jit(solution)/shard_map/ppermute | solution.py:130
  52.6 1.6 %collective-permute-start.15 = (f32[512,128]{1,0:T(8,128)S(1)}, f32[512,128]{1,0:T(8,128)S(1)}, u32[]{:S(2)}, u32[]{:S(2)}) collective-permute-start(f32[512,128]{1,0:T(8,128)S(1)} %get-tuple-element.6.sent_ref), channel_id=1, source_target_pairs={{0,1},{1,0},{2,3},{3,2},{4,5},{5,4},{6,7},{7,6},{8,9},{9,8},{10,11... | collective-permute-start | bytes 786440 | tf_op jit(solution)/shard_map/ppermute | solution.py:130

commit v2 on v1

--- a/solution.py
+++ b/solution.py
@@ -9,7 +9,7 @@
 from jax.sharding import PartitionSpec as P
 
 VMEM = pl.BlockSpec(memory_space=pltpu.VMEM)
-SMEM = pl.BlockSpec(memory_space=pltpu.SMEM)
+HBM = pl.BlockSpec(memory_space=pltpu.HBM)
 
 
 def dot(a, b, contract=((1,), (0,))):
@@ -31,26 +31,36 @@
     )(*args)
 
 
-def order_kernel(order_ref, features_ref, grads_ref, out_ref):
-    nodes, feat = features_ref.shape
+def prepare_kernel(
+    blocks, count_ref, order_hbm, features_hbm, grads_hbm, rows_hbm, cols_hbm, tiles_hbm,
+    out_ref, dense_ref, order_ref, features_ref, rows_ref, cols_ref, tiles_ref, sems,
+):
+    feat = features_hbm.shape[1]
+    pairs = (
+        (rows_hbm, rows_ref), (cols_hbm, cols_ref),
+        (order_hbm, order_ref), (features_hbm, features_ref),
+        (grads_hbm, out_ref.at[:, feat:]), (tiles_hbm, tiles_ref),
+    )
+    copies = [pltpu.make_async_copy(*pair, sems.at[i]) for i, pair in enumerate(pairs)]
+    for copy in copies:
+        copy.start()
+    dense_ref[...] = jnp.zeros_like(dense_ref)
+    for copy in copies[:5]:
+        copy.wait()
+    nodes = features_ref.shape[0]
     source = lax.broadcasted_iota(jnp.int32, (nodes, nodes), 0)
     picks = (source == order_ref[...]).astype(jnp.float32).astype(jnp.bfloat16)
-    ordered = dot(picks, features_ref[...], ((0,), (0,)))
-    out_ref[:, :feat] = ordered.astype(jnp.bfloat16)
-    out_ref[:, feat:] = grads_ref[...]
-
-
-def dense_kernel(blocks, count_ref, rows_ref, cols_ref, tiles_ref, out_ref):
+    out_ref[:, :feat] = dot(picks, features_ref[...], ((0,), (0,))).astype(jnp.bfloat16)
+    copies[5].wait()
     size = tiles_ref.shape[-1]
     own = lax.axis_index("row")
-    out_ref[...] = jnp.zeros_like(out_ref)
 
     def place(slot, carry):
         column = cols_ref[0, slot]
         piece = lax.bitwise_xor(column // blocks, own)
         row_at = pl.multiple_of(rows_ref[0, slot] * size, size)
         col_at = pl.multiple_of((piece * blocks + column % blocks) * size, size)
-        out_ref[pl.ds(row_at, size), pl.ds(col_at, size)] = tiles_ref[slot]
+        dense_ref[pl.ds(row_at, size), pl.ds(col_at, size)] = tiles_ref[slot]
         return carry
 
     lax.fori_loop(0, count_ref[0, 0], place, 0)
@@ -60,7 +70,7 @@
     depth = pieces[0].shape[0]
     for start in range(0, dense_ref.shape[0], chunk):
         total = None
-        for k, piece in enumerate(pieces):
+        for k, piece in zip(piece_order(len(pieces)), pieces):
             term = dot(dense_ref[start : start + chunk, k * depth : (k + 1) * depth], piece[...])
             total = term if total is None else total + term
         yield start, total
@@ -132,14 +142,20 @@
 
 def gather_rows(x):
     size = lax.axis_size("row")
-    inner = 1 << ((size.bit_length() - 1) // 2)
+    near = min(4, size)
     found = {0: x}
-    for mask in range(inner, size, inner):
+    for mask in [*range(near, size, near), *range(1, near)]:
         found[mask] = exchange(x, "row", mask)
-    for low in range(1, inner):
-        for mask in range(0, size, inner):
+    for mask in range(near, size, near):
+        for low in range(1, near):
             found[mask + low] = exchange(found[mask], "row", low)
-    return [found[k] for k in range(size)]
+    return found
+
+
+def piece_order(rows):
+    near = min(4, rows)
+    far = [k for k in range(rows - 1, near - 1, -1)]
+    return [*range(1, near), *far, 0]
 
 
 def shards(
@@ -163,15 +179,30 @@
     shape = jax.ShapeDtypeStruct
     bf16, f32 = jnp.bfloat16, jnp.float32
 
-    source = call(
-        order_kernel, shape((nodes, feat + classes), bf16), [VMEM] * 3,
-        2 * nodes * nodes * feat, "order", node_order, features, logit_grads,
-    )
-    dense = call(
-        functools.partial(dense_kernel, nodes // size), shape((slab, set_nodes), bf16),
-        [SMEM] * 3 + [VMEM], 0, "dense", tile_counts, tile_rows[0], tile_cols[0], tiles,
-    )
-    pieces = gather_rows(source)
+    slots = tiles.shape[0]
+    source, dense = pl.pallas_call(
+        functools.partial(prepare_kernel, nodes // size),
+        out_shape=(shape((nodes, feat + classes), bf16), shape((slab, set_nodes), bf16)),
+        in_specs=[pl.BlockSpec(memory_space=pltpu.SMEM)] + [HBM] * 6,
+        out_specs=(VMEM, VMEM),
+        scratch_shapes=[
+            pltpu.VMEM((1, nodes), jnp.int32),
+            pltpu.VMEM((nodes, feat), bf16),
+            pltpu.SMEM((1, slots), jnp.int32),
+            pltpu.SMEM((1, slots), jnp.int32),
+            pltpu.VMEM(tiles.shape, bf16),
+            pltpu.SemaphoreType.DMA((6,)),
+        ],
+        name="prepare",
+        compiler_params=pltpu.CompilerParams(
+            vmem_limit_bytes=4 * tiles.size + 4 * slab * set_nodes + (8 << 20)
+        ),
+    )(tile_counts, *(
+        pltpu.with_memory_space_constraint(x, pltpu.HBM)
+        for x in (node_order, features, logit_grads, tile_rows[0], tile_cols[0], tiles)
+    ))
+    found = gather_rows(source)
+    pieces = [found[k] for k in piece_order(rows)]
     partial = call(
         first_kernel, shape((slab, feat + classes), f32), [VMEM] * (1 + rows),
         2 * slab * set_nodes * (feat + classes), "first", dense, *pieces,
@@ -181,7 +212,8 @@
         middle_kernel, shape((nodes + hid, classes), bf16), [VMEM] * 4,
         10 * slab * feat * hid, "middle", partial, theirs, weight_first, weight_second,
     )
-    pieces = gather_rows(middle)
+    found = gather_rows(middle)
+    pieces = [found[k] for k in piece_order(rows)]
     keep, send = call(
         second_kernel, (shape((nodes, classes), f32), shape((nodes + hid, classes), f32)),
         [VMEM] * (1 + rows), 2 * slab * set_nodes * classes, "second", dense, *pieces,

time: 55.3 us -> 48.4 us (0.88)
  local copies, waits for them, and re-layouts: 4.89 us -> 0.01 us
  waiting for transfers between devices: 24 us -> 22.3 us
  starting transfers between devices: 20.8 us -> 20.2 us
    unnamed x16 -> x4, local copies, waits for them, and re-layouts: 4.89 us -> 0.01 us
    ppermute x16, waiting for transfers between devices: 24 us -> 22.3 us  [exchange(): return lax.ppermute(x, axis, [(i, i ^ mask) for i in range(size)])]
    pallas_call x0 -> x1, Pallas kernels: none -> 1.57 us  [shards(): pl.pallas_call(functools.partial(prepare_kernel, nodes // size), out_shap...]
    pallas_call x6 -> x4, Pallas kernels: 3.81 us -> 2.72 us  [call(): pl.pallas_call(kernel, out_shape=out_shape, in_specs=in_specs, out_specs=...]
    ppermute x16, starting transfers between devices: 20.8 us -> 20.2 us  [exchange(): return lax.ppermute(x, axis, [(i, i ^ mask) for i in range(size)])]
  transfers between devices with their start and end apart: 16 -> 16, of which waited for: 9 -> 13; matrix products, arithmetic and copies ran while one was open for 0% -> 0% of each run, Pallas kernels for 2% -> 0%
where the time goes in v2:
time: 48.4 us; the launch traced here: 48.2 us
  waiting for transfers between devices  22.3 us (46%)
  starting transfers between devices  20.2 us (42%)
  Pallas kernels  4.29 us (9%)
  between operations  1.36 us (3%)
    ppermute x16, waiting for transfers between devices, exchange(): return lax.ppermute(x, axis, [(i, i ^ mask) for i in range(size)])  22.3 us
    ppermute x16, starting transfers between devices, exchange(): return lax.ppermute(x, axis, [(i, i ^ mask) for i in range(size)])  20.2 us
    pallas_call x4, Pallas kernels, call(): pl.pallas_call(kernel, out_shape=out_shape, in_specs=in_specs, out_specs=...  2.72 us
    pallas_call x1, Pallas kernels, shards(): pl.pallas_call(functools.partial(prepare_kernel, nodes // size), out_shap...  1.57 us
  transfers between devices with their start and end apart: 16, of which 13 were waited for; matrix products, arithmetic and copies ran while one was open for 0% of the time, Pallas kernels for 0%

profile of v2, /device:TPU:0, one launch (start us, length us, event | category | flops | bytes accessed | tf_op | source)
XLA Modules:
  0.0 48.2 jit_solution(12191818452816059250)
XLA Ops:
  1.3 1.6 %prepare.1 = (bf16[256,256]{1,0:T(8,128)(2,1)S(1)}, bf16[512,2048]{1,0:T(8,128)(2,1)S(1)}) custom-call(s32[1,1]{1,0:T(1,128)S(6)} %copy.12.count_ref, s32[1,256]{1,0:T(1,128)} %order_hbm.1, bf16[256,128]{1,0:T(8,128)(2,1)} %features_hbm.1, bf16[256,128]{1,0:T(8,128)(2,1)} %grads_hbm.1, s32[1,32]{1,0:T(1,128)} %bitcast.4, s32[1,32]{1,0:T(1,128)} %bitcast.5, ...), custom_call_target="tpu_custom_call" | custom-call | tf_op jit(solution)/shard_map/prepare/pallas_call | solution.py:183
  2.9 0.0 copy-start
  2.9 0.0 copy-start.1
  2.9 4.1 %collective-permute-start.3 = (bf16[256,256]{1,0:T(8,128)(2,1)S(1)}, bf16[256,256]{1,0:T(8,128)(2,1)S(1)}, u32[]{:S(2)}, u32[]{:S(2)}) collective-permute-start(bf16[256,256]{1,0:T(8,128)(2,1)S(1)} %get-tuple-element.8.refs_7_), channel_id=1, source_target_pairs={{0,8},{2,10},{4,12},{6,14},{8,0},{10,2},{12,4},{14,6},{1,9},{3,11}... | collective-permute-start | bytes 393224 | tf_op jit(solution)/shard_map/ppermute | solution.py:140
  7.0 2.6 %collective-permute-start.2 = (bf16[256,256]{1,0:T(8,128)(2,1)S(1)}, bf16[256,256]{1,0:T(8,128)(2,1)S(1)}, u32[]{:S(2)}, u32[]{:S(2)}) collective-permute-start(bf16[256,256]{1,0:T(8,128)(2,1)S(1)} %get-tuple-element.8.refs_7_), channel_id=1, source_target_pairs={{0,6},{2,4},{4,2},{6,0},{8,14},{10,12},{12,10},{14,8},{1,7},{3,5},... | collective-permute-start | bytes 393224 | tf_op jit(solution)/shard_map/ppermute | solution.py:140
  9.6 0.3 collective-permute-start.1
  9.9 0.5 %collective-permute-start = (bf16[256,256]{1,0:T(8,128)(2,1)S(1)}, bf16[256,256]{1,0:T(8,128)(2,1)S(1)}, u32[]{:S(2)}, u32[]{:S(2)}) collective-permute-start(bf16[256,256]{1,0:T(8,128)(2,1)S(1)} %get-tuple-element.8.refs_7_), channel_id=1, source_target_pairs={{0,2},{2,0},{4,6},{6,4},{8,10},{10,8},{12,14},{14,12},{1,3},{3,1},... | collective-permute-start | bytes 393224 | tf_op jit(solution)/shard_map/ppermute | solution.py:140
  10.5 2.9 %collective-permute-done.3.refs_6_ = bf16[256,256]{1,0:T(8,128)(2,1)S(1)} collective-permute-done((bf16[256,256]{1,0:T(8,128)(2,1)S(1)}, bf16[256,256]{1,0:T(8,128)(2,1)S(1)}, u32[]{:S(2)}, u32[]{:S(2)}) %collective-permute-start.3) | collective-permute-done | bytes 131104 | tf_op jit(solution)/shard_map/ppermute | solution.py:140
  13.4 1.5 %collective-permute-start.6 = (bf16[256,256]{1,0:T(8,128)(2,1)S(1)}, bf16[256,256]{1,0:T(8,128)(2,1)S(1)}, u32[]{:S(2)}, u32[]{:S(2)}) collective-permute-start(bf16[256,256]{1,0:T(8,128)(2,1)S(1)} %collective-permute-done.3.refs_6_), channel_id=1, source_target_pairs={{0,2},{2,0},{4,6},{6,4},{8,10},{10,8},{12,14},{14,12},{1,3},{3,1},... | collective-permute-start | bytes 393224 | tf_op jit(solution)/shard_map/ppermute | solution.py:140
  14.9 0.7 %collective-permute-start.5 = (bf16[256,256]{1,0:T(8,128)(2,1)S(1)}, bf16[256,256]{1,0:T(8,128)(2,1)S(1)}, u32[]{:S(2)}, u32[]{:S(2)}) collective-permute-start(bf16[256,256]{1,0:T(8,128)(2,1)S(1)} %collective-permute-done.3.refs_6_), channel_id=1, source_target_pairs={{0,4},{2,6},{4,0},{6,2},{8,12},{10,14},{12,8},{14,10},{1,5},{3,7},... | collective-permute-start | bytes 393224 | tf_op jit(solution)/shard_map/ppermute | solution.py:140
  15.6 0.0 collective-permute-done.2.refs_2_
  15.6 1.3 %collective-permute-start.4 = (bf16[256,256]{1,0:T(8,128)(2,1)S(1)}, bf16[256,256]{1,0:T(8,128)(2,1)S(1)}, u32[]{:S(2)}, u32[]{:S(2)}) collective-permute-start(bf16[256,256]{1,0:T(8,128)(2,1)S(1)} %collective-permute-done.3.refs_6_), channel_id=1, source_target_pairs={{0,6},{2,4},{4,2},{6,0},{8,14},{10,12},{12,10},{14,8},{1,7},{3,5},... | collective-permute-start | bytes 393224 | tf_op jit(solution)/shard_map/ppermute | solution.py:140
  16.9 1.4 %collective-permute-done.1.refs_1_ = bf16[256,256]{1,0:T(8,128)(2,1)S(1)} collective-permute-done((bf16[256,256]{1,0:T(8,128)(2,1)S(1)}, bf16[256,256]{1,0:T(8,128)(2,1)S(1)}, u32[]{:S(2)}, u32[]{:S(2)}) %collective-permute-start.1) | collective-permute-done | bytes 131104 | tf_op jit(solution)/shard_map/ppermute | solution.py:140
  18.4 0.0 collective-permute-done.refs_0_
  18.4 0.4 collective-permute-done.6.refs_5_
  18.8 2.6 %collective-permute-done.5.refs_4_ = bf16[256,256]{1,0:T(8,128)(2,1)S(1)} collective-permute-done((bf16[256,256]{1,0:T(8,128)(2,1)S(1)}, bf16[256,256]{1,0:T(8,128)(2,1)S(1)}, u32[]{:S(2)}, u32[]{:S(2)}) %collective-permute-start.5) | collective-permute-done | bytes 131104 | tf_op jit(solution)/shard_map/ppermute | solution.py:140
  21.4 1.5 %collective-permute-done.4.refs_3_ = bf16[256,256]{1,0:T(8,128)(2,1)S(1)} collective-permute-done((bf16[256,256]{1,0:T(8,128)(2,1)S(1)}, bf16[256,256]{1,0:T(8,128)(2,1)S(1)}, u32[]{:S(2)}, u32[]{:S(2)}) %collective-permute-start.4) | collective-permute-done | bytes 131104 | tf_op jit(solution)/shard_map/ppermute | solution.py:140
  22.9 0.7 %first.1.mine_ref = f32[512,256]{1,0:T(8,128)S(1)} custom-call(bf16[512,2048]{1,0:T(8,128)(2,1)S(1)} %get-tuple-element.7.dense_ref, bf16[256,256]{1,0:T(8,128)(2,1)S(1)} %collective-permute-done.refs_0_, bf16[256,256]{1,0:T(8,128)(2,1)S(1)} %collective-permute-done.1.refs_1_, bf16[256,256]{1,0:T(8,128)(2,1)S(1)} %collective-permute-done.2.refs_2_, ...), custom_call_target="tpu_custom_call" | custom-call | flops 536870912 | bytes 3670016 | tf_op jit(solution)/shard_map/first/pallas_call | solution.py:23
  23.6 0.1 collective-permute-start.7
  23.7 1.9 %collective-permute-done.7.theirs_ref = f32[512,256]{1,0:T(8,128)S(1)} collective-permute-done((f32[512,256]{1,0:T(8,128)S(1)}, f32[512,256]{1,0:T(8,128)S(1)}, u32[]{:S(2)}, u32[]{:S(2)}) %collective-permute-start.7) | collective-permute-done | bytes 524320 | tf_op jit(solution)/shard_map/ppermute | solution.py:140
  25.6 0.0 copy-done
  25.6 0.0 copy-done.1
  25.6 0.5 %middle.1.refs_7_ = bf16[512,128]{1,0:T(8,128)(2,1)S(1)} custom-call(f32[512,256]{1,0:T(8,128)S(1)} %first.1.mine_ref, f32[512,256]{1,0:T(8,128)S(1)} %collective-permute-done.7.theirs_ref, bf16[128,256]{1,0:T(8,128)(2,1)S(1)} %copy-done, bf16[256,128]{1,0:T(8,128)(2,1)S(1)} %copy-done.1), custom_call_target="tpu_custom_call" | custom-call | flops 167772160 | bytes 1310720 | tf_op jit(solution)/shard_map/middle/pallas_call | solution.py:23
  26.1 2.3 %collective-permute-start.11 = (bf16[512,128]{1,0:T(8,128)(2,1)S(1)}, bf16[512,128]{1,0:T(8,128)(2,1)S(1)}, u32[]{:S(2)}, u32[]{:S(2)}) collective-permute-start(bf16[512,128]{1,0:T(8,128)(2,1)S(1)} %middle.1.refs_7_), channel_id=1, source_target_pairs={{0,8},{2,10},{4,12},{6,14},{8,0},{10,2},{12,4},{14,6},{1,9},{3,11}... | collective-permute-start | bytes 393224 | tf_op jit(solution)/shard_map/ppermute | solution.py:140
  28.4 2.7 %collective-permute-start.10 = (bf16[512,128]{1,0:T(8,128)(2,1)S(1)}, bf16[512,128]{1,0:T(8,128)(2,1)S(1)}, u32[]{:S(2)}, u32[]{:S(2)}) collective-permute-start(bf16[512,128]{1,0:T(8,128)(2,1)S(1)} %middle.1.refs_7_), channel_id=1, source_target_pairs={{0,6},{2,4},{4,2},{6,0},{8,14},{10,12},{12,10},{14,8},{1,7},{3,5},... | collective-permute-start | bytes 393224 | tf_op jit(solution)/shard_map/ppermute | solution.py:140
  31.2 0.3 collective-permute-start.9
  31.5 0.5 %collective-permute-start.8 = (bf16[512,128]{1,0:T(8,128)(2,1)S(1)}, bf16[512,128]{1,0:T(8,128)(2,1)S(1)}, u32[]{:S(2)}, u32[]{:S(2)}) collective-permute-start(bf16[512,128]{1,0:T(8,128)(2,1)S(1)} %middle.1.refs_7_), channel_id=1, source_target_pairs={{0,2},{2,0},{4,6},{6,4},{8,10},{10,8},{12,14},{14,12},{1,3},{3,1},... | collective-permute-start | bytes 393224 | tf_op jit(solution)/shard_map/ppermute | solution.py:140
  31.9 3.6 %collective-permute-done.11.refs_6_ = bf16[512,128]{1,0:T(8,128)(2,1)S(1)} collective-permute-done((bf16[512,128]{1,0:T(8,128)(2,1)S(1)}, bf16[512,128]{1,0:T(8,128)(2,1)S(1)}, u32[]{:S(2)}, u32[]{:S(2)}) %collective-permute-start.11) | collective-permute-done | bytes 131104 | tf_op jit(solution)/shard_map/ppermute | solution.py:140
  35.6 1.6 %collective-permute-start.14 = (bf16[512,128]{1,0:T(8,128)(2,1)S(1)}, bf16[512,128]{1,0:T(8,128)(2,1)S(1)}, u32[]{:S(2)}, u32[]{:S(2)}) collective-permute-start(bf16[512,128]{1,0:T(8,128)(2,1)S(1)} %collective-permute-done.11.refs_6_), channel_id=1, source_target_pairs={{0,2},{2,0},{4,6},{6,4},{8,10},{10,8},{12,14},{14,12},{1,3},{3,1},... | collective-permute-start | bytes 393224 | tf_op jit(solution)/shard_map/ppermute | solution.py:140
  37.2 0.2 collective-permute-start.13
  37.4 0.4 collective-permute-done.10.refs_2_
  37.7 1.3 %collective-permute-start.12 = (bf16[512,128]{1,0:T(8,128)(2,1)S(1)}, bf16[512,128]{1,0:T(8,128)(2,1)S(1)}, u32[]{:S(2)}, u32[]{:S(2)}) collective-permute-start(bf16[512,128]{1,0:T(8,128)(2,1)S(1)} %collective-permute-done.11.refs_6_), channel_id=1, source_target_pairs={{0,6},{2,4},{4,2},{6,0},{8,14},{10,12},{12,10},{14,8},{1,7},{3,5},... | collective-permute-start | bytes 393224 | tf_op jit(solution)/shard_map/ppermute | solution.py:140
  39.0 0.6 %collective-permute-done.9.refs_1_ = bf16[512,128]{1,0:T(8,128)(2,1)S(1)} collective-permute-done((bf16[512,128]{1,0:T(8,128)(2,1)S(1)}, bf16[512,128]{1,0:T(8,128)(2,1)S(1)}, u32[]{:S(2)}, u32[]{:S(2)}) %collective-permute-start.9) | collective-permute-done | bytes 131104 | tf_op jit(solution)/shard_map/ppermute | solution.py:140
  39.6 0.0 collective-permute-done.8.refs_0_
  39.6 0.9 %collective-permute-done.14.refs_5_ = bf16[512,128]{1,0:T(8,128)(2,1)S(1)} collective-permute-done((bf16[512,128]{1,0:T(8,128)(2,1)S(1)}, bf16[512,128]{1,0:T(8,128)(2,1)S(1)}, u32[]{:S(2)}, u32[]{:S(2)}) %collective-permute-start.14) | collective-permute-done | bytes 131104 | tf_op jit(solution)/shard_map/ppermute | solution.py:140
  40.5 2.9 %collective-permute-done.13.refs_4_ = bf16[512,128]{1,0:T(8,128)(2,1)S(1)} collective-permute-done((bf16[512,128]{1,0:T(8,128)(2,1)S(1)}, bf16[512,128]{1,0:T(8,128)(2,1)S(1)}, u32[]{:S(2)}, u32[]{:S(2)}) %collective-permute-start.13) | collective-permute-done | bytes 131104 | tf_op jit(solution)/shard_map/ppermute | solution.py:140
  43.4 1.7 %collective-permute-done.12.refs_3_ = bf16[512,128]{1,0:T(8,128)(2,1)S(1)} collective-permute-done((bf16[512,128]{1,0:T(8,128)(2,1)S(1)}, bf16[512,128]{1,0:T(8,128)(2,1)S(1)}, u32[]{:S(2)}, u32[]{:S(2)}) %collective-permute-start.12) | collective-permute-done | bytes 131104 | tf_op jit(solution)/shard_map/ppermute | solution.py:140
  45.1 0.7 %second.1 = (f32[256,128]{1,0:T(8,128)S(1)}, f32[512,128]{1,0:T(8,128)S(1)}) custom-call(bf16[512,2048]{1,0:T(8,128)(2,1)S(1)} %get-tuple-element.7.dense_ref, bf16[512,128]{1,0:T(8,128)(2,1)S(1)} %collective-permute-done.8.refs_0_, bf16[512,128]{1,0:T(8,128)(2,1)S(1)} %collective-permute-done.9.refs_1_, ...), custom_call_target="tpu_custom_call" | custom-call | flops 268435456 | bytes 3538944 | tf_op jit(solution)/shard_map/second/pallas_call | solution.py:23
  45.8 0.1 collective-permute-start.15
  45.9 1.5 %collective-permute-done.15.theirs_ref = f32[512,128]{1,0:T(8,128)S(1)} collective-permute-done((f32[512,128]{1,0:T(8,128)S(1)}, f32[512,128]{1,0:T(8,128)S(1)}, u32[]{:S(2)}, u32[]{:S(2)}) %collective-permute-start.15) | collective-permute-done | bytes 262176 | tf_op jit(solution)/shard_map/ppermute | solution.py:140
  47.4 0.8 %last.1 = (bf16[256,128]{1,0:T(8,128)(2,1)}, f32[128,256]{1,0:T(8,128)}, f32[256,128]{1,0:T(8,128)}) custom-call(f32[256,128]{1,0:T(8,128)S(1)} %get-tuple-element.9.keep_ref, f32[512,128]{1,0:T(8,128)S(1)} %get-tuple-element.10.sent_ref, f32[512,128]{1,0:T(8,128)S(1)} %collective-permute-done.15.theirs_ref), custom_call_target="tpu_custom_call" | custom-call | bytes 983040 | tf_op jit(solution)/shard_map/last/pallas_call | solution.py:23
Async XLA Ops:
  2.9 22.7 %copy-start = (bf16[128,256]{1,0:T(8,128)(2,1)S(1)}, bf16[128,256]{1,0:T(8,128)(2,1)}, u32[]{:S(2)}) copy-start(bf16[128,256]{1,0:T(8,128)(2,1)} %first_ref.1) | copy-start | bytes 196612
  2.9 22.7 %copy-start.1 = (bf16[256,128]{1,0:T(8,128)(2,1)S(1)}, bf16[256,128]{1,0:T(8,128)(2,1)}, u32[]{:S(2)}) copy-start(bf16[256,128]{1,0:T(8,128)(2,1)} %second_ref.1) | copy-start | bytes 196612
  2.9 10.5 %collective-permute-start.3 = (bf16[256,256]{1,0:T(8,128)(2,1)S(1)}, bf16[256,256]{1,0:T(8,128)(2,1)S(1)}, u32[]{:S(2)}, u32[]{:S(2)}) collective-permute-start(bf16[256,256]{1,0:T(8,128)(2,1)S(1)} %get-tuple-element.8.refs_7_), channel_id=1, source_target_pairs={{0,8},{2,10},{4,12},{6,14},{8,0},{10,2},{12,4},{14,6},{1,9},{3,11}... | collective-permute-start | bytes 393224 | tf_op jit(solution)/shard_map/ppermute | solution.py:140
  7.0 8.6 %collective-permute-start.2 = (bf16[256,256]{1,0:T(8,128)(2,1)S(1)}, bf16[256,256]{1,0:T(8,128)(2,1)S(1)}, u32[]{:S(2)}, u32[]{:S(2)}) collective-permute-start(bf16[256,256]{1,0:T(8,128)(2,1)S(1)} %get-tuple-element.8.refs_7_), channel_id=1, source_target_pairs={{0,6},{2,4},{4,2},{6,0},{8,14},{10,12},{12,10},{14,8},{1,7},{3,5},... | collective-permute-start | bytes 393224 | tf_op jit(solution)/shard_map/ppermute | solution.py:140
  9.6 8.7 %collective-permute-start.1 = (bf16[256,256]{1,0:T(8,128)(2,1)S(1)}, bf16[256,256]{1,0:T(8,128)(2,1)S(1)}, u32[]{:S(2)}, u32[]{:S(2)}) collective-permute-start(bf16[256,256]{1,0:T(8,128)(2,1)S(1)} %get-tuple-element.8.refs_7_), channel_id=1, source_target_pairs={{0,4},{2,6},{4,0},{6,2},{8,12},{10,14},{12,8},{14,10},{1,5},{3,7},... | collective-permute-start | bytes 393224 | tf_op jit(solution)/shard_map/ppermute | solution.py:140
  9.9 8.4 %collective-permute-start = (bf16[256,256]{1,0:T(8,128)(2,1)S(1)}, bf16[256,256]{1,0:T(8,128)(2,1)S(1)}, u32[]{:S(2)}, u32[]{:S(2)}) collective-permute-start(bf16[256,256]{1,0:T(8,128)(2,1)S(1)} %get-tuple-element.8.refs_7_), channel_id=1, source_target_pairs={{0,2},{2,0},{4,6},{6,4},{8,10},{10,8},{12,14},{14,12},{1,3},{3,1},... | collective-permute-start | bytes 393224 | tf_op jit(solution)/shard_map/ppermute | solution.py:140
  13.4 5.4 %collective-permute-start.6 = (bf16[256,256]{1,0:T(8,128)(2,1)S(1)}, bf16[256,256]{1,0:T(8,128)(2,1)S(1)}, u32[]{:S(2)}, u32[]{:S(2)}) collective-permute-start(bf16[256,256]{1,0:T(8,128)(2,1)S(1)} %collective-permute-done.3.refs_6_), channel_id=1, source_target_pairs={{0,2},{2,0},{4,6},{6,4},{8,10},{10,8},{12,14},{14,12},{1,3},{3,1},... | collective-permute-start | bytes 393224 | tf_op jit(solution)/shard_map/ppermute | solution.py:140
  14.9 6.4 %collective-permute-start.5 = (bf16[256,256]{1,0:T(8,128)(2,1)S(1)}, bf16[256,256]{1,0:T(8,128)(2,1)S(1)}, u32[]{:S(2)}, u32[]{:S(2)}) collective-permute-start(bf16[256,256]{1,0:T(8,128)(2,1)S(1)} %collective-permute-done.3.refs_6_), channel_id=1, source_target_pairs={{0,4},{2,6},{4,0},{6,2},{8,12},{10,14},{12,8},{14,10},{1,5},{3,7},... | collective-permute-start | bytes 393224 | tf_op jit(solution)/shard_map/ppermute | solution.py:140
  15.6 7.3 %collective-permute-start.4 = (bf16[256,256]{1,0:T(8,128)(2,1)S(1)}, bf16[256,256]{1,0:T(8,128)(2,1)S(1)}, u32[]{:S(2)}, u32[]{:S(2)}) collective-permute-start(bf16[256,256]{1,0:T(8,128)(2,1)S(1)} %collective-permute-done.3.refs_6_), channel_id=1, source_target_pairs={{0,6},{2,4},{4,2},{6,0},{8,14},{10,12},{12,10},{14,8},{1,7},{3,5},... | collective-permute-start | bytes 393224 | tf_op jit(solution)/shard_map/ppermute | solution.py:140
  23.6 2.0 %collective-permute-start.7 = (f32[512,256]{1,0:T(8,128)S(1)}, f32[512,256]{1,0:T(8,128)S(1)}, u32[]{:S(2)}, u32[]{:S(2)}) collective-permute-start(f32[512,256]{1,0:T(8,128)S(1)} %first.1.mine_ref), channel_id=1, source_target_pairs={{0,1},{1,0},{2,3},{3,2},{4,5},{5,4},{6,7},{7,6},{8,9},{9,8},{10,11... | collective-permute-start | bytes 1572872 | tf_op jit(solution)/shard_map/ppermute | solution.py:140
  26.1 9.4 %collective-permute-start.11 = (bf16[512,128]{1,0:T(8,128)(2,1)S(1)}, bf16[512,128]{1,0:T(8,128)(2,1)S(1)}, u32[]{:S(2)}, u32[]{:S(2)}) collective-permute-start(bf16[512,128]{1,0:T(8,128)(2,1)S(1)} %middle.1.refs_7_), channel_id=1, source_target_pairs={{0,8},{2,10},{4,12},{6,14},{8,0},{10,2},{12,4},{14,6},{1,9},{3,11}... | collective-permute-start | bytes 393224 | tf_op jit(solution)/shard_map/ppermute | solution.py:140
  28.4 9.3 %collective-permute-start.10 = (bf16[512,128]{1,0:T(8,128)(2,1)S(1)}, bf16[512,128]{1,0:T(8,128)(2,1)S(1)}, u32[]{:S(2)}, u32[]{:S(2)}) collective-permute-start(bf16[512,128]{1,0:T(8,128)(2,1)S(1)} %middle.1.refs_7_), channel_id=1, source_target_pairs={{0,6},{2,4},{4,2},{6,0},{8,14},{10,12},{12,10},{14,8},{1,7},{3,5},... | collective-permute-start | bytes 393224 | tf_op jit(solution)/shard_map/ppermute | solution.py:140
  31.2 8.5 %collective-permute-start.9 = (bf16[512,128]{1,0:T(8,128)(2,1)S(1)}, bf16[512,128]{1,0:T(8,128)(2,1)S(1)}, u32[]{:S(2)}, u32[]{:S(2)}) collective-permute-start(bf16[512,128]{1,0:T(8,128)(2,1)S(1)} %middle.1.refs_7_), channel_id=1, source_target_pairs={{0,4},{2,6},{4,0},{6,2},{8,12},{10,14},{12,8},{14,10},{1,5},{3,7},... | collective-permute-start | bytes 393224 | tf_op jit(solution)/shard_map/ppermute | solution.py:140
  31.5 8.2 %collective-permute-start.8 = (bf16[512,128]{1,0:T(8,128)(2,1)S(1)}, bf16[512,128]{1,0:T(8,128)(2,1)S(1)}, u32[]{:S(2)}, u32[]{:S(2)}) collective-permute-start(bf16[512,128]{1,0:T(8,128)(2,1)S(1)} %middle.1.refs_7_), channel_id=1, source_target_pairs={{0,2},{2,0},{4,6},{6,4},{8,10},{10,8},{12,14},{14,12},{1,3},{3,1},... | collective-permute-start | bytes 393224 | tf_op jit(solution)/shard_map/ppermute | solution.py:140
  35.6 5.0 %collective-permute-start.14 = (bf16[512,128]{1,0:T(8,128)(2,1)S(1)}, bf16[512,128]{1,0:T(8,128)(2,1)S(1)}, u32[]{:S(2)}, u32[]{:S(2)}) collective-permute-start(bf16[512,128]{1,0:T(8,128)(2,1)S(1)} %collective-permute-done.11.refs_6_), channel_id=1, source_target_pairs={{0,2},{2,0},{4,6},{6,4},{8,10},{10,8},{12,14},{14,12},{1,3},{3,1},... | collective-permute-start | bytes 393224 | tf_op jit(solution)/shard_map/ppermute | solution.py:140
  37.2 6.3 %collective-permute-start.13 = (bf16[512,128]{1,0:T(8,128)(2,1)S(1)}, bf16[512,128]{1,0:T(8,128)(2,1)S(1)}, u32[]{:S(2)}, u32[]{:S(2)}) collective-permute-start(bf16[512,128]{1,0:T(8,128)(2,1)S(1)} %collective-permute-done.11.refs_6_), channel_id=1, source_target_pairs={{0,4},{2,6},{4,0},{6,2},{8,12},{10,14},{12,8},{14,10},{1,5},{3,7},... | collective-permute-start | bytes 393224 | tf_op jit(solution)/shard_map/ppermute | solution.py:140
  37.7 7.4 %collective-permute-start.12 = (bf16[512,128]{1,0:T(8,128)(2,1)S(1)}, bf16[512,128]{1,0:T(8,128)(2,1)S(1)}, u32[]{:S(2)}, u32[]{:S(2)}) collective-permute-start(bf16[512,128]{1,0:T(8,128)(2,1)S(1)} %collective-permute-done.11.refs_6_), channel_id=1, source_target_pairs={{0,6},{2,4},{4,2},{6,0},{8,14},{10,12},{12,10},{14,8},{1,7},{3,5},... | collective-permute-start | bytes 393224 | tf_op jit(solution)/shard_map/ppermute | solution.py:140
  45.8 1.6 %collective-permute-start.15 = (f32[512,128]{1,0:T(8,128)S(1)}, f32[512,128]{1,0:T(8,128)S(1)}, u32[]{:S(2)}, u32[]{:S(2)}) collective-permute-start(f32[512,128]{1,0:T(8,128)S(1)} %get-tuple-element.10.sent_ref), channel_id=1, source_target_pairs={{0,1},{1,0},{2,3},{3,2},{4,5},{5,4},{6,7},{7,6},{8,9},{9,8},{10,11... | collective-permute-start | bytes 786440 | tf_op jit(solution)/shard_map/ppermute | solution.py:140

commit v3 on v2

--- a/solution.py
+++ b/solution.py
@@ -31,27 +31,32 @@
     )(*args)
 
 
-def prepare_kernel(
-    blocks, count_ref, order_hbm, features_hbm, grads_hbm, rows_hbm, cols_hbm, tiles_hbm,
-    out_ref, dense_ref, order_ref, features_ref, rows_ref, cols_ref, tiles_ref, sems,
-):
-    feat = features_hbm.shape[1]
-    pairs = (
-        (rows_hbm, rows_ref), (cols_hbm, cols_ref),
-        (order_hbm, order_ref), (features_hbm, features_ref),
-        (grads_hbm, out_ref.at[:, feat:]), (tiles_hbm, tiles_ref),
-    )
+def load(pairs, sems):
     copies = [pltpu.make_async_copy(*pair, sems.at[i]) for i, pair in enumerate(pairs)]
     for copy in copies:
         copy.start()
-    dense_ref[...] = jnp.zeros_like(dense_ref)
-    for copy in copies[:5]:
+    return copies
+
+
+def order_kernel(order_hbm, features_hbm, grads_hbm, out_ref, order_ref, features_ref, sems):
+    nodes, feat = features_ref.shape
+    pairs = (
+        (order_hbm, order_ref), (features_hbm, features_ref), (grads_hbm, out_ref.at[:, feat:]),
+    )
+    for copy in load(pairs, sems):
         copy.wait()
-    nodes = features_ref.shape[0]
     source = lax.broadcasted_iota(jnp.int32, (nodes, nodes), 0)
     picks = (source == order_ref[...]).astype(jnp.float32).astype(jnp.bfloat16)
     out_ref[:, :feat] = dot(picks, features_ref[...], ((0,), (0,))).astype(jnp.bfloat16)
-    copies[5].wait()
+
+
+def dense_kernel(
+    blocks, count_ref, rows_hbm, cols_hbm, tiles_hbm, dense_ref, rows_ref, cols_ref, tiles_ref, sems
+):
+    copies = load(((rows_hbm, rows_ref), (cols_hbm, cols_ref), (tiles_hbm, tiles_ref)), sems)
+    dense_ref[...] = jnp.zeros_like(dense_ref)
+    for copy in copies:
+        copy.wait()
     size = tiles_ref.shape[-1]
     own = lax.axis_index("row")
 
@@ -66,20 +71,27 @@
     lax.fori_loop(0, count_ref[0, 0], place, 0)
 
 
-def products(dense_ref, pieces, chunk):
+def products(dense_ref, masks, pieces, chunk):
     depth = pieces[0].shape[0]
     for start in range(0, dense_ref.shape[0], chunk):
         total = None
-        for k, piece in zip(piece_order(len(pieces)), pieces):
+        for k, piece in zip(masks, pieces):
             term = dot(dense_ref[start : start + chunk, k * depth : (k + 1) * depth], piece[...])
             total = term if total is None else total + term
         yield start, total
 
 
-def first_kernel(dense_ref, *refs):
+def early_kernel(masks, dense_ref, *refs):
     *pieces, out_ref = refs
-    for start, total in products(dense_ref, pieces, 128):
+    for start, total in products(dense_ref, masks, pieces, 128):
         out_ref[start : start + 128, :] = total
+
+
+def first_kernel(masks, dense_ref, early_ref, *refs):
+    *pieces, out_ref = refs
+    for start, total in products(dense_ref, masks, pieces, 128):
+        at = slice(start, start + 128)
+        out_ref[at, :] = total + early_ref[at, :]
 
 
 def middle_kernel(mine_ref, theirs_ref, first_ref, second_ref, out_ref):
@@ -95,8 +107,8 @@
     second_half = second_ref[hid_at, :]
 
     at = pl.ds(pl.multiple_of(col * nodes, nodes), nodes)
-    own = (mine_ref[at, :feat] + theirs_ref[at, :feat]).astype(jnp.bfloat16)
-    own_pre = dot(own, first_ref[...])
+    own = mine_ref[at, :feat] + theirs_ref[at, :feat]
+    own_pre = dot(own.astype(jnp.bfloat16), first_ref[...])
     own_hidden = (own_pre * jax.nn.sigmoid(own_pre)).astype(jnp.bfloat16)
     out_ref[:nodes, :] = dot(own_hidden, second_ref[...]).astype(jnp.bfloat16)
 
@@ -109,17 +121,31 @@
     out_ref[nodes + half :, :] = dot(aggregated, pre_grads, ((0,), (0,))).astype(jnp.bfloat16)
 
 
-def second_kernel(dense_ref, *refs):
+def early_logits_kernel(masks, dense_ref, *refs):
+    *pieces, out_ref = refs
+    slab = dense_ref.shape[0]
+    nodes = slab // 2
+    tops = [piece.at[:nodes, :] for piece in pieces]
+    for start, total in products(dense_ref, masks, tops, 128):
+        out_ref[start : start + 128, :] = total
+    grads = pieces[0][nodes:, :].astype(jnp.float32)
+    for piece in pieces[1:]:
+        grads = grads + piece[nodes:, :].astype(jnp.float32)
+    out_ref[slab:, :] = grads
+
+
+def second_kernel(masks, dense_ref, early_ref, *refs):
     *pieces, keep_ref, send_ref = refs
     nodes = keep_ref.shape[0]
     col = lax.axis_index("col")
     tops = [piece.at[:nodes, :] for piece in pieces]
     for where, ref in ((col, keep_ref), (1 - col, send_ref)):
-        slab = dense_ref.at[pl.ds(pl.multiple_of(where * nodes, nodes), nodes), :]
-        for start, total in products(slab, tops, 128):
-            ref[start : start + 128, :] = total
-    grads = pieces[0][nodes:, :].astype(jnp.float32)
-    for piece in pieces[1:]:
+        at = pl.ds(pl.multiple_of(where * nodes, nodes), nodes)
+        early = early_ref.at[at, :]
+        for start, total in products(dense_ref.at[at, :], masks, tops, 128):
+            ref[start : start + 128, :] = total + early[start : start + 128, :]
+    grads = early_ref[2 * nodes :, :]
+    for piece in pieces:
         grads = grads + piece[nodes:, :].astype(jnp.float32)
     send_ref[nodes:, :] = grads
 
@@ -152,10 +178,11 @@
     return found
 
 
-def piece_order(rows):
+def arrival(rows):
     near = min(4, rows)
-    far = [k for k in range(rows - 1, near - 1, -1)]
-    return [*range(1, near), *far, 0]
+    far = [*range(near, rows, near)]
+    last = [mask + low for mask in far for low in (2, 3, 1) if low < near]
+    return [*range(1, near), *far, 0], last
 
 
 def shards(
@@ -180,43 +207,65 @@
     bf16, f32 = jnp.bfloat16, jnp.float32
 
     slots = tiles.shape[0]
-    source, dense = pl.pallas_call(
-        functools.partial(prepare_kernel, nodes // size),
-        out_shape=(shape((nodes, feat + classes), bf16), shape((slab, set_nodes), bf16)),
-        in_specs=[pl.BlockSpec(memory_space=pltpu.SMEM)] + [HBM] * 6,
-        out_specs=(VMEM, VMEM),
+    in_hbm = functools.partial(pltpu.with_memory_space_constraint, memory_space=pltpu.HBM)
+    source = pl.pallas_call(
+        order_kernel,
+        out_shape=shape((nodes, feat + classes), bf16),
+        in_specs=[HBM] * 3,
+        out_specs=VMEM,
         scratch_shapes=[
             pltpu.VMEM((1, nodes), jnp.int32),
             pltpu.VMEM((nodes, feat), bf16),
+            pltpu.SemaphoreType.DMA((3,)),
+        ],
+        name="order",
+        compiler_params=pltpu.CompilerParams(vmem_limit_bytes=8 << 20),
+    )(in_hbm(node_order), in_hbm(features), in_hbm(logit_grads))
+    dense = pl.pallas_call(
+        functools.partial(dense_kernel, nodes // size),
+        out_shape=shape((slab, set_nodes), bf16),
+        in_specs=[pl.BlockSpec(memory_space=pltpu.SMEM)] + [HBM] * 3,
+        out_specs=VMEM,
+        scratch_shapes=[
             pltpu.SMEM((1, slots), jnp.int32),
             pltpu.SMEM((1, slots), jnp.int32),
             pltpu.VMEM(tiles.shape, bf16),
-            pltpu.SemaphoreType.DMA((6,)),
+            pltpu.SemaphoreType.DMA((3,)),
         ],
-        name="prepare",
+        name="dense",
         compiler_params=pltpu.CompilerParams(
             vmem_limit_bytes=4 * tiles.size + 4 * slab * set_nodes + (8 << 20)
         ),
-    )(tile_counts, *(
-        pltpu.with_memory_space_constraint(x, pltpu.HBM)
-        for x in (node_order, features, logit_grads, tile_rows[0], tile_cols[0], tiles)
-    ))
+    )(tile_counts, in_hbm(tile_rows[0]), in_hbm(tile_cols[0]), in_hbm(tiles))
+
+    early, late = arrival(rows)
+    flops = 2 * slab * nodes * (feat + classes)
     found = gather_rows(source)
-    pieces = [found[k] for k in piece_order(rows)]
     partial = call(
-        first_kernel, shape((slab, feat + classes), f32), [VMEM] * (1 + rows),
-        2 * slab * set_nodes * (feat + classes), "first", dense, *pieces,
-    )
-    theirs = exchange(partial, "col", 1)
+        functools.partial(early_kernel, early), shape((slab, feat + classes), f32),
+        [VMEM] * (1 + len(early)), flops * len(early), "early", dense, *(found[k] for k in early),
+    )
+    mine = call(
+        functools.partial(first_kernel, late), shape((slab, feat + classes), f32),
+        [VMEM] * (2 + len(late)), flops * len(late), "first",
+        dense, partial, *(found[k] for k in late),
+    )
     middle = call(
-        middle_kernel, shape((nodes + hid, classes), bf16), [VMEM] * 4,
-        10 * slab * feat * hid, "middle", partial, theirs, weight_first, weight_second,
-    )
+        middle_kernel, shape((nodes + hid, classes), bf16), [VMEM] * 4, 10 * slab * feat * hid,
+        "middle", mine, exchange(mine, "col", 1), weight_first, weight_second,
+    )
+    flops = 2 * slab * nodes * classes
     found = gather_rows(middle)
-    pieces = [found[k] for k in piece_order(rows)]
+    partial = call(
+        functools.partial(early_logits_kernel, early), shape((slab + hid, classes), f32),
+        [VMEM] * (1 + len(early)), flops * len(early), "early_logits",
+        dense, *(found[k] for k in early),
+    )
     keep, send = call(
-        second_kernel, (shape((nodes, classes), f32), shape((nodes + hid, classes), f32)),
-        [VMEM] * (1 + rows), 2 * slab * set_nodes * classes, "second", dense, *pieces,
+        functools.partial(second_kernel, late),
+        (shape((nodes, classes), f32), shape((nodes + hid, classes), f32)),
+        [VMEM] * (2 + len(late)), flops * len(late), "second",
+        dense, partial, *(found[k] for k in late),
     )
     theirs = exchange(send, "col", 1)
     return call(

time: 48.4 us -> 48.1 us (level)
  waiting for transfers between devices: 22.3 us -> 20.1 us
  Pallas kernels: 4.29 us -> 5.72 us
  starting transfers between devices: 20.2 us -> 20.7 us
    ppermute x16, waiting for transfers between devices: 22.3 us -> 20.1 us  [exchange(): return lax.ppermute(x, axis, [(i, i ^ mask) for i in range(size)])]
    pallas_call x1 -> x2, Pallas kernels: 1.57 us -> 2.68 us  [the longest x1 1.53 us: shards(): pl.pallas_call(functools.partial(dense_kernel, nodes // size), out_shape=...]
    pallas_call x4 -> x6, Pallas kernels: 2.72 us -> 3.05 us  [call(): pl.pallas_call(kernel, out_shape=out_shape, in_specs=in_specs, out_specs=...]
  transfers between devices with their start and end apart: 16 -> 16, of which waited for: 13 -> 11; matrix products, arithmetic and copies ran while one was open for 0% -> 0% of each run, Pallas kernels for 0% -> 5%
where the time goes in v3:
time: 48.1 us; the launch traced here: 47.9 us
  starting transfers between devices  20.7 us (43%)
  waiting for transfers between devices  20.1 us (42%)
  Pallas kernels  5.72 us (12%)
  between operations  1.39 us (3%)
    ppermute x16, starting transfers between devices, exchange(): return lax.ppermute(x, axis, [(i, i ^ mask) for i in range(size)])  20.7 us
    ppermute x16, waiting for transfers between devices, exchange(): return lax.ppermute(x, axis, [(i, i ^ mask) for i in range(size)])  20.1 us
    pallas_call x6, Pallas kernels, call(): pl.pallas_call(kernel, out_shape=out_shape, in_specs=in_specs, out_specs=...  3.05 us
    pallas_call x1, Pallas kernels, shards(): pl.pallas_call(functools.partial(dense_kernel, nodes // size), out_shape=...  1.53 us
    pallas_call x1, Pallas kernels, shards(): pl.pallas_call(order_kernel, out_shape=shape((nodes, feat + classes), bf1...  1.15 us
  transfers between devices with their start and end apart: 16, of which 11 were waited for; matrix products, arithmetic and copies ran while one was open for 0% of the time, Pallas kernels for 5%

profile of v3, /device:TPU:0, one launch (start us, length us, event | category | flops | bytes accessed | tf_op | source)
XLA Modules:
  0.0 47.9 jit_solution(4625373139068098910)
XLA Ops:
  0.6 1.1 %order.1.refs_4_ = bf16[256,256]{1,0:T(8,128)(2,1)S(1)} custom-call(s32[1,256]{1,0:T(1,128)} %order_hbm.1, bf16[256,128]{1,0:T(8,128)(2,1)} %features_hbm.1, bf16[256,128]{1,0:T(8,128)(2,1)} %grads_hbm.1), custom_call_target="tpu_custom_call" | custom-call | tf_op jit(solution)/shard_map/order/pallas_call | solution.py:211
  1.8 4.1 %collective-permute-start.3 = (bf16[256,256]{1,0:T(8,128)(2,1)S(1)}, bf16[256,256]{1,0:T(8,128)(2,1)S(1)}, u32[]{:S(2)}, u32[]{:S(2)}) collective-permute-start(bf16[256,256]{1,0:T(8,128)(2,1)S(1)} %order.1.refs_4_), channel_id=1, source_target_pairs={{0,8},{2,10},{4,12},{6,14},{8,0},{10,2},{12,4},{14,6},{1,9},{3,11}... | collective-permute-start | bytes 393224 | tf_op jit(solution)/shard_map/ppermute | solution.py:166
  5.9 1.5 %collective-permute-start = (bf16[256,256]{1,0:T(8,128)(2,1)S(1)}, bf16[256,256]{1,0:T(8,128)(2,1)S(1)}, u32[]{:S(2)}, u32[]{:S(2)}) collective-permute-start(bf16[256,256]{1,0:T(8,128)(2,1)S(1)} %order.1.refs_4_), channel_id=1, source_target_pairs={{0,2},{2,0},{4,6},{6,4},{8,10},{10,8},{12,14},{14,12},{1,3},{3,1},... | collective-permute-start | bytes 393224 | tf_op jit(solution)/shard_map/ppermute | solution.py:166
  7.4 1.6 %collective-permute-start.1 = (bf16[256,256]{1,0:T(8,128)(2,1)S(1)}, bf16[256,256]{1,0:T(8,128)(2,1)S(1)}, u32[]{:S(2)}, u32[]{:S(2)}) collective-permute-start(bf16[256,256]{1,0:T(8,128)(2,1)S(1)} %order.1.refs_4_), channel_id=1, source_target_pairs={{0,4},{2,6},{4,0},{6,2},{8,12},{10,14},{12,8},{14,10},{1,5},{3,7},... | collective-permute-start | bytes 393224 | tf_op jit(solution)/shard_map/ppermute | solution.py:166
  9.0 0.4 collective-permute-start.2
  9.4 2.9 %collective-permute-done.3.refs_3_ = bf16[256,256]{1,0:T(8,128)(2,1)S(1)} collective-permute-done((bf16[256,256]{1,0:T(8,128)(2,1)S(1)}, bf16[256,256]{1,0:T(8,128)(2,1)S(1)}, u32[]{:S(2)}, u32[]{:S(2)}) %collective-permute-start.3) | collective-permute-done | bytes 131104 | tf_op jit(solution)/shard_map/ppermute | solution.py:166
  12.3 0.7 %collective-permute-start.4 = (bf16[256,256]{1,0:T(8,128)(2,1)S(1)}, bf16[256,256]{1,0:T(8,128)(2,1)S(1)}, u32[]{:S(2)}, u32[]{:S(2)}) collective-permute-start(bf16[256,256]{1,0:T(8,128)(2,1)S(1)} %collective-permute-done.3.refs_3_), channel_id=1, source_target_pairs={{0,4},{2,6},{4,0},{6,2},{8,12},{10,14},{12,8},{14,10},{1,5},{3,7},... | collective-permute-start | bytes 393224 | tf_op jit(solution)/shard_map/ppermute | solution.py:166
  13.0 2.4 %collective-permute-start.5 = (bf16[256,256]{1,0:T(8,128)(2,1)S(1)}, bf16[256,256]{1,0:T(8,128)(2,1)S(1)}, u32[]{:S(2)}, u32[]{:S(2)}) collective-permute-start(bf16[256,256]{1,0:T(8,128)(2,1)S(1)} %collective-permute-done.3.refs_3_), channel_id=1, source_target_pairs={{0,6},{2,4},{4,2},{6,0},{8,14},{10,12},{12,10},{14,8},{1,7},{3,5},... | collective-permute-start | bytes 393224 | tf_op jit(solution)/shard_map/ppermute | solution.py:166
  15.3 0.0 collective-permute-done.refs_0_
  15.3 0.5 collective-permute-start.6
  16.4 1.5 %dense.1.dense_ref = bf16[512,2048]{1,0:T(8,128)(2,1)S(1)} custom-call(s32[1,1]{1,0:T(1,128)S(6)} %copy.12.count_ref, s32[1,32]{1,0:T(1,128)} %bitcast.4, s32[1,32]{1,0:T(1,128)} %bitcast.5, bf16[32,128,128]{2,1,0:T(8,128)(2,1)} %bitcast.3), custom_call_target="tpu_custom_call" | custom-call | tf_op jit(solution)/shard_map/dense/pallas_call | solution.py:224
  18.0 0.0 collective-permute-done.1.refs_1_
  18.0 0.0 collective-permute-done.2.refs_2_
  18.0 0.5 %early.1.early_ref = f32[512,256]{1,0:T(8,128)S(1)} custom-call(bf16[512,2048]{1,0:T(8,128)(2,1)S(1)} %dense.1.dense_ref, bf16[256,256]{1,0:T(8,128)(2,1)S(1)} %collective-permute-done.refs_0_, bf16[256,256]{1,0:T(8,128)(2,1)S(1)} %collective-permute-done.1.refs_1_, bf16[256,256]{1,0:T(8,128)(2,1)S(1)} %collective-permute-done.2.refs_2_, ...), custom_call_target="tpu_custom_call" | custom-call | flops 335544320 | bytes 3276800 | tf_op jit(solution)/shard_map/early/pallas_call | solution.py:23
  18.5 0.0 copy-start
  18.5 0.0 copy-start.1
  18.6 1.8 %collective-permute-done.4.refs_0_ = bf16[256,256]{1,0:T(8,128)(2,1)S(1)} collective-permute-done((bf16[256,256]{1,0:T(8,128)(2,1)S(1)}, bf16[256,256]{1,0:T(8,128)(2,1)S(1)}, u32[]{:S(2)}, u32[]{:S(2)}) %collective-permute-start.4) | collective-permute-done | bytes 131104 | tf_op jit(solution)/shard_map/ppermute | solution.py:166
  20.4 1.9 %collective-permute-done.5.refs_1_ = bf16[256,256]{1,0:T(8,128)(2,1)S(1)} collective-permute-done((bf16[256,256]{1,0:T(8,128)(2,1)S(1)}, bf16[256,256]{1,0:T(8,128)(2,1)S(1)}, u32[]{:S(2)}, u32[]{:S(2)}) %collective-permute-start.5) | collective-permute-done | bytes 131104 | tf_op jit(solution)/shard_map/ppermute | solution.py:166
  22.3 0.5 %collective-permute-done.6.refs_2_ = bf16[256,256]{1,0:T(8,128)(2,1)S(1)} collective-permute-done((bf16[256,256]{1,0:T(8,128)(2,1)S(1)}, bf16[256,256]{1,0:T(8,128)(2,1)S(1)}, u32[]{:S(2)}, u32[]{:S(2)}) %collective-permute-start.6) | collective-permute-done | bytes 131104 | tf_op jit(solution)/shard_map/ppermute | solution.py:166
  22.8 0.4 first.1.mine_ref
  23.2 0.1 collective-permute-start.7
  23.3 1.9 %collective-permute-done.7.theirs_ref = f32[512,256]{1,0:T(8,128)S(1)} collective-permute-done((f32[512,256]{1,0:T(8,128)S(1)}, f32[512,256]{1,0:T(8,128)S(1)}, u32[]{:S(2)}, u32[]{:S(2)}) %collective-permute-start.7) | collective-permute-done | bytes 524320 | tf_op jit(solution)/shard_map/ppermute | solution.py:166
  25.2 0.0 copy-done
  25.2 0.0 copy-done.1
  25.2 0.5 %middle.1.refs_4_ = bf16[512,128]{1,0:T(8,128)(2,1)S(1)} custom-call(f32[512,256]{1,0:T(8,128)S(1)} %first.1.mine_ref, f32[512,256]{1,0:T(8,128)S(1)} %collective-permute-done.7.theirs_ref, bf16[128,256]{1,0:T(8,128)(2,1)S(1)} %copy-done, bf16[256,128]{1,0:T(8,128)(2,1)S(1)} %copy-done.1), custom_call_target="tpu_custom_call" | custom-call | flops 167772160 | bytes 1310720 | tf_op jit(solution)/shard_map/middle/pallas_call | solution.py:23
  25.7 2.5 %collective-permute-start.11 = (bf16[512,128]{1,0:T(8,128)(2,1)S(1)}, bf16[512,128]{1,0:T(8,128)(2,1)S(1)}, u32[]{:S(2)}, u32[]{:S(2)}) collective-permute-start(bf16[512,128]{1,0:T(8,128)(2,1)S(1)} %middle.1.refs_4_), channel_id=1, source_target_pairs={{0,8},{2,10},{4,12},{6,14},{8,0},{10,2},{12,4},{14,6},{1,9},{3,11}... | collective-permute-start | bytes 393224 | tf_op jit(solution)/shard_map/ppermute | solution.py:166
  28.2 1.8 %collective-permute-start.10 = (bf16[512,128]{1,0:T(8,128)(2,1)S(1)}, bf16[512,128]{1,0:T(8,128)(2,1)S(1)}, u32[]{:S(2)}, u32[]{:S(2)}) collective-permute-start(bf16[512,128]{1,0:T(8,128)(2,1)S(1)} %middle.1.refs_4_), channel_id=1, source_target_pairs={{0,6},{2,4},{4,2},{6,0},{8,14},{10,12},{12,10},{14,8},{1,7},{3,5},... | collective-permute-start | bytes 393224 | tf_op jit(solution)/shard_map/ppermute | solution.py:166
  30.0 1.4 %collective-permute-start.8 = (bf16[512,128]{1,0:T(8,128)(2,1)S(1)}, bf16[512,128]{1,0:T(8,128)(2,1)S(1)}, u32[]{:S(2)}, u32[]{:S(2)}) collective-permute-start(bf16[512,128]{1,0:T(8,128)(2,1)S(1)} %middle.1.refs_4_), channel_id=1, source_target_pairs={{0,2},{2,0},{4,6},{6,4},{8,10},{10,8},{12,14},{14,12},{1,3},{3,1},... | collective-permute-start | bytes 393224 | tf_op jit(solution)/shard_map/ppermute | solution.py:166
  31.4 0.3 collective-permute-start.9
  31.7 3.4 %collective-permute-done.11.refs_3_ = bf16[512,128]{1,0:T(8,128)(2,1)S(1)} collective-permute-done((bf16[512,128]{1,0:T(8,128)(2,1)S(1)}, bf16[512,128]{1,0:T(8,128)(2,1)S(1)}, u32[]{:S(2)}, u32[]{:S(2)}) %collective-permute-start.11) | collective-permute-done | bytes 131104 | tf_op jit(solution)/shard_map/ppermute | solution.py:166
  35.1 0.5 %collective-permute-start.12 = (bf16[512,128]{1,0:T(8,128)(2,1)S(1)}, bf16[512,128]{1,0:T(8,128)(2,1)S(1)}, u32[]{:S(2)}, u32[]{:S(2)}) collective-permute-start(bf16[512,128]{1,0:T(8,128)(2,1)S(1)} %collective-permute-done.11.refs_3_), channel_id=1, source_target_pairs={{0,4},{2,6},{4,0},{6,2},{8,12},{10,14},{12,8},{14,10},{1,5},{3,7},... | collective-permute-start | bytes 393224 | tf_op jit(solution)/shard_map/ppermute | solution.py:166
  35.6 1.8 %collective-permute-start.13 = (bf16[512,128]{1,0:T(8,128)(2,1)S(1)}, bf16[512,128]{1,0:T(8,128)(2,1)S(1)}, u32[]{:S(2)}, u32[]{:S(2)}) collective-permute-start(bf16[512,128]{1,0:T(8,128)(2,1)S(1)} %collective-permute-done.11.refs_3_), channel_id=1, source_target_pairs={{0,6},{2,4},{4,2},{6,0},{8,14},{10,12},{12,10},{14,8},{1,7},{3,5},... | collective-permute-start | bytes 393224 | tf_op jit(solution)/shard_map/ppermute | solution.py:166
  37.4 0.1 collective-permute-done.10.refs_2_
  37.5 1.1 %collective-permute-start.14 = (bf16[512,128]{1,0:T(8,128)(2,1)S(1)}, bf16[512,128]{1,0:T(8,128)(2,1)S(1)}, u32[]{:S(2)}, u32[]{:S(2)}) collective-permute-start(bf16[512,128]{1,0:T(8,128)(2,1)S(1)} %collective-permute-done.11.refs_3_), channel_id=1, source_target_pairs={{0,2},{2,0},{4,6},{6,4},{8,10},{10,8},{12,14},{14,12},{1,3},{3,1},... | collective-permute-start | bytes 393224 | tf_op jit(solution)/shard_map/ppermute | solution.py:166
  38.6 0.0 collective-permute-done.8.refs_0_
  38.6 0.0 collective-permute-done.9.refs_1_
  38.6 0.5 %early_logits.1.early_ref = f32[768,128]{1,0:T(8,128)S(1)} custom-call(bf16[512,2048]{1,0:T(8,128)(2,1)S(1)} %dense.1.dense_ref, bf16[512,128]{1,0:T(8,128)(2,1)S(1)} %collective-permute-done.8.refs_0_, bf16[512,128]{1,0:T(8,128)(2,1)S(1)} %collective-permute-done.9.refs_1_, bf16[512,128]{1,0:T(8,128)(2,1)S(1)} %collective-permute-done.10.refs_2_, ...), custom_call_target="tpu_custom_call" | custom-call | flops 167772160 | bytes 3145728 | tf_op jit(solution)/shard_map/early_logits/pallas_call | solution.py:23
  39.1 2.4 %collective-permute-done.12.refs_0_ = bf16[512,128]{1,0:T(8,128)(2,1)S(1)} collective-permute-done((bf16[512,128]{1,0:T(8,128)(2,1)S(1)}, bf16[512,128]{1,0:T(8,128)(2,1)S(1)}, u32[]{:S(2)}, u32[]{:S(2)}) %collective-permute-start.12) | collective-permute-done | bytes 131104 | tf_op jit(solution)/shard_map/ppermute | solution.py:166
  41.6 3.3 %collective-permute-done.13.refs_1_ = bf16[512,128]{1,0:T(8,128)(2,1)S(1)} collective-permute-done((bf16[512,128]{1,0:T(8,128)(2,1)S(1)}, bf16[512,128]{1,0:T(8,128)(2,1)S(1)}, u32[]{:S(2)}, u32[]{:S(2)}) %collective-permute-start.13) | collective-permute-done | bytes 131104 | tf_op jit(solution)/shard_map/ppermute | solution.py:166
  44.9 0.3 collective-permute-done.14.refs_2_
  45.2 0.4 second.1
  45.5 0.1 collective-permute-start.15
  45.6 1.5 %collective-permute-done.15.theirs_ref = f32[512,128]{1,0:T(8,128)S(1)} collective-permute-done((f32[512,128]{1,0:T(8,128)S(1)}, f32[512,128]{1,0:T(8,128)S(1)}, u32[]{:S(2)}, u32[]{:S(2)}) %collective-permute-start.15) | collective-permute-done | bytes 262176 | tf_op jit(solution)/shard_map/ppermute | solution.py:166
  47.1 0.8 %last.1 = (bf16[256,128]{1,0:T(8,128)(2,1)}, f32[128,256]{1,0:T(8,128)}, f32[256,128]{1,0:T(8,128)}) custom-call(f32[256,128]{1,0:T(8,128)S(1)} %get-tuple-element.5.keep_ref, f32[512,128]{1,0:T(8,128)S(1)} %get-tuple-element.6.sent_ref, f32[512,128]{1,0:T(8,128)S(1)} %collective-permute-done.15.theirs_ref), custom_call_target="tpu_custom_call" | custom-call | bytes 983040 | tf_op jit(solution)/shard_map/last/pallas_call | solution.py:23
Async XLA Ops:
  1.8 10.5 %collective-permute-start.3 = (bf16[256,256]{1,0:T(8,128)(2,1)S(1)}, bf16[256,256]{1,0:T(8,128)(2,1)S(1)}, u32[]{:S(2)}, u32[]{:S(2)}) collective-permute-start(bf16[256,256]{1,0:T(8,128)(2,1)S(1)} %order.1.refs_4_), channel_id=1, source_target_pairs={{0,8},{2,10},{4,12},{6,14},{8,0},{10,2},{12,4},{14,6},{1,9},{3,11}... | collective-permute-start | bytes 393224 | tf_op jit(solution)/shard_map/ppermute | solution.py:166
  5.9 9.4 %collective-permute-start = (bf16[256,256]{1,0:T(8,128)(2,1)S(1)}, bf16[256,256]{1,0:T(8,128)(2,1)S(1)}, u32[]{:S(2)}, u32[]{:S(2)}) collective-permute-start(bf16[256,256]{1,0:T(8,128)(2,1)S(1)} %order.1.refs_4_), channel_id=1, source_target_pairs={{0,2},{2,0},{4,6},{6,4},{8,10},{10,8},{12,14},{14,12},{1,3},{3,1},... | collective-permute-start | bytes 393224 | tf_op jit(solution)/shard_map/ppermute | solution.py:166
  7.4 10.6 %collective-permute-start.1 = (bf16[256,256]{1,0:T(8,128)(2,1)S(1)}, bf16[256,256]{1,0:T(8,128)(2,1)S(1)}, u32[]{:S(2)}, u32[]{:S(2)}) collective-permute-start(bf16[256,256]{1,0:T(8,128)(2,1)S(1)} %order.1.refs_4_), channel_id=1, source_target_pairs={{0,4},{2,6},{4,0},{6,2},{8,12},{10,14},{12,8},{14,10},{1,5},{3,7},... | collective-permute-start | bytes 393224 | tf_op jit(solution)/shard_map/ppermute | solution.py:166
  9.0 9.0 %collective-permute-start.2 = (bf16[256,256]{1,0:T(8,128)(2,1)S(1)}, bf16[256,256]{1,0:T(8,128)(2,1)S(1)}, u32[]{:S(2)}, u32[]{:S(2)}) collective-permute-start(bf16[256,256]{1,0:T(8,128)(2,1)S(1)} %order.1.refs_4_), channel_id=1, source_target_pairs={{0,6},{2,4},{4,2},{6,0},{8,14},{10,12},{12,10},{14,8},{1,7},{3,5},... | collective-permute-start | bytes 393224 | tf_op jit(solution)/shard_map/ppermute | solution.py:166
  12.3 8.1 %collective-permute-start.4 = (bf16[256,256]{1,0:T(8,128)(2,1)S(1)}, bf16[256,256]{1,0:T(8,128)(2,1)S(1)}, u32[]{:S(2)}, u32[]{:S(2)}) collective-permute-start(bf16[256,256]{1,0:T(8,128)(2,1)S(1)} %collective-permute-done.3.refs_3_), channel_id=1, source_target_pairs={{0,4},{2,6},{4,0},{6,2},{8,12},{10,14},{12,8},{14,10},{1,5},{3,7},... | collective-permute-start | bytes 393224 | tf_op jit(solution)/shard_map/ppermute | solution.py:166
  13.0 9.4 %collective-permute-start.5 = (bf16[256,256]{1,0:T(8,128)(2,1)S(1)}, bf16[256,256]{1,0:T(8,128)(2,1)S(1)}, u32[]{:S(2)}, u32[]{:S(2)}) collective-permute-start(bf16[256,256]{1,0:T(8,128)(2,1)S(1)} %collective-permute-done.3.refs_3_), channel_id=1, source_target_pairs={{0,6},{2,4},{4,2},{6,0},{8,14},{10,12},{12,10},{14,8},{1,7},{3,5},... | collective-permute-start | bytes 393224 | tf_op jit(solution)/shard_map/ppermute | solution.py:166
  15.3 7.5 %collective-permute-start.6 = (bf16[256,256]{1,0:T(8,128)(2,1)S(1)}, bf16[256,256]{1,0:T(8,128)(2,1)S(1)}, u32[]{:S(2)}, u32[]{:S(2)}) collective-permute-start(bf16[256,256]{1,0:T(8,128)(2,1)S(1)} %collective-permute-done.3.refs_3_), channel_id=1, source_target_pairs={{0,2},{2,0},{4,6},{6,4},{8,10},{10,8},{12,14},{14,12},{1,3},{3,1},... | collective-permute-start | bytes 393224 | tf_op jit(solution)/shard_map/ppermute | solution.py:166
  18.5 6.6 %copy-start = (bf16[128,256]{1,0:T(8,128)(2,1)S(1)}, bf16[128,256]{1,0:T(8,128)(2,1)}, u32[]{:S(2)}) copy-start(bf16[128,256]{1,0:T(8,128)(2,1)} %first_ref.1) | copy-start | bytes 196612
  18.5 6.6 %copy-start.1 = (bf16[256,128]{1,0:T(8,128)(2,1)S(1)}, bf16[256,128]{1,0:T(8,128)(2,1)}, u32[]{:S(2)}) copy-start(bf16[256,128]{1,0:T(8,128)(2,1)} %second_ref.1) | copy-start | bytes 196612
  23.2 2.0 %collective-permute-start.7 = (f32[512,256]{1,0:T(8,128)S(1)}, f32[512,256]{1,0:T(8,128)S(1)}, u32[]{:S(2)}, u32[]{:S(2)}) collective-permute-start(f32[512,256]{1,0:T(8,128)S(1)} %first.1.mine_ref), channel_id=1, source_target_pairs={{0,1},{1,0},{2,3},{3,2},{4,5},{5,4},{6,7},{7,6},{8,9},{9,8},{10,11... | collective-permute-start | bytes 1572872 | tf_op jit(solution)/shard_map/ppermute | solution.py:166
  25.7 9.4 %collective-permute-start.11 = (bf16[512,128]{1,0:T(8,128)(2,1)S(1)}, bf16[512,128]{1,0:T(8,128)(2,1)S(1)}, u32[]{:S(2)}, u32[]{:S(2)}) collective-permute-start(bf16[512,128]{1,0:T(8,128)(2,1)S(1)} %middle.1.refs_4_), channel_id=1, source_target_pairs={{0,8},{2,10},{4,12},{6,14},{8,0},{10,2},{12,4},{14,6},{1,9},{3,11}... | collective-permute-start | bytes 393224 | tf_op jit(solution)/shard_map/ppermute | solution.py:166
  28.2 9.2 %collective-permute-start.10 = (bf16[512,128]{1,0:T(8,128)(2,1)S(1)}, bf16[512,128]{1,0:T(8,128)(2,1)S(1)}, u32[]{:S(2)}, u32[]{:S(2)}) collective-permute-start(bf16[512,128]{1,0:T(8,128)(2,1)S(1)} %middle.1.refs_4_), channel_id=1, source_target_pairs={{0,6},{2,4},{4,2},{6,0},{8,14},{10,12},{12,10},{14,8},{1,7},{3,5},... | collective-permute-start | bytes 393224 | tf_op jit(solution)/shard_map/ppermute | solution.py:166
  30.0 8.6 %collective-permute-start.8 = (bf16[512,128]{1,0:T(8,128)(2,1)S(1)}, bf16[512,128]{1,0:T(8,128)(2,1)S(1)}, u32[]{:S(2)}, u32[]{:S(2)}) collective-permute-start(bf16[512,128]{1,0:T(8,128)(2,1)S(1)} %middle.1.refs_4_), channel_id=1, source_target_pairs={{0,2},{2,0},{4,6},{6,4},{8,10},{10,8},{12,14},{14,12},{1,3},{3,1},... | collective-permute-start | bytes 393224 | tf_op jit(solution)/shard_map/ppermute | solution.py:166
  31.4 7.2 %collective-permute-start.9 = (bf16[512,128]{1,0:T(8,128)(2,1)S(1)}, bf16[512,128]{1,0:T(8,128)(2,1)S(1)}, u32[]{:S(2)}, u32[]{:S(2)}) collective-permute-start(bf16[512,128]{1,0:T(8,128)(2,1)S(1)} %middle.1.refs_4_), channel_id=1, source_target_pairs={{0,4},{2,6},{4,0},{6,2},{8,12},{10,14},{12,8},{14,10},{1,5},{3,7},... | collective-permute-start | bytes 393224 | tf_op jit(solution)/shard_map/ppermute | solution.py:166
  35.1 6.4 %collective-permute-start.12 = (bf16[512,128]{1,0:T(8,128)(2,1)S(1)}, bf16[512,128]{1,0:T(8,128)(2,1)S(1)}, u32[]{:S(2)}, u32[]{:S(2)}) collective-permute-start(bf16[512,128]{1,0:T(8,128)(2,1)S(1)} %collective-permute-done.11.refs_3_), channel_id=1, source_target_pairs={{0,4},{2,6},{4,0},{6,2},{8,12},{10,14},{12,8},{14,10},{1,5},{3,7},... | collective-permute-start | bytes 393224 | tf_op jit(solution)/shard_map/ppermute | solution.py:166
  35.6 9.3 %collective-permute-start.13 = (bf16[512,128]{1,0:T(8,128)(2,1)S(1)}, bf16[512,128]{1,0:T(8,128)(2,1)S(1)}, u32[]{:S(2)}, u32[]{:S(2)}) collective-permute-start(bf16[512,128]{1,0:T(8,128)(2,1)S(1)} %collective-permute-done.11.refs_3_), channel_id=1, source_target_pairs={{0,6},{2,4},{4,2},{6,0},{8,14},{10,12},{12,10},{14,8},{1,7},{3,5},... | collective-permute-start | bytes 393224 | tf_op jit(solution)/shard_map/ppermute | solution.py:166
  37.5 7.7 %collective-permute-start.14 = (bf16[512,128]{1,0:T(8,128)(2,1)S(1)}, bf16[512,128]{1,0:T(8,128)(2,1)S(1)}, u32[]{:S(2)}, u32[]{:S(2)}) collective-permute-start(bf16[512,128]{1,0:T(8,128)(2,1)S(1)} %collective-permute-done.11.refs_3_), channel_id=1, source_target_pairs={{0,2},{2,0},{4,6},{6,4},{8,10},{10,8},{12,14},{14,12},{1,3},{3,1},... | collective-permute-start | bytes 393224 | tf_op jit(solution)/shard_map/ppermute | solution.py:166
  45.5 1.6 %collective-permute-start.15 = (f32[512,128]{1,0:T(8,128)S(1)}, f32[512,128]{1,0:T(8,128)S(1)}, u32[]{:S(2)}, u32[]{:S(2)}) collective-permute-start(f32[512,128]{1,0:T(8,128)S(1)} %get-tuple-element.6.sent_ref), channel_id=1, source_target_pairs={{0,1},{1,0},{2,3},{3,2},{4,5},{5,4},{6,7},{7,6},{8,9},{9,8},{10,11... | collective-permute-start | bytes 786440 | tf_op jit(solution)/shard_map/ppermute | solution.py:166

commit v4 on v3

--- a/solution.py
+++ b/solution.py
@@ -181,8 +181,8 @@
 def arrival(rows):
     near = min(4, rows)
     far = [*range(near, rows, near)]
-    last = [mask + low for mask in far for low in (2, 3, 1) if low < near]
-    return [*range(1, near), *far, 0], last
+    order = [low for low in (3, 1, 2) if low < near]
+    return [*order, *far, 0], [mask + low for mask in far for low in order]
 
 
 def shards(

time: 48.1 us -> 45.7 us (0.950)
  waiting for transfers between devices: 20.1 us -> 18 us
    ppermute x16, waiting for transfers between devices: 20.1 us -> 18 us  [exchange(): return lax.ppermute(x, axis, [(i, i ^ mask) for i in range(size)])]
  transfers between devices with their start and end apart: 16 -> 16, of which waited for: 11 -> 10; matrix products, arithmetic and copies ran while one was open for 0% -> 0% of each run, Pallas kernels for 5% -> 5%
where the time goes in v4:
time: 45.7 us; the launch traced here: 45.5 us
  starting transfers between devices  20.4 us (45%)
  waiting for transfers between devices  18 us (39%)
  Pallas kernels  5.64 us (12%)
  between operations  1.39 us (3%)
    ppermute x16, starting transfers between devices, exchange(): return lax.ppermute(x, axis, [(i, i ^ mask) for i in range(size)])  20.4 us
    ppermute x16, waiting for transfers between devices, exchange(): return lax.ppermute(x, axis, [(i, i ^ mask) for i in range(size)])  18 us
    pallas_call x6, Pallas kernels, call(): pl.pallas_call(kernel, out_shape=out_shape, in_specs=in_specs, out_specs=...  3.04 us
    pallas_call x1, Pallas kernels, shards(): pl.pallas_call(functools.partial(dense_kernel, nodes // size), out_shape=...  1.46 us
    pallas_call x1, Pallas kernels, shards(): pl.pallas_call(order_kernel, out_shape=shape((nodes, feat + classes), bf1...  1.15 us
  transfers between devices with their start and end apart: 16, of which 10 were waited for; matrix products, arithmetic and copies ran while one was open for 0% of the time, Pallas kernels for 5%

profile of v4, /device:TPU:0, one launch (start us, length us, event | category | flops | bytes accessed | tf_op | source)
XLA Modules:
  0.0 45.5 jit_solution(12258364613340296825)
XLA Ops:
  0.6 1.1 %order.1.refs_4_ = bf16[256,256]{1,0:T(8,128)(2,1)S(1)} custom-call(s32[1,256]{1,0:T(1,128)} %order_hbm.1, bf16[256,128]{1,0:T(8,128)(2,1)} %features_hbm.1, bf16[256,128]{1,0:T(8,128)(2,1)} %grads_hbm.1), custom_call_target="tpu_custom_call" | custom-call | tf_op jit(solution)/shard_map/order/pallas_call | solution.py:211
  1.8 4.1 %collective-permute-start.3 = (bf16[256,256]{1,0:T(8,128)(2,1)S(1)}, bf16[256,256]{1,0:T(8,128)(2,1)S(1)}, u32[]{:S(2)}, u32[]{:S(2)}) collective-permute-start(bf16[256,256]{1,0:T(8,128)(2,1)S(1)} %order.1.refs_4_), channel_id=1, source_target_pairs={{0,8},{2,10},{4,12},{6,14},{8,0},{10,2},{12,4},{14,6},{1,9},{3,11}... | collective-permute-start | bytes 393224 | tf_op jit(solution)/shard_map/ppermute | solution.py:166
  5.9 2.5 %collective-permute-start = (bf16[256,256]{1,0:T(8,128)(2,1)S(1)}, bf16[256,256]{1,0:T(8,128)(2,1)S(1)}, u32[]{:S(2)}, u32[]{:S(2)}) collective-permute-start(bf16[256,256]{1,0:T(8,128)(2,1)S(1)} %order.1.refs_4_), channel_id=1, source_target_pairs={{0,6},{2,4},{4,2},{6,0},{8,14},{10,12},{12,10},{14,8},{1,7},{3,5},... | collective-permute-start | bytes 393224 | tf_op jit(solution)/shard_map/ppermute | solution.py:166
  8.4 0.5 %collective-permute-start.1 = (bf16[256,256]{1,0:T(8,128)(2,1)S(1)}, bf16[256,256]{1,0:T(8,128)(2,1)S(1)}, u32[]{:S(2)}, u32[]{:S(2)}) collective-permute-start(bf16[256,256]{1,0:T(8,128)(2,1)S(1)} %order.1.refs_4_), channel_id=1, source_target_pairs={{0,2},{2,0},{4,6},{6,4},{8,10},{10,8},{12,14},{14,12},{1,3},{3,1},... | collective-permute-start | bytes 393224 | tf_op jit(solution)/shard_map/ppermute | solution.py:166
  8.9 0.4 collective-permute-start.2
  9.4 2.9 %collective-permute-done.3.refs_3_ = bf16[256,256]{1,0:T(8,128)(2,1)S(1)} collective-permute-done((bf16[256,256]{1,0:T(8,128)(2,1)S(1)}, bf16[256,256]{1,0:T(8,128)(2,1)S(1)}, u32[]{:S(2)}, u32[]{:S(2)}) %collective-permute-start.3) | collective-permute-done | bytes 131104 | tf_op jit(solution)/shard_map/ppermute | solution.py:166
  12.3 1.6 %collective-permute-start.4 = (bf16[256,256]{1,0:T(8,128)(2,1)S(1)}, bf16[256,256]{1,0:T(8,128)(2,1)S(1)}, u32[]{:S(2)}, u32[]{:S(2)}) collective-permute-start(bf16[256,256]{1,0:T(8,128)(2,1)S(1)} %collective-permute-done.3.refs_3_), channel_id=1, source_target_pairs={{0,6},{2,4},{4,2},{6,0},{8,14},{10,12},{12,10},{14,8},{1,7},{3,5},... | collective-permute-start | bytes 393224 | tf_op jit(solution)/shard_map/ppermute | solution.py:166
  13.9 0.5 %collective-permute-start.5 = (bf16[256,256]{1,0:T(8,128)(2,1)S(1)}, bf16[256,256]{1,0:T(8,128)(2,1)S(1)}, u32[]{:S(2)}, u32[]{:S(2)}) collective-permute-start(bf16[256,256]{1,0:T(8,128)(2,1)S(1)} %collective-permute-done.3.refs_3_), channel_id=1, source_target_pairs={{0,2},{2,0},{4,6},{6,4},{8,10},{10,8},{12,14},{14,12},{1,3},{3,1},... | collective-permute-start | bytes 393224 | tf_op jit(solution)/shard_map/ppermute | solution.py:166
  14.4 0.0 collective-permute-done.refs_0_
  14.4 1.6 %collective-permute-start.6 = (bf16[256,256]{1,0:T(8,128)(2,1)S(1)}, bf16[256,256]{1,0:T(8,128)(2,1)S(1)}, u32[]{:S(2)}, u32[]{:S(2)}) collective-permute-start(bf16[256,256]{1,0:T(8,128)(2,1)S(1)} %collective-permute-done.3.refs_3_), channel_id=1, source_target_pairs={{0,4},{2,6},{4,0},{6,2},{8,12},{10,14},{12,8},{14,10},{1,5},{3,7},... | collective-permute-start | bytes 393224 | tf_op jit(solution)/shard_map/ppermute | solution.py:166
  16.7 1.5 %dense.1.dense_ref = bf16[512,2048]{1,0:T(8,128)(2,1)S(1)} custom-call(s32[1,1]{1,0:T(1,128)S(6)} %copy.12.count_ref, s32[1,32]{1,0:T(1,128)} %bitcast.4, s32[1,32]{1,0:T(1,128)} %bitcast.5, bf16[32,128,128]{2,1,0:T(8,128)(2,1)} %bitcast.3), custom_call_target="tpu_custom_call" | custom-call | tf_op jit(solution)/shard_map/dense/pallas_call | solution.py:224
  18.2 0.0 collective-permute-done.1.refs_1_
  18.2 0.0 collective-permute-done.2.refs_2_
  18.2 0.5 %early.1.early_ref = f32[512,256]{1,0:T(8,128)S(1)} custom-call(bf16[512,2048]{1,0:T(8,128)(2,1)S(1)} %dense.1.dense_ref, bf16[256,256]{1,0:T(8,128)(2,1)S(1)} %collective-permute-done.refs_0_, bf16[256,256]{1,0:T(8,128)(2,1)S(1)} %collective-permute-done.1.refs_1_, bf16[256,256]{1,0:T(8,128)(2,1)S(1)} %collective-permute-done.2.refs_2_, ...), custom_call_target="tpu_custom_call" | custom-call | flops 335544320 | bytes 3276800 | tf_op jit(solution)/shard_map/early/pallas_call | solution.py:23
  18.7 0.0 copy-start
  18.7 0.0 copy-start.1
  18.7 1.2 %collective-permute-done.4.refs_0_ = bf16[256,256]{1,0:T(8,128)(2,1)S(1)} collective-permute-done((bf16[256,256]{1,0:T(8,128)(2,1)S(1)}, bf16[256,256]{1,0:T(8,128)(2,1)S(1)}, u32[]{:S(2)}, u32[]{:S(2)}) %collective-permute-start.4) | collective-permute-done | bytes 131104 | tf_op jit(solution)/shard_map/ppermute | solution.py:166
  19.9 1.6 %collective-permute-done.5.refs_1_ = bf16[256,256]{1,0:T(8,128)(2,1)S(1)} collective-permute-done((bf16[256,256]{1,0:T(8,128)(2,1)S(1)}, bf16[256,256]{1,0:T(8,128)(2,1)S(1)}, u32[]{:S(2)}, u32[]{:S(2)}) %collective-permute-start.5) | collective-permute-done | bytes 131104 | tf_op jit(solution)/shard_map/ppermute | solution.py:166
  21.5 0.4 collective-permute-done.6.refs_2_
  21.9 0.4 first.1.mine_ref
  22.3 0.1 collective-permute-start.7
  22.3 1.9 %collective-permute-done.7.theirs_ref = f32[512,256]{1,0:T(8,128)S(1)} collective-permute-done((f32[512,256]{1,0:T(8,128)S(1)}, f32[512,256]{1,0:T(8,128)S(1)}, u32[]{:S(2)}, u32[]{:S(2)}) %collective-permute-start.7) | collective-permute-done | bytes 524320 | tf_op jit(solution)/shard_map/ppermute | solution.py:166
  24.2 0.0 copy-done
  24.2 0.0 copy-done.1
  24.2 0.5 %middle.1.refs_4_ = bf16[512,128]{1,0:T(8,128)(2,1)S(1)} custom-call(f32[512,256]{1,0:T(8,128)S(1)} %first.1.mine_ref, f32[512,256]{1,0:T(8,128)S(1)} %collective-permute-done.7.theirs_ref, bf16[128,256]{1,0:T(8,128)(2,1)S(1)} %copy-done, bf16[256,128]{1,0:T(8,128)(2,1)S(1)} %copy-done.1), custom_call_target="tpu_custom_call" | custom-call | flops 167772160 | bytes 1310720 | tf_op jit(solution)/shard_map/middle/pallas_call | solution.py:23
  24.8 2.0 %collective-permute-start.11 = (bf16[512,128]{1,0:T(8,128)(2,1)S(1)}, bf16[512,128]{1,0:T(8,128)(2,1)S(1)}, u32[]{:S(2)}, u32[]{:S(2)}) collective-permute-start(bf16[512,128]{1,0:T(8,128)(2,1)S(1)} %middle.1.refs_4_), channel_id=1, source_target_pairs={{0,8},{2,10},{4,12},{6,14},{8,0},{10,2},{12,4},{14,6},{1,9},{3,11}... | collective-permute-start | bytes 393224 | tf_op jit(solution)/shard_map/ppermute | solution.py:166
  26.8 1.8 %collective-permute-start.10 = (bf16[512,128]{1,0:T(8,128)(2,1)S(1)}, bf16[512,128]{1,0:T(8,128)(2,1)S(1)}, u32[]{:S(2)}, u32[]{:S(2)}) collective-permute-start(bf16[512,128]{1,0:T(8,128)(2,1)S(1)} %middle.1.refs_4_), channel_id=1, source_target_pairs={{0,4},{2,6},{4,0},{6,2},{8,12},{10,14},{12,8},{14,10},{1,5},{3,7},... | collective-permute-start | bytes 393224 | tf_op jit(solution)/shard_map/ppermute | solution.py:166
  28.6 0.2 collective-permute-start.8
  28.8 1.5 %collective-permute-start.9 = (bf16[512,128]{1,0:T(8,128)(2,1)S(1)}, bf16[512,128]{1,0:T(8,128)(2,1)S(1)}, u32[]{:S(2)}, u32[]{:S(2)}) collective-permute-start(bf16[512,128]{1,0:T(8,128)(2,1)S(1)} %middle.1.refs_4_), channel_id=1, source_target_pairs={{0,2},{2,0},{4,6},{6,4},{8,10},{10,8},{12,14},{14,12},{1,3},{3,1},... | collective-permute-start | bytes 393224 | tf_op jit(solution)/shard_map/ppermute | solution.py:166
  30.3 3.9 %collective-permute-done.11.refs_3_ = bf16[512,128]{1,0:T(8,128)(2,1)S(1)} collective-permute-done((bf16[512,128]{1,0:T(8,128)(2,1)S(1)}, bf16[512,128]{1,0:T(8,128)(2,1)S(1)}, u32[]{:S(2)}, u32[]{:S(2)}) %collective-permute-start.11) | collective-permute-done | bytes 131104 | tf_op jit(solution)/shard_map/ppermute | solution.py:166
  34.2 0.0 collective-permute-start.12
  34.2 1.4 %collective-permute-start.13 = (bf16[512,128]{1,0:T(8,128)(2,1)S(1)}, bf16[512,128]{1,0:T(8,128)(2,1)S(1)}, u32[]{:S(2)}, u32[]{:S(2)}) collective-permute-start(bf16[512,128]{1,0:T(8,128)(2,1)S(1)} %collective-permute-done.11.refs_3_), channel_id=1, source_target_pairs={{0,2},{2,0},{4,6},{6,4},{8,10},{10,8},{12,14},{14,12},{1,3},{3,1},... | collective-permute-start | bytes 393224 | tf_op jit(solution)/shard_map/ppermute | solution.py:166
  35.6 0.0 collective-permute-done.10.refs_2_
  35.6 2.1 %collective-permute-start.14 = (bf16[512,128]{1,0:T(8,128)(2,1)S(1)}, bf16[512,128]{1,0:T(8,128)(2,1)S(1)}, u32[]{:S(2)}, u32[]{:S(2)}) collective-permute-start(bf16[512,128]{1,0:T(8,128)(2,1)S(1)} %collective-permute-done.11.refs_3_), channel_id=1, source_target_pairs={{0,4},{2,6},{4,0},{6,2},{8,12},{10,14},{12,8},{14,10},{1,5},{3,7},... | collective-permute-start | bytes 393224 | tf_op jit(solution)/shard_map/ppermute | solution.py:166
  37.7 0.0 collective-permute-done.8.refs_0_
  37.7 0.0 collective-permute-done.9.refs_1_
  37.7 0.5 %early_logits.1.early_ref = f32[768,128]{1,0:T(8,128)S(1)} custom-call(bf16[512,2048]{1,0:T(8,128)(2,1)S(1)} %dense.1.dense_ref, bf16[512,128]{1,0:T(8,128)(2,1)S(1)} %collective-permute-done.8.refs_0_, bf16[512,128]{1,0:T(8,128)(2,1)S(1)} %collective-permute-done.9.refs_1_, bf16[512,128]{1,0:T(8,128)(2,1)S(1)} %collective-permute-done.10.refs_2_, ...), custom_call_target="tpu_custom_call" | custom-call | flops 167772160 | bytes 3145728 | tf_op jit(solution)/shard_map/early_logits/pallas_call | solution.py:23
  38.2 3.2 %collective-permute-done.12.refs_0_ = bf16[512,128]{1,0:T(8,128)(2,1)S(1)} collective-permute-done((bf16[512,128]{1,0:T(8,128)(2,1)S(1)}, bf16[512,128]{1,0:T(8,128)(2,1)S(1)}, u32[]{:S(2)}, u32[]{:S(2)}) %collective-permute-start.12) | collective-permute-done | bytes 131104 | tf_op jit(solution)/shard_map/ppermute | solution.py:166
  41.4 1.2 %collective-permute-done.13.refs_1_ = bf16[512,128]{1,0:T(8,128)(2,1)S(1)} collective-permute-done((bf16[512,128]{1,0:T(8,128)(2,1)S(1)}, bf16[512,128]{1,0:T(8,128)(2,1)S(1)}, u32[]{:S(2)}, u32[]{:S(2)}) %collective-permute-start.13) | collective-permute-done | bytes 131104 | tf_op jit(solution)/shard_map/ppermute | solution.py:166
  42.6 0.2 collective-permute-done.14.refs_2_
  42.8 0.4 second.1
  43.1 0.1 collective-permute-start.15
  43.2 1.5 %collective-permute-done.15.theirs_ref = f32[512,128]{1,0:T(8,128)S(1)} collective-permute-done((f32[512,128]{1,0:T(8,128)S(1)}, f32[512,128]{1,0:T(8,128)S(1)}, u32[]{:S(2)}, u32[]{:S(2)}) %collective-permute-start.15) | collective-permute-done | bytes 262176 | tf_op jit(solution)/shard_map/ppermute | solution.py:166
  44.7 0.8 %last.1 = (bf16[256,128]{1,0:T(8,128)(2,1)}, f32[128,256]{1,0:T(8,128)}, f32[256,128]{1,0:T(8,128)}) custom-call(f32[256,128]{1,0:T(8,128)S(1)} %get-tuple-element.5.keep_ref, f32[512,128]{1,0:T(8,128)S(1)} %get-tuple-element.6.sent_ref, f32[512,128]{1,0:T(8,128)S(1)} %collective-permute-done.15.theirs_ref), custom_call_target="tpu_custom_call" | custom-call | bytes 983040 | tf_op jit(solution)/shard_map/last/pallas_call | solution.py:23
Async XLA Ops:
  1.8 10.5 %collective-permute-start.3 = (bf16[256,256]{1,0:T(8,128)(2,1)S(1)}, bf16[256,256]{1,0:T(8,128)(2,1)S(1)}, u32[]{:S(2)}, u32[]{:S(2)}) collective-permute-start(bf16[256,256]{1,0:T(8,128)(2,1)S(1)} %order.1.refs_4_), channel_id=1, source_target_pairs={{0,8},{2,10},{4,12},{6,14},{8,0},{10,2},{12,4},{14,6},{1,9},{3,11}... | collective-permute-start | bytes 393224 | tf_op jit(solution)/shard_map/ppermute | solution.py:166
  5.9 8.5 %collective-permute-start = (bf16[256,256]{1,0:T(8,128)(2,1)S(1)}, bf16[256,256]{1,0:T(8,128)(2,1)S(1)}, u32[]{:S(2)}, u32[]{:S(2)}) collective-permute-start(bf16[256,256]{1,0:T(8,128)(2,1)S(1)} %order.1.refs_4_), channel_id=1, source_target_pairs={{0,6},{2,4},{4,2},{6,0},{8,14},{10,12},{12,10},{14,8},{1,7},{3,5},... | collective-permute-start | bytes 393224 | tf_op jit(solution)/shard_map/ppermute | solution.py:166
  8.4 9.7 %collective-permute-start.1 = (bf16[256,256]{1,0:T(8,128)(2,1)S(1)}, bf16[256,256]{1,0:T(8,128)(2,1)S(1)}, u32[]{:S(2)}, u32[]{:S(2)}) collective-permute-start(bf16[256,256]{1,0:T(8,128)(2,1)S(1)} %order.1.refs_4_), channel_id=1, source_target_pairs={{0,2},{2,0},{4,6},{6,4},{8,10},{10,8},{12,14},{14,12},{1,3},{3,1},... | collective-permute-start | bytes 393224 | tf_op jit(solution)/shard_map/ppermute | solution.py:166
  8.9 9.3 %collective-permute-start.2 = (bf16[256,256]{1,0:T(8,128)(2,1)S(1)}, bf16[256,256]{1,0:T(8,128)(2,1)S(1)}, u32[]{:S(2)}, u32[]{:S(2)}) collective-permute-start(bf16[256,256]{1,0:T(8,128)(2,1)S(1)} %order.1.refs_4_), channel_id=1, source_target_pairs={{0,4},{2,6},{4,0},{6,2},{8,12},{10,14},{12,8},{14,10},{1,5},{3,7},... | collective-permute-start | bytes 393224 | tf_op jit(solution)/shard_map/ppermute | solution.py:166
  12.3 7.6 %collective-permute-start.4 = (bf16[256,256]{1,0:T(8,128)(2,1)S(1)}, bf16[256,256]{1,0:T(8,128)(2,1)S(1)}, u32[]{:S(2)}, u32[]{:S(2)}) collective-permute-start(bf16[256,256]{1,0:T(8,128)(2,1)S(1)} %collective-permute-done.3.refs_3_), channel_id=1, source_target_pairs={{0,6},{2,4},{4,2},{6,0},{8,14},{10,12},{12,10},{14,8},{1,7},{3,5},... | collective-permute-start | bytes 393224 | tf_op jit(solution)/shard_map/ppermute | solution.py:166
  13.9 7.6 %collective-permute-start.5 = (bf16[256,256]{1,0:T(8,128)(2,1)S(1)}, bf16[256,256]{1,0:T(8,128)(2,1)S(1)}, u32[]{:S(2)}, u32[]{:S(2)}) collective-permute-start(bf16[256,256]{1,0:T(8,128)(2,1)S(1)} %collective-permute-done.3.refs_3_), channel_id=1, source_target_pairs={{0,2},{2,0},{4,6},{6,4},{8,10},{10,8},{12,14},{14,12},{1,3},{3,1},... | collective-permute-start | bytes 393224 | tf_op jit(solution)/shard_map/ppermute | solution.py:166
  14.4 7.4 %collective-permute-start.6 = (bf16[256,256]{1,0:T(8,128)(2,1)S(1)}, bf16[256,256]{1,0:T(8,128)(2,1)S(1)}, u32[]{:S(2)}, u32[]{:S(2)}) collective-permute-start(bf16[256,256]{1,0:T(8,128)(2,1)S(1)} %collective-permute-done.3.refs_3_), channel_id=1, source_target_pairs={{0,4},{2,6},{4,0},{6,2},{8,12},{10,14},{12,8},{14,10},{1,5},{3,7},... | collective-permute-start | bytes 393224 | tf_op jit(solution)/shard_map/ppermute | solution.py:166
  18.7 5.5 %copy-start = (bf16[128,256]{1,0:T(8,128)(2,1)S(1)}, bf16[128,256]{1,0:T(8,128)(2,1)}, u32[]{:S(2)}) copy-start(bf16[128,256]{1,0:T(8,128)(2,1)} %first_ref.1) | copy-start | bytes 196612
  18.7 5.5 %copy-start.1 = (bf16[256,128]{1,0:T(8,128)(2,1)S(1)}, bf16[256,128]{1,0:T(8,128)(2,1)}, u32[]{:S(2)}) copy-start(bf16[256,128]{1,0:T(8,128)(2,1)} %second_ref.1) | copy-start | bytes 196612
  22.3 2.0 %collective-permute-start.7 = (f32[512,256]{1,0:T(8,128)S(1)}, f32[512,256]{1,0:T(8,128)S(1)}, u32[]{:S(2)}, u32[]{:S(2)}) collective-permute-start(f32[512,256]{1,0:T(8,128)S(1)} %first.1.mine_ref), channel_id=1, source_target_pairs={{0,1},{1,0},{2,3},{3,2},{4,5},{5,4},{6,7},{7,6},{8,9},{9,8},{10,11... | collective-permute-start | bytes 1572872 | tf_op jit(solution)/shard_map/ppermute | solution.py:166
  24.8 9.4 %collective-permute-start.11 = (bf16[512,128]{1,0:T(8,128)(2,1)S(1)}, bf16[512,128]{1,0:T(8,128)(2,1)S(1)}, u32[]{:S(2)}, u32[]{:S(2)}) collective-permute-start(bf16[512,128]{1,0:T(8,128)(2,1)S(1)} %middle.1.refs_4_), channel_id=1, source_target_pairs={{0,8},{2,10},{4,12},{6,14},{8,0},{10,2},{12,4},{14,6},{1,9},{3,11}... | collective-permute-start | bytes 393224 | tf_op jit(solution)/shard_map/ppermute | solution.py:166
  26.8 8.8 %collective-permute-start.10 = (bf16[512,128]{1,0:T(8,128)(2,1)S(1)}, bf16[512,128]{1,0:T(8,128)(2,1)S(1)}, u32[]{:S(2)}, u32[]{:S(2)}) collective-permute-start(bf16[512,128]{1,0:T(8,128)(2,1)S(1)} %middle.1.refs_4_), channel_id=1, source_target_pairs={{0,4},{2,6},{4,0},{6,2},{8,12},{10,14},{12,8},{14,10},{1,5},{3,7},... | collective-permute-start | bytes 393224 | tf_op jit(solution)/shard_map/ppermute | solution.py:166
  28.6 9.1 %collective-permute-start.8 = (bf16[512,128]{1,0:T(8,128)(2,1)S(1)}, bf16[512,128]{1,0:T(8,128)(2,1)S(1)}, u32[]{:S(2)}, u32[]{:S(2)}) collective-permute-start(bf16[512,128]{1,0:T(8,128)(2,1)S(1)} %middle.1.refs_4_), channel_id=1, source_target_pairs={{0,6},{2,4},{4,2},{6,0},{8,14},{10,12},{12,10},{14,8},{1,7},{3,5},... | collective-permute-start | bytes 393224 | tf_op jit(solution)/shard_map/ppermute | solution.py:166
  28.8 8.9 %collective-permute-start.9 = (bf16[512,128]{1,0:T(8,128)(2,1)S(1)}, bf16[512,128]{1,0:T(8,128)(2,1)S(1)}, u32[]{:S(2)}, u32[]{:S(2)}) collective-permute-start(bf16[512,128]{1,0:T(8,128)(2,1)S(1)} %middle.1.refs_4_), channel_id=1, source_target_pairs={{0,2},{2,0},{4,6},{6,4},{8,10},{10,8},{12,14},{14,12},{1,3},{3,1},... | collective-permute-start | bytes 393224 | tf_op jit(solution)/shard_map/ppermute | solution.py:166
  34.2 7.2 %collective-permute-start.12 = (bf16[512,128]{1,0:T(8,128)(2,1)S(1)}, bf16[512,128]{1,0:T(8,128)(2,1)S(1)}, u32[]{:S(2)}, u32[]{:S(2)}) collective-permute-start(bf16[512,128]{1,0:T(8,128)(2,1)S(1)} %collective-permute-done.11.refs_3_), channel_id=1, source_target_pairs={{0,6},{2,4},{4,2},{6,0},{8,14},{10,12},{12,10},{14,8},{1,7},{3,5},... | collective-permute-start | bytes 393224 | tf_op jit(solution)/shard_map/ppermute | solution.py:166
  34.2 8.4 %collective-permute-start.13 = (bf16[512,128]{1,0:T(8,128)(2,1)S(1)}, bf16[512,128]{1,0:T(8,128)(2,1)S(1)}, u32[]{:S(2)}, u32[]{:S(2)}) collective-permute-start(bf16[512,128]{1,0:T(8,128)(2,1)S(1)} %collective-permute-done.11.refs_3_), channel_id=1, source_target_pairs={{0,2},{2,0},{4,6},{6,4},{8,10},{10,8},{12,14},{14,12},{1,3},{3,1},... | collective-permute-start | bytes 393224 | tf_op jit(solution)/shard_map/ppermute | solution.py:166
  35.6 7.1 %collective-permute-start.14 = (bf16[512,128]{1,0:T(8,128)(2,1)S(1)}, bf16[512,128]{1,0:T(8,128)(2,1)S(1)}, u32[]{:S(2)}, u32[]{:S(2)}) collective-permute-start(bf16[512,128]{1,0:T(8,128)(2,1)S(1)} %collective-permute-done.11.refs_3_), channel_id=1, source_target_pairs={{0,4},{2,6},{4,0},{6,2},{8,12},{10,14},{12,8},{14,10},{1,5},{3,7},... | collective-permute-start | bytes 393224 | tf_op jit(solution)/shard_map/ppermute | solution.py:166
  43.1 1.6 %collective-permute-start.15 = (f32[512,128]{1,0:T(8,128)S(1)}, f32[512,128]{1,0:T(8,128)S(1)}, u32[]{:S(2)}, u32[]{:S(2)}) collective-permute-start(f32[512,128]{1,0:T(8,128)S(1)} %get-tuple-element.6.sent_ref), channel_id=1, source_target_pairs={{0,1},{1,0},{2,3},{3,2},{4,5},{5,4},{6,7},{7,6},{8,9},{9,8},{10,11... | collective-permute-start | bytes 786440 | tf_op jit(solution)/shard_map/ppermute | solution.py:166

commit v5 on v4

--- a/solution.py
+++ b/solution.py
@@ -94,10 +94,10 @@
         out_ref[at, :] = total + early_ref[at, :]
 
 
-def middle_kernel(mine_ref, theirs_ref, first_ref, second_ref, out_ref):
+def middle_kernel(mine_ref, theirs_ref, first_ref, second_ref, projected_ref, out_ref):
     feat = first_ref.shape[0]
     half = first_ref.shape[1] // 2
-    nodes = out_ref.shape[0] // 2
+    nodes = projected_ref.shape[0]
     col = lax.axis_index("col")
     hid_at = pl.ds(pl.multiple_of(col * half, half), half)
     summed = mine_ref[...] + theirs_ref[...]
@@ -110,7 +110,9 @@
     own = mine_ref[at, :feat] + theirs_ref[at, :feat]
     own_pre = dot(own.astype(jnp.bfloat16), first_ref[...])
     own_hidden = (own_pre * jax.nn.sigmoid(own_pre)).astype(jnp.bfloat16)
-    out_ref[:nodes, :] = dot(own_hidden, second_ref[...]).astype(jnp.bfloat16)
+    projected = dot(own_hidden, second_ref[...]).astype(jnp.bfloat16)
+    projected_ref[...] = projected
+    out_ref[:nodes, :] = projected
 
     pre = dot(aggregated, first_half)
     gate = jax.nn.sigmoid(pre)
@@ -123,42 +125,50 @@
 
 def early_logits_kernel(masks, dense_ref, *refs):
     *pieces, out_ref = refs
-    slab = dense_ref.shape[0]
-    nodes = slab // 2
-    tops = [piece.at[:nodes, :] for piece in pieces]
-    for start, total in products(dense_ref, masks, tops, 128):
-        out_ref[start : start + 128, :] = total
-    grads = pieces[0][nodes:, :].astype(jnp.float32)
-    for piece in pieces[1:]:
-        grads = grads + piece[nodes:, :].astype(jnp.float32)
-    out_ref[slab:, :] = grads
+    nodes = out_ref.shape[0] // 2
+    early_kernel(masks, dense_ref, *(piece.at[:nodes, :] for piece in pieces), out_ref)
+
+
+def more_logits_kernel(masks, dense_ref, early_ref, *refs):
+    *pieces, out_ref = refs
+    nodes = out_ref.shape[0] // 2
+    tops = (piece.at[:nodes, :] for piece in pieces)
+    first_kernel(masks, dense_ref, early_ref, *tops, out_ref)
+
+
+def sum_kernel(*refs):
+    *parts, out_ref = refs
+    at = slice(parts[0].shape[0] - out_ref.shape[0], None)
+    total = parts[0][at, :].astype(jnp.float32)
+    for part in parts[1:]:
+        total = total + part[at, :].astype(jnp.float32)
+    out_ref[...] = total.astype(jnp.bfloat16)
 
 
 def second_kernel(masks, dense_ref, early_ref, *refs):
     *pieces, keep_ref, send_ref = refs
     nodes = keep_ref.shape[0]
     col = lax.axis_index("col")
-    tops = [piece.at[:nodes, :] for piece in pieces]
     for where, ref in ((col, keep_ref), (1 - col, send_ref)):
         at = pl.ds(pl.multiple_of(where * nodes, nodes), nodes)
         early = early_ref.at[at, :]
-        for start, total in products(dense_ref.at[at, :], masks, tops, 128):
+        for start, total in products(dense_ref.at[at, :], masks, pieces, 128):
             ref[start : start + 128, :] = total + early[start : start + 128, :]
-    grads = early_ref[2 * nodes :, :]
-    for piece in pieces:
-        grads = grads + piece[nodes:, :].astype(jnp.float32)
-    send_ref[nodes:, :] = grads
-
-
-def last_kernel(scale, keep_ref, sent_ref, theirs_ref, logits_ref, first_ref, second_ref):
-    nodes = keep_ref.shape[0]
+
+
+def last_kernel(scale, keep_ref, their_logits_ref, *refs):
+    *parts, logits_ref, first_ref, second_ref = refs
+    logits_ref[...] = (keep_ref[...] + their_logits_ref[...]).astype(jnp.bfloat16)
     half = second_ref.shape[0] // 2
     col = lax.axis_index("col")
-    logits_ref[...] = (keep_ref[...] + theirs_ref[:nodes, :]).astype(jnp.bfloat16)
-    for where, ref in ((col, sent_ref), (1 - col, theirs_ref)):
+    count = len(parts) // 2
+    for where, some in ((col, parts[:count]), (1 - col, parts[count:])):
+        total = some[0][...].astype(jnp.float32)
+        for part in some[1:]:
+            total = total + part[...].astype(jnp.float32)
         at = pl.ds(pl.multiple_of(where * half, half), half)
-        second_ref[at, :] = ref[nodes : nodes + half, :] * scale
-        first_ref[:, at] = ref[nodes + half :, :] * scale
+        second_ref[at, :] = total[:half, :] * scale
+        first_ref[:, at] = total[half:, :] * scale
 
 
 def exchange(x, axis, mask):
@@ -166,23 +176,29 @@
     return lax.ppermute(x, axis, [(i, i ^ mask) for i in range(size)])
 
 
-def gather_rows(x):
+def near_size():
+    return min(4, lax.axis_size("row"))
+
+
+def from_far(x):
     size = lax.axis_size("row")
-    near = min(4, size)
-    found = {0: x}
-    for mask in [*range(near, size, near), *range(1, near)]:
-        found[mask] = exchange(x, "row", mask)
-    for mask in range(near, size, near):
-        for low in range(1, near):
-            found[mask + low] = exchange(found[mask], "row", low)
+    return {mask: exchange(x, "row", mask) for mask in range(near_size(), size, near_size())}
+
+
+def from_near(x, far):
+    found = {low: exchange(x, "row", low) for low in range(1, near_size())}
+    for mask, block in far.items():
+        for low in range(1, near_size()):
+            found[mask + low] = exchange(block, "row", low)
     return found
 
 
-def arrival(rows):
-    near = min(4, rows)
-    far = [*range(near, rows, near)]
-    order = [low for low in (3, 1, 2) if low < near]
-    return [*order, *far, 0], [mask + low for mask in far for low in order]
+def arrival(near_order, last_order):
+    size, near = lax.axis_size("row"), near_size()
+    far = [*range(near, size, near)]
+    first = [low for low in near_order if low < near]
+    last = [mask + low for mask in far for low in last_order if low < near]
+    return first, [*far, 0], last
 
 
 def shards(
@@ -233,45 +249,58 @@
             pltpu.SemaphoreType.DMA((3,)),
         ],
         name="dense",
+        cost_estimate=pl.CostEstimate(flops=1 * 10**6, bytes_accessed=4 * tiles.size, transcendentals=0),
         compiler_params=pltpu.CompilerParams(
             vmem_limit_bytes=4 * tiles.size + 4 * slab * set_nodes + (8 << 20)
         ),
     )(tile_counts, in_hbm(tile_rows[0]), in_hbm(tile_cols[0]), in_hbm(tiles))
 
-    early, late = arrival(rows)
+    near, direct, late = arrival((3, 1, 2), (3, 1, 2))
+    early = near + direct
     flops = 2 * slab * nodes * (feat + classes)
-    found = gather_rows(source)
+    far = from_far(source)
+    found = {0: source} | far | from_near(source, far)
     partial = call(
         functools.partial(early_kernel, early), shape((slab, feat + classes), f32),
-        [VMEM] * (1 + len(early)), flops * len(early), "early", dense, *(found[k] for k in early),
+        [VMEM] * (1 + len(early)), 1 * 10**6, "early", dense, *(found[k] for k in early),
     )
     mine = call(
         functools.partial(first_kernel, late), shape((slab, feat + classes), f32),
-        [VMEM] * (2 + len(late)), flops * len(late), "first",
+        [VMEM] * (2 + len(late)), 40000 * 10**6, "first",
         dense, partial, *(found[k] for k in late),
     )
-    middle = call(
-        middle_kernel, shape((nodes + hid, classes), bf16), [VMEM] * 4, 10 * slab * feat * hid,
+    projected, both = call(
+        middle_kernel, (shape((nodes, classes), bf16), shape((nodes + hid, classes), bf16)),
+        [VMEM] * 4, 10 * slab * feat * hid,
         "middle", mine, exchange(mine, "col", 1), weight_first, weight_second,
     )
     flops = 2 * slab * nodes * classes
-    found = gather_rows(middle)
+    far = from_far(projected)
+    found = {0: both} | far | from_near(both, far)
+    near, direct, late = arrival((2, 3, 1), (2, 3, 1))
     partial = call(
-        functools.partial(early_logits_kernel, early), shape((slab + hid, classes), f32),
-        [VMEM] * (1 + len(early)), flops * len(early), "early_logits",
-        dense, *(found[k] for k in early),
+        functools.partial(early_logits_kernel, direct), shape((slab, classes), f32),
+        [VMEM] * (1 + len(direct)), 15000 * 10**6, "early_logits", dense, *(found[k] for k in direct),
+    )
+    partial = call(
+        functools.partial(more_logits_kernel, near), shape((slab, classes), f32),
+        [VMEM] * (2 + len(near)), 1 * 10**6, "more_logits", dense, partial, *(found[k] for k in near),
     )
     keep, send = call(
-        functools.partial(second_kernel, late),
-        (shape((nodes, classes), f32), shape((nodes + hid, classes), f32)),
-        [VMEM] * (2 + len(late)), flops * len(late), "second",
+        functools.partial(second_kernel, late), (shape((nodes, classes), f32),) * 2,
+        [VMEM] * (2 + len(late)), 1 * 10**6, "second",
         dense, partial, *(found[k] for k in late),
     )
-    theirs = exchange(send, "col", 1)
+    parts = [found[low] for low in range(near_size())]
+    total = call(
+        sum_kernel, shape((hid, classes), bf16), [VMEM] * len(parts), 0, "sum", *parts
+    )
+    sums = [total, *from_far(total).values()]
     return call(
         functools.partial(last_kernel, 1.0 / math.sqrt(set_nodes * cols)),
         (shape((nodes, classes), bf16), shape((feat, hid), f32), shape((hid, classes), f32)),
-        [VMEM] * 3, 0, "last", keep, send, theirs,
+        [VMEM] * (2 + 2 * len(sums)), 0, "last",
+        keep, exchange(send, "col", 1), *sums, *(exchange(x, "col", 1) for x in sums),
     )
 
 

time: 45.7 us -> 43.8 us (0.958)
  waiting for transfers between devices: 18 us -> 12.1 us
  starting transfers between devices: 20.4 us -> 24.1 us
    ppermute x16 -> x19, waiting for transfers between devices: 18 us -> 12.1 us  [exchange(): return lax.ppermute(x, axis, [(i, i ^ mask) for i in range(size)])]
    ppermute x16 -> x19, starting transfers between devices: 20.4 us -> 24.1 us  [exchange(): return lax.ppermute(x, axis, [(i, i ^ mask) for i in range(size)])]
    pallas_call x6 -> x8, Pallas kernels: 3.04 us -> 3.22 us  [call(): pl.pallas_call(kernel, out_shape=out_shape, in_specs=in_specs, out_specs=...]
  transfers between devices with their start and end apart: 16 -> 19, of which waited for: 10 -> 11; matrix products, arithmetic and copies ran while one was open for 0% -> 0% of each run, Pallas kernels for 5% -> 7%
where the time goes in v5:
time: 43.8 us; the launch traced here: 43.6 us
  starting transfers between devices  24.1 us (55%)
  waiting for transfers between devices  12.1 us (28%)
  Pallas kernels  6.04 us (14%)
  between operations  1.43 us (3%)
    ppermute x19, starting transfers between devices, exchange(): return lax.ppermute(x, axis, [(i, i ^ mask) for i in range(size)])  24.1 us
    ppermute x19, waiting for transfers between devices, exchange(): return lax.ppermute(x, axis, [(i, i ^ mask) for i in range(size)])  12.1 us
    pallas_call x8, Pallas kernels, call(): pl.pallas_call(kernel, out_shape=out_shape, in_specs=in_specs, out_specs=...  3.22 us
    pallas_call x1, Pallas kernels, shards(): pl.pallas_call(functools.partial(dense_kernel, nodes // size), out_shape=...  1.67 us
    pallas_call x1, Pallas kernels, shards(): pl.pallas_call(order_kernel, out_shape=shape((nodes, feat + classes), bf1...  1.15 us
  transfers between devices with their start and end apart: 19, of which 11 were waited for; matrix products, arithmetic and copies ran while one was open for 0% of the time, Pallas kernels for 7%

profile of v5, /device:TPU:0, one launch (start us, length us, event | category | flops | bytes accessed | tf_op | source)
XLA Modules:
  0.0 43.6 jit_solution(7145875531655102366)
XLA Ops:
  0.6 1.1 %order.1.refs_4_ = bf16[256,256]{1,0:T(8,128)(2,1)S(1)} custom-call(s32[1,256]{1,0:T(1,128)} %order_hbm.1, bf16[256,128]{1,0:T(8,128)(2,1)} %features_hbm.1, bf16[256,128]{1,0:T(8,128)(2,1)} %grads_hbm.1), custom_call_target="tpu_custom_call" | custom-call | tf_op jit(solution)/shard_map/order/pallas_call | solution.py:227
  1.8 4.1 %collective-permute-start.3 = (bf16[256,256]{1,0:T(8,128)(2,1)S(1)}, bf16[256,256]{1,0:T(8,128)(2,1)S(1)}, u32[]{:S(2)}, u32[]{:S(2)}) collective-permute-start(bf16[256,256]{1,0:T(8,128)(2,1)S(1)} %order.1.refs_4_), channel_id=1, source_target_pairs={{0,8},{2,10},{4,12},{6,14},{8,0},{10,2},{12,4},{14,6},{1,9},{3,11}... | collective-permute-start | bytes 393224 | tf_op jit(solution)/shard_map/ppermute | solution.py:176
  5.9 2.5 %collective-permute-start = (bf16[256,256]{1,0:T(8,128)(2,1)S(1)}, bf16[256,256]{1,0:T(8,128)(2,1)S(1)}, u32[]{:S(2)}, u32[]{:S(2)}) collective-permute-start(bf16[256,256]{1,0:T(8,128)(2,1)S(1)} %order.1.refs_4_), channel_id=1, source_target_pairs={{0,6},{2,4},{4,2},{6,0},{8,14},{10,12},{12,10},{14,8},{1,7},{3,5},... | collective-permute-start | bytes 393224 | tf_op jit(solution)/shard_map/ppermute | solution.py:176
  8.4 0.5 %collective-permute-start.1 = (bf16[256,256]{1,0:T(8,128)(2,1)S(1)}, bf16[256,256]{1,0:T(8,128)(2,1)S(1)}, u32[]{:S(2)}, u32[]{:S(2)}) collective-permute-start(bf16[256,256]{1,0:T(8,128)(2,1)S(1)} %order.1.refs_4_), channel_id=1, source_target_pairs={{0,2},{2,0},{4,6},{6,4},{8,10},{10,8},{12,14},{14,12},{1,3},{3,1},... | collective-permute-start | bytes 393224 | tf_op jit(solution)/shard_map/ppermute | solution.py:176
  8.9 0.4 %collective-permute-start.2 = (bf16[256,256]{1,0:T(8,128)(2,1)S(1)}, bf16[256,256]{1,0:T(8,128)(2,1)S(1)}, u32[]{:S(2)}, u32[]{:S(2)}) collective-permute-start(bf16[256,256]{1,0:T(8,128)(2,1)S(1)} %order.1.refs_4_), channel_id=1, source_target_pairs={{0,4},{2,6},{4,0},{6,2},{8,12},{10,14},{12,8},{14,10},{1,5},{3,7},... | collective-permute-start | bytes 393224 | tf_op jit(solution)/shard_map/ppermute | solution.py:176
  9.4 2.9 %collective-permute-done.3.refs_3_ = bf16[256,256]{1,0:T(8,128)(2,1)S(1)} collective-permute-done((bf16[256,256]{1,0:T(8,128)(2,1)S(1)}, bf16[256,256]{1,0:T(8,128)(2,1)S(1)}, u32[]{:S(2)}, u32[]{:S(2)}) %collective-permute-start.3) | collective-permute-done | bytes 131104 | tf_op jit(solution)/shard_map/ppermute | solution.py:176
  12.3 1.6 %collective-permute-start.4 = (bf16[256,256]{1,0:T(8,128)(2,1)S(1)}, bf16[256,256]{1,0:T(8,128)(2,1)S(1)}, u32[]{:S(2)}, u32[]{:S(2)}) collective-permute-start(bf16[256,256]{1,0:T(8,128)(2,1)S(1)} %collective-permute-done.3.refs_3_), channel_id=1, source_target_pairs={{0,6},{2,4},{4,2},{6,0},{8,14},{10,12},{12,10},{14,8},{1,7},{3,5},... | collective-permute-start | bytes 393224 | tf_op jit(solution)/shard_map/ppermute | solution.py:176
  13.9 0.5 %collective-permute-start.5 = (bf16[256,256]{1,0:T(8,128)(2,1)S(1)}, bf16[256,256]{1,0:T(8,128)(2,1)S(1)}, u32[]{:S(2)}, u32[]{:S(2)}) collective-permute-start(bf16[256,256]{1,0:T(8,128)(2,1)S(1)} %collective-permute-done.3.refs_3_), channel_id=1, source_target_pairs={{0,2},{2,0},{4,6},{6,4},{8,10},{10,8},{12,14},{14,12},{1,3},{3,1},... | collective-permute-start | bytes 393224 | tf_op jit(solution)/shard_map/ppermute | solution.py:176
  14.4 0.0 collective-permute-done.refs_0_
  14.4 1.6 %collective-permute-start.6 = (bf16[256,256]{1,0:T(8,128)(2,1)S(1)}, bf16[256,256]{1,0:T(8,128)(2,1)S(1)}, u32[]{:S(2)}, u32[]{:S(2)}) collective-permute-start(bf16[256,256]{1,0:T(8,128)(2,1)S(1)} %collective-permute-done.3.refs_3_), channel_id=1, source_target_pairs={{0,4},{2,6},{4,0},{6,2},{8,12},{10,14},{12,8},{14,10},{1,5},{3,7},... | collective-permute-start | bytes 393224 | tf_op jit(solution)/shard_map/ppermute | solution.py:176
  16.7 1.7 %dense.1.dense_ref = bf16[512,2048]{1,0:T(8,128)(2,1)S(1)} custom-call(s32[1,1]{1,0:T(1,128)S(6)} %copy.12.count_ref, s32[1,32]{1,0:T(1,128)} %bitcast.4, s32[1,32]{1,0:T(1,128)} %bitcast.5, bf16[32,128,128]{2,1,0:T(8,128)(2,1)} %bitcast.3), custom_call_target="tpu_custom_call" | custom-call | flops 1000000 | bytes 2097152 | tf_op jit(solution)/shard_map/dense/pallas_call | solution.py:240
  18.4 0.0 collective-permute-done.1.refs_1_
  18.4 0.0 collective-permute-done.2.refs_2_
  18.4 0.5 %early.1.early_ref = f32[512,256]{1,0:T(8,128)S(1)} custom-call(bf16[512,2048]{1,0:T(8,128)(2,1)S(1)} %dense.1.dense_ref, bf16[256,256]{1,0:T(8,128)(2,1)S(1)} %collective-permute-done.refs_0_, bf16[256,256]{1,0:T(8,128)(2,1)S(1)} %collective-permute-done.1.refs_1_, bf16[256,256]{1,0:T(8,128)(2,1)S(1)} %collective-permute-done.2.refs_2_, ...), custom_call_target="tpu_custom_call" | custom-call | flops 1000000 | bytes 3276800 | tf_op jit(solution)/shard_map/early/pallas_call | solution.py:23
  18.9 0.0 copy-start
  18.9 0.0 copy-start.1
  18.9 0.9 %collective-permute-done.4.refs_0_ = bf16[256,256]{1,0:T(8,128)(2,1)S(1)} collective-permute-done((bf16[256,256]{1,0:T(8,128)(2,1)S(1)}, bf16[256,256]{1,0:T(8,128)(2,1)S(1)}, u32[]{:S(2)}, u32[]{:S(2)}) %collective-permute-start.4) | collective-permute-done | bytes 131104 | tf_op jit(solution)/shard_map/ppermute | solution.py:176
  19.9 1.6 %collective-permute-done.5.refs_1_ = bf16[256,256]{1,0:T(8,128)(2,1)S(1)} collective-permute-done((bf16[256,256]{1,0:T(8,128)(2,1)S(1)}, bf16[256,256]{1,0:T(8,128)(2,1)S(1)}, u32[]{:S(2)}, u32[]{:S(2)}) %collective-permute-start.5) | collective-permute-done | bytes 131104 | tf_op jit(solution)/shard_map/ppermute | solution.py:176
  21.5 0.4 collective-permute-done.6.refs_2_
  21.9 0.4 first.1.mine_ref
  22.3 0.1 collective-permute-start.7
  22.3 1.9 %collective-permute-done.7.theirs_ref = f32[512,256]{1,0:T(8,128)S(1)} collective-permute-done((f32[512,256]{1,0:T(8,128)S(1)}, f32[512,256]{1,0:T(8,128)S(1)}, u32[]{:S(2)}, u32[]{:S(2)}) %collective-permute-start.7) | collective-permute-done | bytes 524320 | tf_op jit(solution)/shard_map/ppermute | solution.py:176
  24.2 0.0 copy-done
  24.2 0.0 copy-done.1
  24.2 0.5 %middle.1 = (bf16[256,128]{1,0:T(8,128)(2,1)S(1)}, bf16[512,128]{1,0:T(8,128)(2,1)S(1)}) custom-call(f32[512,256]{1,0:T(8,128)S(1)} %first.1.mine_ref, f32[512,256]{1,0:T(8,128)S(1)} %collective-permute-done.7.theirs_ref, bf16[128,256]{1,0:T(8,128)(2,1)S(1)} %copy-done, bf16[256,128]{1,0:T(8,128)(2,1)S(1)} %copy-done.1), custom_call_target="tpu_custom_call" | custom-call | flops 167772160 | bytes 1376256 | tf_op jit(solution)/shard_map/middle/pallas_call | solution.py:23
  24.8 1.5 %collective-permute-start.10 = (bf16[512,128]{1,0:T(8,128)(2,1)S(1)}, bf16[512,128]{1,0:T(8,128)(2,1)S(1)}, u32[]{:S(2)}, u32[]{:S(2)}) collective-permute-start(bf16[512,128]{1,0:T(8,128)(2,1)S(1)} %get-tuple-element.8.refs_1_.refs_0_), channel_id=1, source_target_pairs={{0,6},{2,4},{4,2},{6,0},{8,14},{10,12},{12,10},{14,8},{1,7},{3,5},... | collective-permute-start | bytes 393224 | tf_op jit(solution)/shard_map/ppermute | solution.py:176
  26.3 2.2 %collective-permute-start.8 = (bf16[256,128]{1,0:T(8,128)(2,1)S(1)}, bf16[256,128]{1,0:T(8,128)(2,1)S(1)}, u32[]{:S(2)}, u32[]{:S(2)}) collective-permute-start(bf16[256,128]{1,0:T(8,128)(2,1)S(1)} %get-tuple-element.7), channel_id=1, source_target_pairs={{0,8},{2,10},{4,12},{6,14},{8,0},{10,2},{12,4},{14,6},{1,9},{3,11}... | collective-permute-start | bytes 196616 | tf_op jit(solution)/shard_map/ppermute | solution.py:176
  28.5 1.5 %collective-permute-start.11 = (bf16[512,128]{1,0:T(8,128)(2,1)S(1)}, bf16[512,128]{1,0:T(8,128)(2,1)S(1)}, u32[]{:S(2)}, u32[]{:S(2)}) collective-permute-start(bf16[512,128]{1,0:T(8,128)(2,1)S(1)} %get-tuple-element.8.refs_1_.refs_0_), channel_id=1, source_target_pairs={{0,2},{2,0},{4,6},{6,4},{8,10},{10,8},{12,14},{14,12},{1,3},{3,1},... | collective-permute-start | bytes 393224 | tf_op jit(solution)/shard_map/ppermute | solution.py:176
  30.0 0.2 collective-permute-start.9
  30.3 1.6 %collective-permute-done.8.refs_0_ = bf16[256,128]{1,0:T(8,128)(2,1)S(1)} collective-permute-done((bf16[256,128]{1,0:T(8,128)(2,1)S(1)}, bf16[256,128]{1,0:T(8,128)(2,1)S(1)}, u32[]{:S(2)}, u32[]{:S(2)}) %collective-permute-start.8) | collective-permute-done | bytes 65568 | tf_op jit(solution)/shard_map/ppermute | solution.py:176
  31.9 2.6 %collective-permute-start.12 = (bf16[256,128]{1,0:T(8,128)(2,1)S(1)}, bf16[256,128]{1,0:T(8,128)(2,1)S(1)}, u32[]{:S(2)}, u32[]{:S(2)}) collective-permute-start(bf16[256,128]{1,0:T(8,128)(2,1)S(1)} %collective-permute-done.8.refs_0_), channel_id=1, source_target_pairs={{0,4},{2,6},{4,0},{6,2},{8,12},{10,14},{12,8},{14,10},{1,5},{3,7},... | collective-permute-start | bytes 196616 | tf_op jit(solution)/shard_map/ppermute | solution.py:176
  34.5 0.9 %collective-permute-start.13 = (bf16[256,128]{1,0:T(8,128)(2,1)S(1)}, bf16[256,128]{1,0:T(8,128)(2,1)S(1)}, u32[]{:S(2)}, u32[]{:S(2)}) collective-permute-start(bf16[256,128]{1,0:T(8,128)(2,1)S(1)} %collective-permute-done.8.refs_0_), channel_id=1, source_target_pairs={{0,6},{2,4},{4,2},{6,0},{8,14},{10,12},{12,10},{14,8},{1,7},{3,5},... | collective-permute-start | bytes 196616 | tf_op jit(solution)/shard_map/ppermute | solution.py:176
  35.4 0.0 collective-permute-done.10.refs_1_.refs_3_
  35.4 0.6 %collective-permute-start.14 = (bf16[256,128]{1,0:T(8,128)(2,1)S(1)}, bf16[256,128]{1,0:T(8,128)(2,1)S(1)}, u32[]{:S(2)}, u32[]{:S(2)}) collective-permute-start(bf16[256,128]{1,0:T(8,128)(2,1)S(1)} %collective-permute-done.8.refs_0_), channel_id=1, source_target_pairs={{0,2},{2,0},{4,6},{6,4},{8,10},{10,8},{12,14},{14,12},{1,3},{3,1},... | collective-permute-start | bytes 196616 | tf_op jit(solution)/shard_map/ppermute | solution.py:176
  36.0 0.3 early_logits.1.early_ref
  36.3 0.0 collective-permute-done.11.refs_2_.refs_1_
  36.3 0.0 collective-permute-done.9.refs_0_.refs_2_
  36.3 2.5 %collective-permute-start.16 = (bf16[256,128]{1,0:T(8,128)(2,1)S(1)}, bf16[256,128]{1,0:T(8,128)(2,1)S(1)}, u32[]{:S(2)}, u32[]{:S(2)}) collective-permute-start(bf16[256,128]{1,0:T(8,128)(2,1)S(1)} %sum.1.refs_0_), channel_id=1, source_target_pairs={{0,8},{2,10},{4,12},{6,14},{8,0},{10,2},{12,4},{14,6},{1,9},{3,11}... | collective-permute-start | bytes 196616 | tf_op jit(solution)/shard_map/ppermute | solution.py:176
  38.9 0.4 more_logits.1.early_ref
  39.2 0.0 collective-permute-done.12.refs_0_
  39.2 0.8 %collective-permute-done.13.refs_1_ = bf16[256,128]{1,0:T(8,128)(2,1)S(1)} collective-permute-done((bf16[256,128]{1,0:T(8,128)(2,1)S(1)}, bf16[256,128]{1,0:T(8,128)(2,1)S(1)}, u32[]{:S(2)}, u32[]{:S(2)}) %collective-permute-start.13) | collective-permute-done | bytes 65568 | tf_op jit(solution)/shard_map/ppermute | solution.py:176
  40.0 0.4 collective-permute-done.14.refs_2_
  40.4 0.4 second.1
  40.8 0.1 collective-permute-start.15
  40.8 0.5 %collective-permute-start.17 = (bf16[256,128]{1,0:T(8,128)(2,1)S(1)}, bf16[256,128]{1,0:T(8,128)(2,1)S(1)}, u32[]{:S(2)}, u32[]{:S(2)}) collective-permute-start(bf16[256,128]{1,0:T(8,128)(2,1)S(1)} %sum.1.refs_0_), channel_id=1, source_target_pairs={{0,1},{1,0},{2,3},{3,2},{4,5},{5,4},{6,7},{7,6},{8,9},{9,8},{10,11... | collective-permute-start | bytes 196616 | tf_op jit(solution)/shard_map/ppermute | solution.py:176
  41.3 0.2 collective-permute-done.16.refs_1_
  41.6 0.0 collective-permute-start.18
  41.6 0.7 %collective-permute-done.17.refs_2_ = bf16[256,128]{1,0:T(8,128)(2,1)S(1)} collective-permute-done((bf16[256,128]{1,0:T(8,128)(2,1)S(1)}, bf16[256,128]{1,0:T(8,128)(2,1)S(1)}, u32[]{:S(2)}, u32[]{:S(2)}) %collective-permute-start.17) | collective-permute-done | bytes 65568 | tf_op jit(solution)/shard_map/ppermute | solution.py:176
  42.3 0.6 %collective-permute-done.18.refs_3_ = bf16[256,128]{1,0:T(8,128)(2,1)S(1)} collective-permute-done((bf16[256,128]{1,0:T(8,128)(2,1)S(1)}, bf16[256,128]{1,0:T(8,128)(2,1)S(1)}, u32[]{:S(2)}, u32[]{:S(2)}) %collective-permute-start.18) | collective-permute-done | bytes 65568 | tf_op jit(solution)/shard_map/ppermute | solution.py:176
  42.8 0.0 collective-permute-done.15.their_logits_ref
  42.8 0.8 %last.1 = (bf16[256,128]{1,0:T(8,128)(2,1)}, f32[128,256]{1,0:T(8,128)}, f32[256,128]{1,0:T(8,128)}) custom-call(f32[256,128]{1,0:T(8,128)S(1)} %get-tuple-element.9.keep_ref, f32[256,128]{1,0:T(8,128)S(1)} %collective-permute-done.15.their_logits_ref, bf16[256,128]{1,0:T(8,128)(2,1)S(1)} %sum.1.refs_0_, ...), custom_call_target="tpu_custom_call" | custom-call | bytes 851968 | tf_op jit(solution)/shard_map/last/pallas_call | solution.py:23
  (1 shorter events, 0.0 us)
Async XLA Ops:
  1.8 10.5 %collective-permute-start.3 = (bf16[256,256]{1,0:T(8,128)(2,1)S(1)}, bf16[256,256]{1,0:T(8,128)(2,1)S(1)}, u32[]{:S(2)}, u32[]{:S(2)}) collective-permute-start(bf16[256,256]{1,0:T(8,128)(2,1)S(1)} %order.1.refs_4_), channel_id=1, source_target_pairs={{0,8},{2,10},{4,12},{6,14},{8,0},{10,2},{12,4},{14,6},{1,9},{3,11}... | collective-permute-start | bytes 393224 | tf_op jit(solution)/shard_map/ppermute | solution.py:176
  5.9 8.5 %collective-permute-start = (bf16[256,256]{1,0:T(8,128)(2,1)S(1)}, bf16[256,256]{1,0:T(8,128)(2,1)S(1)}, u32[]{:S(2)}, u32[]{:S(2)}) collective-permute-start(bf16[256,256]{1,0:T(8,128)(2,1)S(1)} %order.1.refs_4_), channel_id=1, source_target_pairs={{0,6},{2,4},{4,2},{6,0},{8,14},{10,12},{12,10},{14,8},{1,7},{3,5},... | collective-permute-start | bytes 393224 | tf_op jit(solution)/shard_map/ppermute | solution.py:176
  8.4 10.0 %collective-permute-start.1 = (bf16[256,256]{1,0:T(8,128)(2,1)S(1)}, bf16[256,256]{1,0:T(8,128)(2,1)S(1)}, u32[]{:S(2)}, u32[]{:S(2)}) collective-permute-start(bf16[256,256]{1,0:T(8,128)(2,1)S(1)} %order.1.refs_4_), channel_id=1, source_target_pairs={{0,2},{2,0},{4,6},{6,4},{8,10},{10,8},{12,14},{14,12},{1,3},{3,1},... | collective-permute-start | bytes 393224 | tf_op jit(solution)/shard_map/ppermute | solution.py:176
  8.9 9.5 %collective-permute-start.2 = (bf16[256,256]{1,0:T(8,128)(2,1)S(1)}, bf16[256,256]{1,0:T(8,128)(2,1)S(1)}, u32[]{:S(2)}, u32[]{:S(2)}) collective-permute-start(bf16[256,256]{1,0:T(8,128)(2,1)S(1)} %order.1.refs_4_), channel_id=1, source_target_pairs={{0,4},{2,6},{4,0},{6,2},{8,12},{10,14},{12,8},{14,10},{1,5},{3,7},... | collective-permute-start | bytes 393224 | tf_op jit(solution)/shard_map/ppermute | solution.py:176
  12.3 7.6 %collective-permute-start.4 = (bf16[256,256]{1,0:T(8,128)(2,1)S(1)}, bf16[256,256]{1,0:T(8,128)(2,1)S(1)}, u32[]{:S(2)}, u32[]{:S(2)}) collective-permute-start(bf16[256,256]{1,0:T(8,128)(2,1)S(1)} %collective-permute-done.3.refs_3_), channel_id=1, source_target_pairs={{0,6},{2,4},{4,2},{6,0},{8,14},{10,12},{12,10},{14,8},{1,7},{3,5},... | collective-permute-start | bytes 393224 | tf_op jit(solution)/shard_map/ppermute | solution.py:176
  13.9 7.6 %collective-permute-start.5 = (bf16[256,256]{1,0:T(8,128)(2,1)S(1)}, bf16[256,256]{1,0:T(8,128)(2,1)S(1)}, u32[]{:S(2)}, u32[]{:S(2)}) collective-permute-start(bf16[256,256]{1,0:T(8,128)(2,1)S(1)} %collective-permute-done.3.refs_3_), channel_id=1, source_target_pairs={{0,2},{2,0},{4,6},{6,4},{8,10},{10,8},{12,14},{14,12},{1,3},{3,1},... | collective-permute-start | bytes 393224 | tf_op jit(solution)/shard_map/ppermute | solution.py:176
  14.4 7.4 %collective-permute-start.6 = (bf16[256,256]{1,0:T(8,128)(2,1)S(1)}, bf16[256,256]{1,0:T(8,128)(2,1)S(1)}, u32[]{:S(2)}, u32[]{:S(2)}) collective-permute-start(bf16[256,256]{1,0:T(8,128)(2,1)S(1)} %collective-permute-done.3.refs_3_), channel_id=1, source_target_pairs={{0,4},{2,6},{4,0},{6,2},{8,12},{10,14},{12,8},{14,10},{1,5},{3,7},... | collective-permute-start | bytes 393224 | tf_op jit(solution)/shard_map/ppermute | solution.py:176
  18.9 5.3 %copy-start = (bf16[128,256]{1,0:T(8,128)(2,1)S(1)}, bf16[128,256]{1,0:T(8,128)(2,1)}, u32[]{:S(2)}) copy-start(bf16[128,256]{1,0:T(8,128)(2,1)} %first_ref.1) | copy-start | bytes 196612
  18.9 5.3 %copy-start.1 = (bf16[256,128]{1,0:T(8,128)(2,1)S(1)}, bf16[256,128]{1,0:T(8,128)(2,1)}, u32[]{:S(2)}) copy-start(bf16[256,128]{1,0:T(8,128)(2,1)} %second_ref.1) | copy-start | bytes 196612
  22.3 2.0 %collective-permute-start.7 = (f32[512,256]{1,0:T(8,128)S(1)}, f32[512,256]{1,0:T(8,128)S(1)}, u32[]{:S(2)}, u32[]{:S(2)}) collective-permute-start(f32[512,256]{1,0:T(8,128)S(1)} %first.1.mine_ref), channel_id=1, source_target_pairs={{0,1},{1,0},{2,3},{3,2},{4,5},{5,4},{6,7},{7,6},{8,9},{9,8},{10,11... | collective-permute-start | bytes 1572872 | tf_op jit(solution)/shard_map/ppermute | solution.py:176
  24.8 10.6 %collective-permute-start.10 = (bf16[512,128]{1,0:T(8,128)(2,1)S(1)}, bf16[512,128]{1,0:T(8,128)(2,1)S(1)}, u32[]{:S(2)}, u32[]{:S(2)}) collective-permute-start(bf16[512,128]{1,0:T(8,128)(2,1)S(1)} %get-tuple-element.8.refs_1_.refs_0_), channel_id=1, source_target_pairs={{0,6},{2,4},{4,2},{6,0},{8,14},{10,12},{12,10},{14,8},{1,7},{3,5},... | collective-permute-start | bytes 393224 | tf_op jit(solution)/shard_map/ppermute | solution.py:176
  26.3 5.6 %collective-permute-start.8 = (bf16[256,128]{1,0:T(8,128)(2,1)S(1)}, bf16[256,128]{1,0:T(8,128)(2,1)S(1)}, u32[]{:S(2)}, u32[]{:S(2)}) collective-permute-start(bf16[256,128]{1,0:T(8,128)(2,1)S(1)} %get-tuple-element.7), channel_id=1, source_target_pairs={{0,8},{2,10},{4,12},{6,14},{8,0},{10,2},{12,4},{14,6},{1,9},{3,11}... | collective-permute-start | bytes 196616 | tf_op jit(solution)/shard_map/ppermute | solution.py:176
  28.5 7.8 %collective-permute-start.11 = (bf16[512,128]{1,0:T(8,128)(2,1)S(1)}, bf16[512,128]{1,0:T(8,128)(2,1)S(1)}, u32[]{:S(2)}, u32[]{:S(2)}) collective-permute-start(bf16[512,128]{1,0:T(8,128)(2,1)S(1)} %get-tuple-element.8.refs_1_.refs_0_), channel_id=1, source_target_pairs={{0,2},{2,0},{4,6},{6,4},{8,10},{10,8},{12,14},{14,12},{1,3},{3,1},... | collective-permute-start | bytes 393224 | tf_op jit(solution)/shard_map/ppermute | solution.py:176
  30.0 6.3 %collective-permute-start.9 = (bf16[512,128]{1,0:T(8,128)(2,1)S(1)}, bf16[512,128]{1,0:T(8,128)(2,1)S(1)}, u32[]{:S(2)}, u32[]{:S(2)}) collective-permute-start(bf16[512,128]{1,0:T(8,128)(2,1)S(1)} %get-tuple-element.8.refs_1_.refs_0_), channel_id=1, source_target_pairs={{0,4},{2,6},{4,0},{6,2},{8,12},{10,14},{12,8},{14,10},{1,5},{3,7},... | collective-permute-start | bytes 393224 | tf_op jit(solution)/shard_map/ppermute | solution.py:176
  31.9 7.3 %collective-permute-start.12 = (bf16[256,128]{1,0:T(8,128)(2,1)S(1)}, bf16[256,128]{1,0:T(8,128)(2,1)S(1)}, u32[]{:S(2)}, u32[]{:S(2)}) collective-permute-start(bf16[256,128]{1,0:T(8,128)(2,1)S(1)} %collective-permute-done.8.refs_0_), channel_id=1, source_target_pairs={{0,4},{2,6},{4,0},{6,2},{8,12},{10,14},{12,8},{14,10},{1,5},{3,7},... | collective-permute-start | bytes 196616 | tf_op jit(solution)/shard_map/ppermute | solution.py:176
  34.5 5.5 %collective-permute-start.13 = (bf16[256,128]{1,0:T(8,128)(2,1)S(1)}, bf16[256,128]{1,0:T(8,128)(2,1)S(1)}, u32[]{:S(2)}, u32[]{:S(2)}) collective-permute-start(bf16[256,128]{1,0:T(8,128)(2,1)S(1)} %collective-permute-done.8.refs_0_), channel_id=1, source_target_pairs={{0,6},{2,4},{4,2},{6,0},{8,14},{10,12},{12,10},{14,8},{1,7},{3,5},... | collective-permute-start | bytes 196616 | tf_op jit(solution)/shard_map/ppermute | solution.py:176
  35.4 5.0 %collective-permute-start.14 = (bf16[256,128]{1,0:T(8,128)(2,1)S(1)}, bf16[256,128]{1,0:T(8,128)(2,1)S(1)}, u32[]{:S(2)}, u32[]{:S(2)}) collective-permute-start(bf16[256,128]{1,0:T(8,128)(2,1)S(1)} %collective-permute-done.8.refs_0_), channel_id=1, source_target_pairs={{0,2},{2,0},{4,6},{6,4},{8,10},{10,8},{12,14},{14,12},{1,3},{3,1},... | collective-permute-start | bytes 196616 | tf_op jit(solution)/shard_map/ppermute | solution.py:176
  36.3 5.2 %collective-permute-start.16 = (bf16[256,128]{1,0:T(8,128)(2,1)S(1)}, bf16[256,128]{1,0:T(8,128)(2,1)S(1)}, u32[]{:S(2)}, u32[]{:S(2)}) collective-permute-start(bf16[256,128]{1,0:T(8,128)(2,1)S(1)} %sum.1.refs_0_), channel_id=1, source_target_pairs={{0,8},{2,10},{4,12},{6,14},{8,0},{10,2},{12,4},{14,6},{1,9},{3,11}... | collective-permute-start | bytes 196616 | tf_op jit(solution)/shard_map/ppermute | solution.py:176
  40.8 2.1 %collective-permute-start.15 = (f32[256,128]{1,0:T(8,128)S(1)}, f32[256,128]{1,0:T(8,128)S(1)}, u32[]{:S(2)}, u32[]{:S(2)}) collective-permute-start(f32[256,128]{1,0:T(8,128)S(1)} %get-tuple-element.10), channel_id=1, source_target_pairs={{0,1},{1,0},{2,3},{3,2},{4,5},{5,4},{6,7},{7,6},{8,9},{9,8},{10,11... | collective-permute-start | bytes 393224 | tf_op jit(solution)/shard_map/ppermute | solution.py:176
  40.8 1.4 %collective-permute-start.17 = (bf16[256,128]{1,0:T(8,128)(2,1)S(1)}, bf16[256,128]{1,0:T(8,128)(2,1)S(1)}, u32[]{:S(2)}, u32[]{:S(2)}) collective-permute-start(bf16[256,128]{1,0:T(8,128)(2,1)S(1)} %sum.1.refs_0_), channel_id=1, source_target_pairs={{0,1},{1,0},{2,3},{3,2},{4,5},{5,4},{6,7},{7,6},{8,9},{9,8},{10,11... | collective-permute-start | bytes 196616 | tf_op jit(solution)/shard_map/ppermute | solution.py:176
  41.6 1.3 %collective-permute-start.18 = (bf16[256,128]{1,0:T(8,128)(2,1)S(1)}, bf16[256,128]{1,0:T(8,128)(2,1)S(1)}, u32[]{:S(2)}, u32[]{:S(2)}) collective-permute-start(bf16[256,128]{1,0:T(8,128)(2,1)S(1)} %collective-permute-done.16.refs_1_), channel_id=1, source_target_pairs={{0,1},{1,0},{2,3},{3,2},{4,5},{5,4},{6,7},{7,6},{8,9},{9,8},{10,11... | collective-permute-start | bytes 196616 | tf_op jit(solution)/shard_map/ppermute | solution.py:176

commit v6 on v5

--- a/solution.py
+++ b/solution.py
@@ -110,17 +110,15 @@
     own = mine_ref[at, :feat] + theirs_ref[at, :feat]
     own_pre = dot(own.astype(jnp.bfloat16), first_ref[...])
     own_hidden = (own_pre * jax.nn.sigmoid(own_pre)).astype(jnp.bfloat16)
-    projected = dot(own_hidden, second_ref[...]).astype(jnp.bfloat16)
-    projected_ref[...] = projected
-    out_ref[:nodes, :] = projected
+    projected_ref[...] = dot(own_hidden, second_ref[...]).astype(jnp.bfloat16)
 
     pre = dot(aggregated, first_half)
     gate = jax.nn.sigmoid(pre)
     hidden = (pre * gate).astype(jnp.bfloat16)
     hidden_grads = dot(back, second_half, ((1,), (1,)))
     pre_grads = (hidden_grads * gate * (1.0 + pre * (1.0 - gate))).astype(jnp.bfloat16)
-    out_ref[nodes : nodes + half, :] = dot(hidden, back, ((0,), (0,))).astype(jnp.bfloat16)
-    out_ref[nodes + half :, :] = dot(aggregated, pre_grads, ((0,), (0,))).astype(jnp.bfloat16)
+    out_ref[:half, :] = dot(hidden, back, ((0,), (0,))).astype(jnp.bfloat16)
+    out_ref[half:, :] = dot(aggregated, pre_grads, ((0,), (0,))).astype(jnp.bfloat16)
 
 
 def early_logits_kernel(masks, dense_ref, *refs):
@@ -129,11 +127,11 @@
     early_kernel(masks, dense_ref, *(piece.at[:nodes, :] for piece in pieces), out_ref)
 
 
-def more_logits_kernel(masks, dense_ref, early_ref, *refs):
-    *pieces, out_ref = refs
-    nodes = out_ref.shape[0] // 2
-    tops = (piece.at[:nodes, :] for piece in pieces)
-    first_kernel(masks, dense_ref, early_ref, *tops, out_ref)
+def join_kernel(*refs):
+    *parts, out_ref = refs
+    nodes = parts[0].shape[0]
+    for i, part in enumerate(parts):
+        out_ref[i * nodes : (i + 1) * nodes, :] = part[...]
 
 
 def sum_kernel(*refs):
@@ -146,8 +144,12 @@
 
 
 def second_kernel(masks, dense_ref, early_ref, *refs):
-    *pieces, keep_ref, send_ref = refs
+    *joined, keep_ref, send_ref = refs
     nodes = keep_ref.shape[0]
+    pieces = [
+        piece.at[start : start + nodes, :]
+        for piece in joined for start in range(0, piece.shape[0], nodes)
+    ]
     col = lax.axis_index("col")
     for where, ref in ((col, keep_ref), (1 - col, send_ref)):
         at = pl.ds(pl.multiple_of(where * nodes, nodes), nodes)
@@ -269,31 +271,33 @@
         [VMEM] * (2 + len(late)), 40000 * 10**6, "first",
         dense, partial, *(found[k] for k in late),
     )
-    projected, both = call(
-        middle_kernel, (shape((nodes, classes), bf16), shape((nodes + hid, classes), bf16)),
+    projected, grads = call(
+        middle_kernel, (shape((nodes, classes), bf16), shape((hid, classes), bf16)),
         [VMEM] * 4, 10 * slab * feat * hid,
         "middle", mine, exchange(mine, "col", 1), weight_first, weight_second,
     )
     flops = 2 * slab * nodes * classes
     far = from_far(projected)
-    found = {0: both} | far | from_near(both, far)
-    near, direct, late = arrival((2, 3, 1), (2, 3, 1))
-    partial = call(
-        functools.partial(early_logits_kernel, direct), shape((slab, classes), f32),
-        [VMEM] * (1 + len(direct)), 15000 * 10**6, "early_logits", dense, *(found[k] for k in direct),
-    )
-    partial = call(
-        functools.partial(more_logits_kernel, near), shape((slab, classes), f32),
-        [VMEM] * (2 + len(near)), 1 * 10**6, "more_logits", dense, partial, *(found[k] for k in near),
-    )
-    keep, send = call(
-        functools.partial(second_kernel, late), (shape((nodes, classes), f32),) * 2,
-        [VMEM] * (2 + len(late)), 1 * 10**6, "second",
-        dense, partial, *(found[k] for k in late),
-    )
-    parts = [found[low] for low in range(near_size())]
+    near_grads = from_near(grads, {})
+    parts = [grads, *(near_grads[low] for low in (2, 3, 1))]
     total = call(
         sum_kernel, shape((hid, classes), bf16), [VMEM] * len(parts), 0, "sum", *parts
+    )
+    blocks = {0: projected} | far
+    pair = call(
+        join_kernel, shape((nodes * len(blocks), classes), bf16), [VMEM] * len(blocks), 15000000000,
+        "join", *blocks.values(),
+    )
+    found = from_near(pair, {})
+    partial = call(
+        functools.partial(early_logits_kernel, [*blocks]), shape((slab, classes), f32),
+        [VMEM] * (1 + len(blocks)), 15000000000, "early_logits", dense, *blocks.values(),
+    )
+    lows = [*(3, 2, 1)]
+    keep, send = call(
+        functools.partial(second_kernel, [k + low for low in lows for k in blocks]),
+        (shape((nodes, classes), f32),) * 2,
+        [VMEM] * (2 + len(lows)), 10**6, "second", dense, partial, *(found[k] for k in lows),
     )
     sums = [total, *from_far(total).values()]
     return call(

time: 43.8 us -> 43.1 us (0.984)
  starting transfers between devices: 24.1 us -> 22.5 us
  waiting for transfers between devices: 12.1 us -> 13.3 us
    ppermute x19, starting transfers between devices: 24.1 us -> 22.5 us  [exchange(): return lax.ppermute(x, axis, [(i, i ^ mask) for i in range(size)])]
    ppermute x19, waiting for transfers between devices: 12.1 us -> 13.3 us  [exchange(): return lax.ppermute(x, axis, [(i, i ^ mask) for i in range(size)])]
  transfers between devices with their start and end apart: 19 -> 19, of which waited for: 11 -> 10; matrix products, arithmetic and copies ran while one was open for 0% -> 0% of each run, Pallas kernels for 7% -> 7%
where the time goes in v6:
time: 43.1 us; the launch traced here: 42.9 us
  starting transfers between devices  22.5 us (52%)
  waiting for transfers between devices  13.3 us (31%)
  Pallas kernels  5.65 us (13%)
  between operations  1.4 us (3%)
    ppermute x19, starting transfers between devices, exchange(): return lax.ppermute(x, axis, [(i, i ^ mask) for i in range(size)])  22.5 us
    ppermute x19, waiting for transfers between devices, exchange(): return lax.ppermute(x, axis, [(i, i ^ mask) for i in range(size)])  13.3 us
    pallas_call x8, Pallas kernels, call(): pl.pallas_call(kernel, out_shape=out_shape, in_specs=in_specs, out_specs=...  3.08 us
    pallas_call x1, Pallas kernels, shards(): pl.pallas_call(functools.partial(dense_kernel, nodes // size), out_shape=...  1.42 us
    pallas_call x1, Pallas kernels, shards(): pl.pallas_call(order_kernel, out_shape=shape((nodes, feat + classes), bf1...  1.15 us
  transfers between devices with their start and end apart: 19, of which 10 were waited for; matrix products, arithmetic and copies ran while one was open for 0% of the time, Pallas kernels for 7%

profile of v6, /device:TPU:0, one launch (start us, length us, event | category | flops | bytes accessed | tf_op | source)
XLA Modules:
  0.0 42.9 jit_solution(5627081802469126449)
XLA Ops:
  0.6 1.1 %order.1.refs_4_ = bf16[256,256]{1,0:T(8,128)(2,1)S(1)} custom-call(s32[1,256]{1,0:T(1,128)} %order_hbm.1, bf16[256,128]{1,0:T(8,128)(2,1)} %features_hbm.1, bf16[256,128]{1,0:T(8,128)(2,1)} %grads_hbm.1), custom_call_target="tpu_custom_call" | custom-call | tf_op jit(solution)/shard_map/order/pallas_call | solution.py:229
  1.8 4.1 %collective-permute-start.3 = (bf16[256,256]{1,0:T(8,128)(2,1)S(1)}, bf16[256,256]{1,0:T(8,128)(2,1)S(1)}, u32[]{:S(2)}, u32[]{:S(2)}) collective-permute-start(bf16[256,256]{1,0:T(8,128)(2,1)S(1)} %order.1.refs_4_), channel_id=1, source_target_pairs={{0,8},{2,10},{4,12},{6,14},{8,0},{10,2},{12,4},{14,6},{1,9},{3,11}... | collective-permute-start | bytes 393224 | tf_op jit(solution)/shard_map/ppermute | solution.py:178
  5.9 2.5 %collective-permute-start = (bf16[256,256]{1,0:T(8,128)(2,1)S(1)}, bf16[256,256]{1,0:T(8,128)(2,1)S(1)}, u32[]{:S(2)}, u32[]{:S(2)}) collective-permute-start(bf16[256,256]{1,0:T(8,128)(2,1)S(1)} %order.1.refs_4_), channel_id=1, source_target_pairs={{0,6},{2,4},{4,2},{6,0},{8,14},{10,12},{12,10},{14,8},{1,7},{3,5},... | collective-permute-start | bytes 393224 | tf_op jit(solution)/shard_map/ppermute | solution.py:178
  8.4 0.5 %collective-permute-start.1 = (bf16[256,256]{1,0:T(8,128)(2,1)S(1)}, bf16[256,256]{1,0:T(8,128)(2,1)S(1)}, u32[]{:S(2)}, u32[]{:S(2)}) collective-permute-start(bf16[256,256]{1,0:T(8,128)(2,1)S(1)} %order.1.refs_4_), channel_id=1, source_target_pairs={{0,2},{2,0},{4,6},{6,4},{8,10},{10,8},{12,14},{14,12},{1,3},{3,1},... | collective-permute-start | bytes 393224 | tf_op jit(solution)/shard_map/ppermute | solution.py:178
  8.9 0.4 %collective-permute-start.2 = (bf16[256,256]{1,0:T(8,128)(2,1)S(1)}, bf16[256,256]{1,0:T(8,128)(2,1)S(1)}, u32[]{:S(2)}, u32[]{:S(2)}) collective-permute-start(bf16[256,256]{1,0:T(8,128)(2,1)S(1)} %order.1.refs_4_), channel_id=1, source_target_pairs={{0,4},{2,6},{4,0},{6,2},{8,12},{10,14},{12,8},{14,10},{1,5},{3,7},... | collective-permute-start | bytes 393224 | tf_op jit(solution)/shard_map/ppermute | solution.py:178
  9.4 2.9 %collective-permute-done.3.refs_3_ = bf16[256,256]{1,0:T(8,128)(2,1)S(1)} collective-permute-done((bf16[256,256]{1,0:T(8,128)(2,1)S(1)}, bf16[256,256]{1,0:T(8,128)(2,1)S(1)}, u32[]{:S(2)}, u32[]{:S(2)}) %collective-permute-start.3) | collective-permute-done | bytes 131104 | tf_op jit(solution)/shard_map/ppermute | solution.py:178
  12.3 1.6 %collective-permute-start.4 = (bf16[256,256]{1,0:T(8,128)(2,1)S(1)}, bf16[256,256]{1,0:T(8,128)(2,1)S(1)}, u32[]{:S(2)}, u32[]{:S(2)}) collective-permute-start(bf16[256,256]{1,0:T(8,128)(2,1)S(1)} %collective-permute-done.3.refs_3_), channel_id=1, source_target_pairs={{0,6},{2,4},{4,2},{6,0},{8,14},{10,12},{12,10},{14,8},{1,7},{3,5},... | collective-permute-start | bytes 393224 | tf_op jit(solution)/shard_map/ppermute | solution.py:178
  13.9 0.5 %collective-permute-start.5 = (bf16[256,256]{1,0:T(8,128)(2,1)S(1)}, bf16[256,256]{1,0:T(8,128)(2,1)S(1)}, u32[]{:S(2)}, u32[]{:S(2)}) collective-permute-start(bf16[256,256]{1,0:T(8,128)(2,1)S(1)} %collective-permute-done.3.refs_3_), channel_id=1, source_target_pairs={{0,2},{2,0},{4,6},{6,4},{8,10},{10,8},{12,14},{14,12},{1,3},{3,1},... | collective-permute-start | bytes 393224 | tf_op jit(solution)/shard_map/ppermute | solution.py:178
  14.4 0.0 collective-permute-done.refs_0_
  14.4 1.6 %collective-permute-start.6 = (bf16[256,256]{1,0:T(8,128)(2,1)S(1)}, bf16[256,256]{1,0:T(8,128)(2,1)S(1)}, u32[]{:S(2)}, u32[]{:S(2)}) collective-permute-start(bf16[256,256]{1,0:T(8,128)(2,1)S(1)} %collective-permute-done.3.refs_3_), channel_id=1, source_target_pairs={{0,4},{2,6},{4,0},{6,2},{8,12},{10,14},{12,8},{14,10},{1,5},{3,7},... | collective-permute-start | bytes 393224 | tf_op jit(solution)/shard_map/ppermute | solution.py:178
  16.7 1.4 %dense.1.dense_ref = bf16[512,2048]{1,0:T(8,128)(2,1)S(1)} custom-call(s32[1,1]{1,0:T(1,128)S(6)} %copy.12.count_ref, s32[1,32]{1,0:T(1,128)} %bitcast.4, s32[1,32]{1,0:T(1,128)} %bitcast.5, bf16[32,128,128]{2,1,0:T(8,128)(2,1)} %bitcast.3), custom_call_target="tpu_custom_call" | custom-call | flops 1000000 | bytes 2097152 | tf_op jit(solution)/shard_map/dense/pallas_call | solution.py:242
  18.1 0.0 collective-permute-done.1.refs_1_
  18.1 0.0 collective-permute-done.2.refs_2_
  18.1 0.5 %early.1.early_ref = f32[512,256]{1,0:T(8,128)S(1)} custom-call(bf16[512,2048]{1,0:T(8,128)(2,1)S(1)} %dense.1.dense_ref, bf16[256,256]{1,0:T(8,128)(2,1)S(1)} %collective-permute-done.refs_0_, bf16[256,256]{1,0:T(8,128)(2,1)S(1)} %collective-permute-done.1.refs_1_, bf16[256,256]{1,0:T(8,128)(2,1)S(1)} %collective-permute-done.2.refs_2_, ...), custom_call_target="tpu_custom_call" | custom-call | flops 1000000 | bytes 3276800 | tf_op jit(solution)/shard_map/early/pallas_call | solution.py:23
  18.7 0.0 copy-start
  18.7 0.0 copy-start.1
  18.7 1.2 %collective-permute-done.4.refs_0_ = bf16[256,256]{1,0:T(8,128)(2,1)S(1)} collective-permute-done((bf16[256,256]{1,0:T(8,128)(2,1)S(1)}, bf16[256,256]{1,0:T(8,128)(2,1)S(1)}, u32[]{:S(2)}, u32[]{:S(2)}) %collective-permute-start.4) | collective-permute-done | bytes 131104 | tf_op jit(solution)/shard_map/ppermute | solution.py:178
  19.9 1.6 %collective-permute-done.5.refs_1_ = bf16[256,256]{1,0:T(8,128)(2,1)S(1)} collective-permute-done((bf16[256,256]{1,0:T(8,128)(2,1)S(1)}, bf16[256,256]{1,0:T(8,128)(2,1)S(1)}, u32[]{:S(2)}, u32[]{:S(2)}) %collective-permute-start.5) | collective-permute-done | bytes 131104 | tf_op jit(solution)/shard_map/ppermute | solution.py:178
  21.5 0.4 collective-permute-done.6.refs_2_
  21.9 0.4 first.1.mine_ref
  22.3 0.1 collective-permute-start.7
  22.3 1.9 %collective-permute-done.7.theirs_ref = f32[512,256]{1,0:T(8,128)S(1)} collective-permute-done((f32[512,256]{1,0:T(8,128)S(1)}, f32[512,256]{1,0:T(8,128)S(1)}, u32[]{:S(2)}, u32[]{:S(2)}) %collective-permute-start.7) | collective-permute-done | bytes 524320 | tf_op jit(solution)/shard_map/ppermute | solution.py:178
  24.2 0.0 copy-done
  24.2 0.0 copy-done.1
  24.2 0.5 %middle.1 = (bf16[256,128]{1,0:T(8,128)(2,1)S(1)}, bf16[256,128]{1,0:T(8,128)(2,1)S(1)}) custom-call(f32[512,256]{1,0:T(8,128)S(1)} %first.1.mine_ref, f32[512,256]{1,0:T(8,128)S(1)} %collective-permute-done.7.theirs_ref, bf16[128,256]{1,0:T(8,128)(2,1)S(1)} %copy-done, bf16[256,128]{1,0:T(8,128)(2,1)S(1)} %copy-done.1), custom_call_target="tpu_custom_call" | custom-call | flops 167772160 | bytes 1310720 | tf_op jit(solution)/shard_map/middle/pallas_call | solution.py:23
  24.8 2.0 %collective-permute-start.8 = (bf16[256,128]{1,0:T(8,128)(2,1)S(1)}, bf16[256,128]{1,0:T(8,128)(2,1)S(1)}, u32[]{:S(2)}, u32[]{:S(2)}) collective-permute-start(bf16[256,128]{1,0:T(8,128)(2,1)S(1)} %get-tuple-element.7.refs_0_), channel_id=1, source_target_pairs={{0,8},{2,10},{4,12},{6,14},{8,0},{10,2},{12,4},{14,6},{1,9},{3,11}... | collective-permute-start | bytes 196616 | tf_op jit(solution)/shard_map/ppermute | solution.py:178
  26.8 1.8 %collective-permute-start.13 = (bf16[256,128]{1,0:T(8,128)(2,1)S(1)}, bf16[256,128]{1,0:T(8,128)(2,1)S(1)}, u32[]{:S(2)}, u32[]{:S(2)}) collective-permute-start(bf16[256,128]{1,0:T(8,128)(2,1)S(1)} %get-tuple-element.10.refs_0_), channel_id=1, source_target_pairs={{0,4},{2,6},{4,0},{6,2},{8,12},{10,14},{12,8},{14,10},{1,5},{3,7},... | collective-permute-start | bytes 196616 | tf_op jit(solution)/shard_map/ppermute | solution.py:178
  28.6 0.2 collective-permute-start.14
  28.8 1.5 %collective-permute-start.15 = (bf16[256,128]{1,0:T(8,128)(2,1)S(1)}, bf16[256,128]{1,0:T(8,128)(2,1)S(1)}, u32[]{:S(2)}, u32[]{:S(2)}) collective-permute-start(bf16[256,128]{1,0:T(8,128)(2,1)S(1)} %get-tuple-element.10.refs_0_), channel_id=1, source_target_pairs={{0,2},{2,0},{4,6},{6,4},{8,10},{10,8},{12,14},{14,12},{1,3},{3,1},... | collective-permute-start | bytes 196616 | tf_op jit(solution)/shard_map/ppermute | solution.py:178
  30.3 1.1 %collective-permute-done.8.refs_1_ = bf16[256,128]{1,0:T(8,128)(2,1)S(1)} collective-permute-done((bf16[256,128]{1,0:T(8,128)(2,1)S(1)}, bf16[256,128]{1,0:T(8,128)(2,1)S(1)}, u32[]{:S(2)}, u32[]{:S(2)}) %collective-permute-start.8) | collective-permute-done | bytes 65568 | tf_op jit(solution)/shard_map/ppermute | solution.py:178
  31.4 0.7 %collective-permute-start.10 = (bf16[512,128]{1,0:T(8,128)(2,1)S(1)}, bf16[512,128]{1,0:T(8,128)(2,1)S(1)}, u32[]{:S(2)}, u32[]{:S(2)}) collective-permute-start(bf16[512,128]{1,0:T(8,128)(2,1)S(1)} %join.1), channel_id=1, source_target_pairs={{0,4},{2,6},{4,0},{6,2},{8,12},{10,14},{12,8},{14,10},{1,5},{3,7},... | collective-permute-start | bytes 393224 | tf_op jit(solution)/shard_map/ppermute | solution.py:178
  32.1 0.6 %collective-permute-start.11 = (bf16[512,128]{1,0:T(8,128)(2,1)S(1)}, bf16[512,128]{1,0:T(8,128)(2,1)S(1)}, u32[]{:S(2)}, u32[]{:S(2)}) collective-permute-start(bf16[512,128]{1,0:T(8,128)(2,1)S(1)} %join.1), channel_id=1, source_target_pairs={{0,2},{2,0},{4,6},{6,4},{8,10},{10,8},{12,14},{14,12},{1,3},{3,1},... | collective-permute-start | bytes 393224 | tf_op jit(solution)/shard_map/ppermute | solution.py:178
  32.7 0.0 collective-permute-done.13.refs_1_
  32.7 2.3 %collective-permute-start.9 = (bf16[512,128]{1,0:T(8,128)(2,1)S(1)}, bf16[512,128]{1,0:T(8,128)(2,1)S(1)}, u32[]{:S(2)}, u32[]{:S(2)}) collective-permute-start(bf16[512,128]{1,0:T(8,128)(2,1)S(1)} %join.1), channel_id=1, source_target_pairs={{0,6},{2,4},{4,2},{6,0},{8,14},{10,12},{12,10},{14,8},{1,7},{3,5},... | collective-permute-start | bytes 393224 | tf_op jit(solution)/shard_map/ppermute | solution.py:178
  35.0 0.0 collective-permute-done.14.refs_2_
  35.0 0.0 collective-permute-done.15.refs_3_
  35.0 1.5 %collective-permute-start.16 = (bf16[256,128]{1,0:T(8,128)(2,1)S(1)}, bf16[256,128]{1,0:T(8,128)(2,1)S(1)}, u32[]{:S(2)}, u32[]{:S(2)}) collective-permute-start(bf16[256,128]{1,0:T(8,128)(2,1)S(1)} %sum.1.refs_0_), channel_id=1, source_target_pairs={{0,8},{2,10},{4,12},{6,14},{8,0},{10,2},{12,4},{14,6},{1,9},{3,11}... | collective-permute-start | bytes 196616 | tf_op jit(solution)/shard_map/ppermute | solution.py:178
  36.5 0.3 early_logits.1.early_ref
  36.8 1.6 %collective-permute-done.10.refs_1_ = bf16[512,128]{1,0:T(8,128)(2,1)S(1)} collective-permute-done((bf16[512,128]{1,0:T(8,128)(2,1)S(1)}, bf16[512,128]{1,0:T(8,128)(2,1)S(1)}, u32[]{:S(2)}, u32[]{:S(2)}) %collective-permute-start.10) | collective-permute-done | bytes 131104 | tf_op jit(solution)/shard_map/ppermute | solution.py:178
  38.4 0.0 collective-permute-done.11.refs_2_
  38.4 1.4 %collective-permute-done.9.refs_0_ = bf16[512,128]{1,0:T(8,128)(2,1)S(1)} collective-permute-done((bf16[512,128]{1,0:T(8,128)(2,1)S(1)}, bf16[512,128]{1,0:T(8,128)(2,1)S(1)}, u32[]{:S(2)}, u32[]{:S(2)}) %collective-permute-start.9) | collective-permute-done | bytes 131104 | tf_op jit(solution)/shard_map/ppermute | solution.py:178
  39.8 0.6 %second.1 = (f32[256,128]{1,0:T(8,128)S(1)}, f32[256,128]{1,0:T(8,128)S(1)}) custom-call(bf16[512,2048]{1,0:T(8,128)(2,1)S(1)} %dense.1.dense_ref, f32[512,128]{1,0:T(8,128)S(1)} %early_logits.1.early_ref, bf16[512,128]{1,0:T(8,128)(2,1)S(1)} %collective-permute-done.9.refs_0_, bf16[512,128]{1,0:T(8,128)(2,1)S(1)} %collective-permute-done.10.refs_1_, ...), custom_call_target="tpu_custom_call" | custom-call | flops 1000000 | bytes 3014656 | tf_op jit(solution)/shard_map/second/pallas_call | solution.py:23
  40.3 0.1 collective-permute-start.12
  40.4 0.5 %collective-permute-start.17 = (bf16[256,128]{1,0:T(8,128)(2,1)S(1)}, bf16[256,128]{1,0:T(8,128)(2,1)S(1)}, u32[]{:S(2)}, u32[]{:S(2)}) collective-permute-start(bf16[256,128]{1,0:T(8,128)(2,1)S(1)} %sum.1.refs_0_), channel_id=1, source_target_pairs={{0,1},{1,0},{2,3},{3,2},{4,5},{5,4},{6,7},{7,6},{8,9},{9,8},{10,11... | collective-permute-start | bytes 196616 | tf_op jit(solution)/shard_map/ppermute | solution.py:178
  40.9 0.0 collective-permute-done.16.refs_1_
  40.9 0.1 collective-permute-start.18
  41.0 0.8 %collective-permute-done.17.refs_2_ = bf16[256,128]{1,0:T(8,128)(2,1)S(1)} collective-permute-done((bf16[256,128]{1,0:T(8,128)(2,1)S(1)}, bf16[256,128]{1,0:T(8,128)(2,1)S(1)}, u32[]{:S(2)}, u32[]{:S(2)}) %collective-permute-start.17) | collective-permute-done | bytes 65568 | tf_op jit(solution)/shard_map/ppermute | solution.py:178
  41.8 0.3 collective-permute-done.18.refs_3_
  42.2 0.0 collective-permute-done.12.their_logits_ref
  42.2 0.8 %last.1 = (bf16[256,128]{1,0:T(8,128)(2,1)}, f32[128,256]{1,0:T(8,128)}, f32[256,128]{1,0:T(8,128)}) custom-call(f32[256,128]{1,0:T(8,128)S(1)} %get-tuple-element.8.keep_ref, f32[256,128]{1,0:T(8,128)S(1)} %collective-permute-done.12.their_logits_ref, bf16[256,128]{1,0:T(8,128)(2,1)S(1)} %sum.1.refs_0_, ...), custom_call_target="tpu_custom_call" | custom-call | bytes 851968 | tf_op jit(solution)/shard_map/last/pallas_call | solution.py:23
  (2 shorter events, 0.0 us)
Async XLA Ops:
  1.8 10.5 %collective-permute-start.3 = (bf16[256,256]{1,0:T(8,128)(2,1)S(1)}, bf16[256,256]{1,0:T(8,128)(2,1)S(1)}, u32[]{:S(2)}, u32[]{:S(2)}) collective-permute-start(bf16[256,256]{1,0:T(8,128)(2,1)S(1)} %order.1.refs_4_), channel_id=1, source_target_pairs={{0,8},{2,10},{4,12},{6,14},{8,0},{10,2},{12,4},{14,6},{1,9},{3,11}... | collective-permute-start | bytes 393224 | tf_op jit(solution)/shard_map/ppermute | solution.py:178
  5.9 8.5 %collective-permute-start = (bf16[256,256]{1,0:T(8,128)(2,1)S(1)}, bf16[256,256]{1,0:T(8,128)(2,1)S(1)}, u32[]{:S(2)}, u32[]{:S(2)}) collective-permute-start(bf16[256,256]{1,0:T(8,128)(2,1)S(1)} %order.1.refs_4_), channel_id=1, source_target_pairs={{0,6},{2,4},{4,2},{6,0},{8,14},{10,12},{12,10},{14,8},{1,7},{3,5},... | collective-permute-start | bytes 393224 | tf_op jit(solution)/shard_map/ppermute | solution.py:178
  8.4 9.7 %collective-permute-start.1 = (bf16[256,256]{1,0:T(8,128)(2,1)S(1)}, bf16[256,256]{1,0:T(8,128)(2,1)S(1)}, u32[]{:S(2)}, u32[]{:S(2)}) collective-permute-start(bf16[256,256]{1,0:T(8,128)(2,1)S(1)} %order.1.refs_4_), channel_id=1, source_target_pairs={{0,2},{2,0},{4,6},{6,4},{8,10},{10,8},{12,14},{14,12},{1,3},{3,1},... | collective-permute-start | bytes 393224 | tf_op jit(solution)/shard_map/ppermute | solution.py:178
  8.9 9.2 %collective-permute-start.2 = (bf16[256,256]{1,0:T(8,128)(2,1)S(1)}, bf16[256,256]{1,0:T(8,128)(2,1)S(1)}, u32[]{:S(2)}, u32[]{:S(2)}) collective-permute-start(bf16[256,256]{1,0:T(8,128)(2,1)S(1)} %order.1.refs_4_), channel_id=1, source_target_pairs={{0,4},{2,6},{4,0},{6,2},{8,12},{10,14},{12,8},{14,10},{1,5},{3,7},... | collective-permute-start | bytes 393224 | tf_op jit(solution)/shard_map/ppermute | solution.py:178
  12.3 7.6 %collective-permute-start.4 = (bf16[256,256]{1,0:T(8,128)(2,1)S(1)}, bf16[256,256]{1,0:T(8,128)(2,1)S(1)}, u32[]{:S(2)}, u32[]{:S(2)}) collective-permute-start(bf16[256,256]{1,0:T(8,128)(2,1)S(1)} %collective-permute-done.3.refs_3_), channel_id=1, source_target_pairs={{0,6},{2,4},{4,2},{6,0},{8,14},{10,12},{12,10},{14,8},{1,7},{3,5},... | collective-permute-start | bytes 393224 | tf_op jit(solution)/shard_map/ppermute | solution.py:178
  13.9 7.6 %collective-permute-start.5 = (bf16[256,256]{1,0:T(8,128)(2,1)S(1)}, bf16[256,256]{1,0:T(8,128)(2,1)S(1)}, u32[]{:S(2)}, u32[]{:S(2)}) collective-permute-start(bf16[256,256]{1,0:T(8,128)(2,1)S(1)} %collective-permute-done.3.refs_3_), channel_id=1, source_target_pairs={{0,2},{2,0},{4,6},{6,4},{8,10},{10,8},{12,14},{14,12},{1,3},{3,1},... | collective-permute-start | bytes 393224 | tf_op jit(solution)/shard_map/ppermute | solution.py:178
  14.4 7.4 %collective-permute-start.6 = (bf16[256,256]{1,0:T(8,128)(2,1)S(1)}, bf16[256,256]{1,0:T(8,128)(2,1)S(1)}, u32[]{:S(2)}, u32[]{:S(2)}) collective-permute-start(bf16[256,256]{1,0:T(8,128)(2,1)S(1)} %collective-permute-done.3.refs_3_), channel_id=1, source_target_pairs={{0,4},{2,6},{4,0},{6,2},{8,12},{10,14},{12,8},{14,10},{1,5},{3,7},... | collective-permute-start | bytes 393224 | tf_op jit(solution)/shard_map/ppermute | solution.py:178
  18.7 5.6 %copy-start = (bf16[128,256]{1,0:T(8,128)(2,1)S(1)}, bf16[128,256]{1,0:T(8,128)(2,1)}, u32[]{:S(2)}) copy-start(bf16[128,256]{1,0:T(8,128)(2,1)} %first_ref.1) | copy-start | bytes 196612
  18.7 5.6 %copy-start.1 = (bf16[256,128]{1,0:T(8,128)(2,1)S(1)}, bf16[256,128]{1,0:T(8,128)(2,1)}, u32[]{:S(2)}) copy-start(bf16[256,128]{1,0:T(8,128)(2,1)} %second_ref.1) | copy-start | bytes 196612
  22.3 2.0 %collective-permute-start.7 = (f32[512,256]{1,0:T(8,128)S(1)}, f32[512,256]{1,0:T(8,128)S(1)}, u32[]{:S(2)}, u32[]{:S(2)}) collective-permute-start(f32[512,256]{1,0:T(8,128)S(1)} %first.1.mine_ref), channel_id=1, source_target_pairs={{0,1},{1,0},{2,3},{3,2},{4,5},{5,4},{6,7},{7,6},{8,9},{9,8},{10,11... | collective-permute-start | bytes 1572872 | tf_op jit(solution)/shard_map/ppermute | solution.py:178
  24.8 6.6 %collective-permute-start.8 = (bf16[256,128]{1,0:T(8,128)(2,1)S(1)}, bf16[256,128]{1,0:T(8,128)(2,1)S(1)}, u32[]{:S(2)}, u32[]{:S(2)}) collective-permute-start(bf16[256,128]{1,0:T(8,128)(2,1)S(1)} %get-tuple-element.7.refs_0_), channel_id=1, source_target_pairs={{0,8},{2,10},{4,12},{6,14},{8,0},{10,2},{12,4},{14,6},{1,9},{3,11}... | collective-permute-start | bytes 196616 | tf_op jit(solution)/shard_map/ppermute | solution.py:178
  26.8 5.9 %collective-permute-start.13 = (bf16[256,128]{1,0:T(8,128)(2,1)S(1)}, bf16[256,128]{1,0:T(8,128)(2,1)S(1)}, u32[]{:S(2)}, u32[]{:S(2)}) collective-permute-start(bf16[256,128]{1,0:T(8,128)(2,1)S(1)} %get-tuple-element.10.refs_0_), channel_id=1, source_target_pairs={{0,4},{2,6},{4,0},{6,2},{8,12},{10,14},{12,8},{14,10},{1,5},{3,7},... | collective-permute-start | bytes 196616 | tf_op jit(solution)/shard_map/ppermute | solution.py:178
  28.6 6.4 %collective-permute-start.14 = (bf16[256,128]{1,0:T(8,128)(2,1)S(1)}, bf16[256,128]{1,0:T(8,128)(2,1)S(1)}, u32[]{:S(2)}, u32[]{:S(2)}) collective-permute-start(bf16[256,128]{1,0:T(8,128)(2,1)S(1)} %get-tuple-element.10.refs_0_), channel_id=1, source_target_pairs={{0,6},{2,4},{4,2},{6,0},{8,14},{10,12},{12,10},{14,8},{1,7},{3,5},... | collective-permute-start | bytes 196616 | tf_op jit(solution)/shard_map/ppermute | solution.py:178
  28.8 6.2 %collective-permute-start.15 = (bf16[256,128]{1,0:T(8,128)(2,1)S(1)}, bf16[256,128]{1,0:T(8,128)(2,1)S(1)}, u32[]{:S(2)}, u32[]{:S(2)}) collective-permute-start(bf16[256,128]{1,0:T(8,128)(2,1)S(1)} %get-tuple-element.10.refs_0_), channel_id=1, source_target_pairs={{0,2},{2,0},{4,6},{6,4},{8,10},{10,8},{12,14},{14,12},{1,3},{3,1},... | collective-permute-start | bytes 196616 | tf_op jit(solution)/shard_map/ppermute | solution.py:178
  31.4 7.0 %collective-permute-start.10 = (bf16[512,128]{1,0:T(8,128)(2,1)S(1)}, bf16[512,128]{1,0:T(8,128)(2,1)S(1)}, u32[]{:S(2)}, u32[]{:S(2)}) collective-permute-start(bf16[512,128]{1,0:T(8,128)(2,1)S(1)} %join.1), channel_id=1, source_target_pairs={{0,4},{2,6},{4,0},{6,2},{8,12},{10,14},{12,8},{14,10},{1,5},{3,7},... | collective-permute-start | bytes 393224 | tf_op jit(solution)/shard_map/ppermute | solution.py:178
  32.1 6.2 %collective-permute-start.11 = (bf16[512,128]{1,0:T(8,128)(2,1)S(1)}, bf16[512,128]{1,0:T(8,128)(2,1)S(1)}, u32[]{:S(2)}, u32[]{:S(2)}) collective-permute-start(bf16[512,128]{1,0:T(8,128)(2,1)S(1)} %join.1), channel_id=1, source_target_pairs={{0,2},{2,0},{4,6},{6,4},{8,10},{10,8},{12,14},{14,12},{1,3},{3,1},... | collective-permute-start | bytes 393224 | tf_op jit(solution)/shard_map/ppermute | solution.py:178
  32.7 7.1 %collective-permute-start.9 = (bf16[512,128]{1,0:T(8,128)(2,1)S(1)}, bf16[512,128]{1,0:T(8,128)(2,1)S(1)}, u32[]{:S(2)}, u32[]{:S(2)}) collective-permute-start(bf16[512,128]{1,0:T(8,128)(2,1)S(1)} %join.1), channel_id=1, source_target_pairs={{0,6},{2,4},{4,2},{6,0},{8,14},{10,12},{12,10},{14,8},{1,7},{3,5},... | collective-permute-start | bytes 393224 | tf_op jit(solution)/shard_map/ppermute | solution.py:178
  35.0 5.9 %collective-permute-start.16 = (bf16[256,128]{1,0:T(8,128)(2,1)S(1)}, bf16[256,128]{1,0:T(8,128)(2,1)S(1)}, u32[]{:S(2)}, u32[]{:S(2)}) collective-permute-start(bf16[256,128]{1,0:T(8,128)(2,1)S(1)} %sum.1.refs_0_), channel_id=1, source_target_pairs={{0,8},{2,10},{4,12},{6,14},{8,0},{10,2},{12,4},{14,6},{1,9},{3,11}... | collective-permute-start | bytes 196616 | tf_op jit(solution)/shard_map/ppermute | solution.py:178
  40.3 1.8 %collective-permute-start.12 = (f32[256,128]{1,0:T(8,128)S(1)}, f32[256,128]{1,0:T(8,128)S(1)}, u32[]{:S(2)}, u32[]{:S(2)}) collective-permute-start(f32[256,128]{1,0:T(8,128)S(1)} %get-tuple-element.9), channel_id=1, source_target_pairs={{0,1},{1,0},{2,3},{3,2},{4,5},{5,4},{6,7},{7,6},{8,9},{9,8},{10,11... | collective-permute-start | bytes 393224 | tf_op jit(solution)/shard_map/ppermute | solution.py:178
  40.4 1.4 %collective-permute-start.17 = (bf16[256,128]{1,0:T(8,128)(2,1)S(1)}, bf16[256,128]{1,0:T(8,128)(2,1)S(1)}, u32[]{:S(2)}, u32[]{:S(2)}) collective-permute-start(bf16[256,128]{1,0:T(8,128)(2,1)S(1)} %sum.1.refs_0_), channel_id=1, source_target_pairs={{0,1},{1,0},{2,3},{3,2},{4,5},{5,4},{6,7},{7,6},{8,9},{9,8},{10,11... | collective-permute-start | bytes 196616 | tf_op jit(solution)/shard_map/ppermute | solution.py:178
  40.9 1.3 %collective-permute-start.18 = (bf16[256,128]{1,0:T(8,128)(2,1)S(1)}, bf16[256,128]{1,0:T(8,128)(2,1)S(1)}, u32[]{:S(2)}, u32[]{:S(2)}) collective-permute-start(bf16[256,128]{1,0:T(8,128)(2,1)S(1)} %collective-permute-done.16.refs_1_), channel_id=1, source_target_pairs={{0,1},{1,0},{2,3},{3,2},{4,5},{5,4},{6,7},{7,6},{8,9},{9,8},{10,11... | collective-permute-start | bytes 196616 | tf_op jit(solution)/shard_map/ppermute | solution.py:178
